TPU v7x, 128 devices: a whole 4x4x4 slice. The times are simulated.
128 devices in a mesh: dp: 16 (over z, y), frame: 8 (over x, core).
Axes of the slice: x: 4, y: 4, z: 4, core: 2. Of those that a mesh axis runs over, the one named last changes fastest.
Arguments:
- frames: bfloat16 [2048, 8, 768], P('dp', 'frame'), may hold values from -34 to 34
- frame_gain: float32 [768], replicated, may hold values from 0.25 to 1.75
- w_up: bfloat16 [768, 3072], replicated, may hold values from -0.21875 to 0.21875
- w_down: bfloat16 [3072, 768], replicated, may hold values from -0.109375 to 0.109375
- pool_query: float32 [768], replicated, may hold values from -4 to 4
- pos_embed: bfloat16 [50, 768], replicated, may hold values from -5 to 5
- user_gain: float32 [768], replicated, may hold values from 0.25 to 1.75
- w_qkv: bfloat16 [768, 2304], replicated, may hold values from -0.7577722 to 0.7577722
- w_out: bfloat16 [768, 768], replicated, may hold values from -0.21875 to 0.21875
- request_rows: int32 [128, 16, 64], P(('dp', 'frame')), may hold values from -1 to 127, as said below
- hist_slot: int32 [2048, 50], P(('dp', 'frame')), may hold values from 0 to 1023, as said below
- hist_len: int32 [2048], P(('dp', 'frame')), may hold values from 1 to 50
- d_encoded: bfloat16 [2048, 50, 768], P(('dp', 'frame')), may hold values from -6 to 6
Outputs:
- encoded: bfloat16 [2048, 50, 768], P(('dp', 'frame'))
- d_frames: bfloat16 [2048, 8, 768], P('dp', 'frame')
Inputs may be any that keep to these rules, and one draw needn't show every extreme that they name: `request_rows`: in each list of 64 entries the first ones are distinct local rows of that owner and the rest are -1; a list holds 16 to 64 rows; in every draw one owner index receives 64 rows from every device, and one device fills all its lists. `hist_slot`: every entry names a filled slot of the request lists of the device that holds the user.
All inputs are finite; a program needn't handle non-finite values.
Results may differ from a plain program's by a relative error of at most 0.025.
Values may be sent and summed in bfloat16 or wider, within the bound.
No kernel may reach another device: no remote copies, remote signals or barrier semaphores. Data moves between devices by JAX's collectives and lax.ppermute only.
A program may use at most 128 MiB of HBM per device.

v0:
```python
from functools import partial
import math

import jax
import jax.numpy as jnp
from jax import lax
from jax.sharding import PartitionSpec as P

epsilon = 1e-06
masked_score = -1000000000.0


def merged(x, axis, combine):
    everything = jax.tree.map(lambda part: lax.all_gather(part, axis), x)
    initial = jax.tree.map(lambda part: part[0], everything)

    def step(k, so_far):
        return combine(so_far, jax.tree.map(lambda part: part[k], everything))

    return lax.fori_loop(1, lax.axis_size(axis), step, initial)


def layer_norm(values, norm_gain):
    row_mean = jnp.mean(values, axis=-1, keepdims=True)
    centred = values - row_mean
    variance = jnp.mean(centred * centred, axis=-1, keepdims=True)
    return centred * lax.rsqrt(variance + epsilon) * norm_gain


def frame_block(frames32, norm_gain, w_up, w_down):
    normed = layer_norm(frames32, norm_gain).astype(jnp.bfloat16)
    hidden = jax.nn.gelu(jnp.dot(normed, w_up, preferred_element_type=jnp.float32)).astype(
        jnp.bfloat16
    )
    return frames32 + jnp.dot(hidden, w_down, preferred_element_type=jnp.float32)


def user_encoder(inputs, norm_gain, w_qkv, w_out, lengths):
    user_count, seq_length, feature_width = inputs.shape
    normed = (
        layer_norm(inputs, norm_gain)
        .astype(jnp.bfloat16)
        .reshape(user_count * seq_length, feature_width)
    )
    packed = jnp.dot(normed, w_qkv, preferred_element_type=jnp.float32).astype(jnp.bfloat16)
    packed = packed.reshape(user_count, seq_length, 3 * feature_width)
    query_part = packed[..., :feature_width]
    key_part = packed[..., feature_width : 2 * feature_width]
    value_part = packed[..., 2 * feature_width :]
    attn_scores = jnp.einsum(
        "usd,utd->ust", query_part, key_part, preferred_element_type=jnp.float32
    ) / math.sqrt(feature_width)
    positions = jnp.arange(seq_length, dtype=jnp.int32)
    allowed = (positions[None, None, :] <= positions[None, :, None]) & (
        positions[None, None, :] < lengths[:, None, None]
    )
    attn_scores = jnp.where(allowed, attn_scores, masked_score)
    attn_probs = jax.nn.softmax(attn_scores, axis=-1).astype(jnp.bfloat16)
    attended = jnp.einsum(
        "ust,utd->usd", attn_probs, value_part, preferred_element_type=jnp.float32
    ).astype(jnp.bfloat16)
    projected = jnp.dot(
        attended.reshape(user_count * seq_length, feature_width),
        w_out,
        preferred_element_type=jnp.float32,
    )
    updated = inputs + projected.reshape(inputs.shape)
    live_rows = positions[None, :] < lengths[:, None]
    return jnp.where(live_rows[..., None], updated, 0.0)


def combine_softmax(earlier, later):
    top_a, total_a, sum_a = earlier
    top_b, total_b, sum_b = later
    row_top = jnp.maximum(top_a, top_b)
    scale_a = jnp.exp(top_a - row_top)
    scale_b = jnp.exp(top_b - row_top)
    return (
        row_top,
        total_a * scale_a + total_b * scale_b,
        sum_a * scale_a[:, None] + sum_b * scale_b[:, None],
    )


def sum_by_index(values, indices, count):
    table = (jnp.arange(count, dtype=jnp.int32)[:, None] == indices[None, :]).astype(jnp.float32)
    return jnp.dot(
        table, values, precision=lax.Precision.HIGHEST, preferred_element_type=jnp.float32
    )


def shards(
    frames,
    frame_gain,
    w_up,
    w_down,
    pool_query,
    pos_embed,
    user_gain,
    w_qkv,
    w_out,
    request_rows,
    hist_slot,
    hist_len,
    d_encoded,
):
    owned_rows, frame_count, feature_width = frames.shape
    scale_root = math.sqrt(feature_width)
    flat_frames = frames.reshape(owned_rows * frame_count, feature_width).astype(jnp.float32)
    raw_out, frame_back = jax.vjp(
        partial(frame_block, norm_gain=frame_gain, w_up=w_up, w_down=w_down), flat_frames
    )
    stored = raw_out.astype(jnp.bfloat16).reshape(owned_rows, frame_count, feature_width)
    framed = stored.astype(jnp.float32)
    pool_scores = jnp.sum(framed * pool_query, axis=-1) / scale_root
    local_top = jnp.max(pool_scores, axis=-1)
    raised = jnp.exp(pool_scores - local_top[:, None])
    local_total = jnp.sum(raised, axis=-1)
    weighted = jnp.sum(raised[..., None] * framed, axis=1)
    top_all, total_all, weighted_all = merged(
        (local_top, local_total, weighted), "frame", combine_softmax
    )
    pool_weights = jnp.exp(pool_scores - top_all[:, None]) / total_all[:, None]
    pooled = weighted_all / total_all[:, None]
    pooled_table = pooled.astype(jnp.bfloat16)
    wanted = request_rows[0]
    owner_count, slot_count = wanted.shape
    asked_rows = lax.all_to_all(wanted, "dp", split_axis=0, concat_axis=0, tiled=True)
    served = jnp.take(pooled_table, jnp.maximum(asked_rows, 0), axis=0)
    fetched = lax.all_to_all(served, "dp", split_axis=0, concat_axis=0, tiled=True)
    fetched = fetched.reshape(owner_count * slot_count, feature_width)
    user_count, seq_length = hist_slot.shape
    flat_slots = hist_slot.reshape(-1)
    gathered_rows = jnp.take(fetched, flat_slots, axis=0).reshape(
        user_count, seq_length, feature_width
    )
    inputs = gathered_rows.astype(jnp.float32) + pos_embed.astype(jnp.float32)[None]
    encoded32, encoder_back = jax.vjp(
        partial(user_encoder, norm_gain=user_gain, w_qkv=w_qkv, w_out=w_out, lengths=hist_len),
        inputs,
    )
    (d_inputs,) = encoder_back(d_encoded.astype(jnp.float32))
    d_slots = sum_by_index(
        d_inputs.reshape(-1, feature_width), flat_slots, owner_count * slot_count
    )
    returned = lax.all_to_all(
        d_slots.reshape(owner_count, slot_count, feature_width).astype(jnp.bfloat16),
        "dp",
        split_axis=0,
        concat_axis=0,
        tiled=True,
    ).astype(jnp.float32)
    targets = jnp.where(asked_rows >= 0, asked_rows, owned_rows).reshape(-1)
    partial_grad = sum_by_index(returned.reshape(-1, feature_width), targets, owned_rows)
    d_pooled = lax.psum(partial_grad.astype(jnp.bfloat16), "frame").astype(jnp.float32)
    cross_dots = jnp.sum(d_pooled[:, None, :] * framed, axis=-1)
    self_dot = jnp.sum(d_pooled * pooled, axis=-1)
    d_frame_out = pool_weights[..., None] * (
        d_pooled[:, None, :]
        + ((cross_dots - self_dot[:, None]) / scale_root)[..., None] * pool_query
    )
    (d_flat,) = frame_back(d_frame_out.reshape(owned_rows * frame_count, feature_width))
    d_frames = d_flat.astype(jnp.bfloat16).reshape(owned_rows, frame_count, feature_width)
    return (encoded32.astype(jnp.bfloat16), d_frames)


def solution(mesh):
    in_specs = (
        P("dp", "frame", None),
        P(),
        P(),
        P(),
        P(),
        P(),
        P(),
        P(),
        P(),
        P(("dp", "frame"), None, None),
        P(("dp", "frame"), None),
        P(("dp", "frame")),
        P(("dp", "frame"), None, None),
    )
    out_specs = (P(("dp", "frame"), None, None), P("dp", "frame", None))
    return jax.shard_map(shards, mesh=mesh, in_specs=in_specs, out_specs=out_specs, check_vma=False)
```

profile of v0, /device:TPU:1, one launch (start us, length us, event | category | flops | bytes accessed | tf_op | source)
XLA Modules:
  0.0 319.0 jit_solution(3891165261330935487)
XLA Ops:
  10.7 3.4 %fusion.98 = f32[128,3072]{1,0:T(8,128)S(1)} fusion(bf16[768,3072]{1,0:T(8,128)(2,1)} %param.17, bf16[128,1,768]{2,0,1:T(8,128)(2,1)} %param.15, f32[768]{0:T(1024)} %param.16, f32[128]{0:T(128)S(1)} %fusion.112, f32[128]{0:T(128)S(1)} %broadcast_multiply_fusion.3), kind=kOutput, calls=%fused_computation.128 | convolution fusion | flops 604471296 | bytes 6492160 | tf_op jit(solution)/shard_map/jvp()/dot_general | solution.py:32
  17.8 8.6 %all-to-all-start = ((s32[16,1,64]{2,1,0:T(1,128)}), s32[16,1,64]{2,1,0:T(1,128)S(1)}, u32[]{:S(2)}, u32[]{:S(2)}) async-start(s32[16,1,64]{2,1,0:T(1,128)} %bitcast.100), calls=%async_computation | async-start | bytes 16384 | tf_op jit(solution)/shard_map/all_to_all | solution.py:128
  26.5 11.4 %all-gather.4 = f32[8,1,128]{2,1,0:T(1,128)S(1)} all-gather(f32[1,1,128]{2,1,0:T(1,128)} %get-tuple-element.216), channel_id=4, replica_groups=mesh['dp'=16,'frame'=8] {'frame'}, dimensions={0}, use_global_device_ids=true | all-gather | bytes 4608 | tf_op jit(solution)/shard_map/all_gather | solution.py:14
  37.9 8.3 %all-gather.3 = f32[8,1,128]{2,1,0:T(1,128)S(1)} all-gather(f32[1,1,128]{2,1,0:T(1,128)} %get-tuple-element.217), channel_id=2, replica_groups=mesh['dp'=16,'frame'=8] {'frame'}, dimensions={0}, use_global_device_ids=true | all-gather | bytes 4608 | tf_op jit(solution)/shard_map/all_gather | solution.py:14
  49.2 1.4 reshape.428
  52.4 1.8 slice.35
  54.2 22.8 %while.19 = (s32[]{:T(128)}, f32[128]{0:T(128)}, f32[128]{0:T(128)}, f32[128,768]{1,0:T(8,128)}, f32[8,128]{1,0:T(8,128)}, /*index=5*/f32[8,128]{1,0:T(8,128)}, ...) while((s32[]{:T(128)}, f32[128]{0:T(128)}, f32[128]{0:T(128)}, f32[128,768]{1,0:T(8,128)}, ...), condition=%wide.region_4.0_spmd, body=%wide.region_3.0_spmd.sunk | while | flops 295685 | bytes 1184911 | solution.py:20
  54.2 1.3 fusion.156
  55.5 2.0 fusion.157
  57.5 1.3 fusion.156
  58.7 2.0 fusion.157
  60.7 1.3 fusion.156
  62.0 2.0 fusion.157
  64.0 1.3 fusion.156
  65.2 2.0 fusion.157
  68.5 2.0 fusion.157
  71.7 2.0 fusion.157
  75.0 2.0 fusion.157
  77.0 1.8 fusion.109
  78.7 6.8 %gather_fusion = bf16[1024,768]{1,0:T(8,128)(2,1)} fusion(bf16[128,768]{1,0:T(8,128)(2,1)} %fusion.109, s32[1024]{0:T(1024)} %broadcast_clamp_fusion), kind=kCustom, calls=%fused_computation | custom fusion | bytes 3149824 | tf_op jit(solution)/shard_map/jit(_take)/gather | solution.py:129
  85.5 2.8 broadcast_select_fusion
  88.3 7.0 %all-to-all-start.1 = ((bf16[16,64,768]{2,1,0:T(8,128)(2,1)}), bf16[16,64,768]{2,1,0:T(8,128)(2,1)}, u32[]{:S(2)}, u32[]{:S(2)}) async-start(bf16[16,64,768]{2,1,0:T(8,128)(2,1)} %broadcast_select_fusion), calls=%async_computation.1 | async-start | bytes 3145728 | tf_op jit(solution)/shard_map/all_to_all | solution.py:130
  95.3 1.3 iota_compare_fusion.3
  96.6 1.3 broadcast_in_dim.115
  97.9 1.6 convert_element_type.128
  99.5 2.9 convert_select_fusion
  102.3 2.3 reshape.419
  104.6 3.8 %fusion.135 = bf16[800,768]{1,0:T(8,128)(2,1)} fusion(bf16[800,768]{1,0:T(8,128)(2,1)} %reshape.419, bf16[768,768]{1,0:T(8,128)(2,1)} %param.23), kind=kOutput, calls=%fused_computation.187 | convolution fusion | flops 943718400 | bytes 3637248 | tf_op jit(solution)/shard_map/transpose(jvp())/dot_general | solution.py:62
  108.5 2.4 reshape.420
  110.9 2.6 add.179
  113.5 3.0 add.183
  118.3 1.7 all-to-all-done.1
  120.0 6.4 %gather_fusion.1 = bf16[800,768]{1,0:T(8,128)(2,1)} fusion(bf16[1024,768]{1,0:T(8,128)(2,1)} %bitcast.15, s32[1024]{0:T(1024)S(1)} %pad_clamp_fusion), kind=kCustom, calls=%fused_computation.1 | custom fusion | bytes 2460800 | tf_op jit(solution)/shard_map/jit(_take)/gather | solution.py:134
  126.4 2.3 gather.12
  128.7 2.7 fusion.129
  134.5 7.3 %convolution_convert_fusion = bf16[800,2304]{1,0:T(8,128)(2,1)} fusion(bf16[768,2304]{1,0:T(8,128)(2,1)S(1)} %copy-done, f32[800,768]{1,0:T(8,128)} %add.183, f32[768]{0:T(1024)} %param.21, f32[800]{0:T(1024)S(1)} %get-tuple-element.214, f32[800]{0:T(1024)S(1)} %broadcast_multiply_fusion.1, bf16[800,768]{1,0:T(8,128)(2,1)} %gather_fusion.1, ...), kind=kOutput, calls=%fused_computation.14 | convolution fusion | flops 2837299200 | bytes 10922016 | tf_op jit(solution)/shard_map/jvp()/dot_general | solution.py:45
  141.8 4.9 %reshape.418 = bf16[16,50,2304]{2,1,0:T(8,128)(2,1)} reshape(bf16[800,2304]{1,0:T(8,128)(2,1)} %convolution_convert_fusion) | data formatting | bytes 7372800 | tf_op jit(solution)/shard_map/jvp()/reshape | solution.py:46
  146.7 2.3 fusion.43
  151.9 3.3 %convolution_convert_fusion.4 = bf16[16,50,768]{2,1,0:T(8,128)(2,1)} fusion(bf16[16,50,768]{2,1,0:T(8,128)(2,1)} %reshape.420, f32[16,50]{1,0:T(8,128)} %copy-done.8, f32[16,50,50]{1,2,0:T(8,128)} %copy-done.6), kind=kOutput, calls=%fused_computation.40 | convolution fusion | flops 62175248 | bytes 2620800 | tf_op jit(solution)/shard_map/transpose(jvp(ust,utd->usd))/dot_general | solution.py:59
  155.2 3.2 multiply_reduce_fusion.2
  159.0 3.8 %convolution_convert_fusion.2 = bf16[16,50,768]{2,1,0:T(8,128)(2,1)} fusion(bf16[16,50,2304]{2,1,0:T(8,128)(2,1)} %reshape.418, f32[16,50,50]{1,2,0:T(8,128)} %get-tuple-element.223, f32[16,50]{1,0:T(8,128)} %neg.12, f32[16,50]{1,0:T(8,128)} %copy-done.8, pred[16,50]{1,0:T(8,128)(4,1)} %get-tuple-element.228, pred[50,50]{0,1:T(8,128)(4,1)} %iota_compare_fusion.2, ...), kind=kOutput, calls=%fused_computation.38 | convolution fusion | flops 62335248 | bytes 4006912 | tf_op jit(solution)/shard_map/transpose(jvp(usd,utd->ust))/dot_general | solution.py:50
  162.8 3.5 %convolution_convert_fusion.3 = bf16[16,50,768]{2,1,0:T(8,128)(2,1)} fusion(bf16[16,50,2304]{2,1,0:T(8,128)(2,1)} %reshape.418, f32[16,50,50]{1,2,0:T(8,128)} %get-tuple-element.223, f32[16,50]{1,0:T(8,128)} %neg.12, f32[16,50]{1,0:T(8,128)} %copy-done.8, pred[16,50]{1,0:T(8,128)(4,1)} %get-tuple-element.228, pred[50,50]{0,1:T(8,128)(4,1)} %iota_compare_fusion.2, ...), kind=kOutput, calls=%fused_computation.39 | convolution fusion | flops 62335248 | bytes 4006912 | tf_op jit(solution)/shard_map/transpose(jvp(usd,utd->ust))/dot_general | solution.py:50
  166.4 3.6 %pad_add_fusion = bf16[16,50,2304]{2,1,0:T(8,128)(2,1)} fusion(bf16[16,50,768]{2,1,0:T(8,128)(2,1)} %convolution_convert_fusion.2, bf16[16,50,768]{2,1,0:T(8,128)(2,1)} %convolution_convert_fusion.3, bf16[16,50,768]{2,1,0:T(8,128)(2,1)} %convolution_convert_fusion.4), kind=kLoop, calls=%fused_computation.15 | loop fusion | flops 11059200 | bytes 7372800 | tf_op jit(solution)/shard_map/transpose(jvp())/add_any | solution.py:47
  170.0 5.0 %reshape.421 = bf16[800,2304]{1,0:T(8,128)(2,1)} reshape(bf16[16,50,2304]{2,1,0:T(8,128)(2,1)} %pad_add_fusion) | data formatting | bytes 7372800 | tf_op jit(solution)/shard_map/transpose(jvp())/reshape | solution.py:46
  174.9 7.7 %multiply_reduce_fusion = (f32[800]{0:T(1024)S(1)}, f32[800,768]{1,0:T(8,128)}) fusion(f32[768]{0:T(1024)} %param.21, f32[800]{0:T(1024)S(1)} %broadcast_multiply_fusion.1, f32[800,768]{1,0:T(8,128)} %add.183, bf16[800,768]{1,0:T(8,128)(2,1)} %gather_fusion.1, pred[800]{0:T(1024)(128)(4,1)} %broadcast_in_dim.115, bf16[800,2304]{1,0:T(8,128)(2,1)} %reshape.421, ...), kind=kOutput, calls=%fused_computation.28 | convolution fusion | flops 2836684032 | bytes 13379616 | tf_op jit(solution)/shard_map/transpose(jvp())/dot_general | solution.py:45
  183.8 1.4 reduce_sum.132
  185.2 1.4 add.190
  186.6 3.0 reshape.425
  189.6 4.1 %fusion.12 = f32[800]{0:T(1024)S(1)} fusion(f32[800,768]{1,0:T(8,128)} %get-tuple-element.225, f32[800,768]{1,0:T(8,128)} %add.183, f32[800]{0:T(1024)} %multiply_multiply_fusion.3, f32[768]{0:T(1024)S(1)} %copy-done.16, f32[800]{0:T(1024)} %copy-done.17, f32[800]{0:T(1024)S(1)} %broadcast_multiply_fusion.1, bf16[800,768]{1,0:T(8,128)(2,1)} %gather_fusion.1, ...), kind=kLoop, calls=%fused_computation.27 | loop fusion | flops 6143200 | bytes 6160672 | tf_op jit(solution)/shard_map/transpose(jvp())/reduce_sum | solution.py:25
  195.8 4.4 %fusion.11 = f32[16,50,768]{2,1,0:T(8,128)} fusion(f32[16,50,768]{2,1,0:T(8,128)} %reshape.425, f32[16,50]{1,0:T(8,128)S(1)} %div.114, f32[16,50]{1,0:T(8,128)S(1)} %get-tuple-element.212, f32[16,50]{1,0:T(8,128)} %div.108, f32[16,50]{1,0:T(8,128)S(1)} %get-tuple-element.211, f32[768]{0:T(1024)} %param.21, f32[50,768]{1,0:T(8,128)} %convert_element_type.128, ...), kind=kLoop, calls=%fused_computation.23 | loop fusion | flops 7987200 | bytes 7543872 | tf_op jit(solution)/shard_map/transpose(jvp())/add_any | solution.py:24
  200.2 3.0 reshape.464
  203.2 8.3 %fusion.15 = bf16[16,64,768]{2,1,0:T(8,128)(2,1)} fusion(f32[800,768,1]{1,0,2:T(8,128)} %reshape.464, s32[800]{0:T(1024)S(1)} %copy-done.15, s32[16,64]{1,0:T(8,128)} %multiply_add_fusion), kind=kOutput, calls=%fused_computation.37 | convolution fusion | flops 7551352832 | bytes 4037760 | tf_op jit(solution)/shard_map/dot_general | solution.py:87
  211.5 5.0 %all-to-all-start.2 = ((bf16[16,64,768]{2,1,0:T(8,128)(2,1)}), bf16[16,64,768]{2,1,0:T(8,128)(2,1)}, u32[]{:S(2)}, u32[]{:S(2)}) async-start(bf16[16,64,768]{2,1,0:T(8,128)(2,1)} %fusion.15), calls=%async_computation.2 | async-start | bytes 3145728 | tf_op jit(solution)/shard_map/all_to_all | solution.py:146
  218.6 1.4 all_to_all.17
  220.0 1.3 compare_select_fusion.2
  222.5 16.6 %all-to-all-done.2 = bf16[16,64,768]{2,1,0:T(8,128)(2,1)} async-done(((bf16[16,64,768]{2,1,0:T(8,128)(2,1)}), bf16[16,64,768]{2,1,0:T(8,128)(2,1)}, u32[]{:S(2)}, u32[]{:S(2)}) %all-to-all-start.2) | async-done | bytes 1572896 | tf_op jit(solution)/shard_map/all_to_all | solution.py:146
  239.1 2.5 convolution_convert_fusion.8
  241.7 5.4 %select_convert_fusion = bf16[16,50,768]{2,1,0:T(8,128)(2,1)} fusion(f32[50,768]{1,0:T(8,128)} %convert_element_type.128, pred[16,50]{1,0:T(8,128)(4,1)S(1)} %copy-done.12, bf16[16,50,2304]{2,1,0:T(8,128)(2,1)} %reshape.418, bf16[16,50,768]{2,1,0:T(8,128)(2,1)} %gather.12, pred[16,50]{1,0:T(8,128)(4,1)S(1)} %copy-done.11, bf16[768,768]{1,0:T(8,128)(2,1)} %param.23, ...), kind=kOutput, calls=%fused_computation.25 | convolution fusion | flops 1009580032 | bytes 6255296 | tf_op jit(solution)/shard_map/jvp()/dot_general | solution.py:62
  247.1 2.6 copy.29
  249.7 47.6 %all-reduce.5.cloned.1.call-done = bf16[128,768]{1,0:T(8,128)(2,1)} async-done(((bf16[128,768]{1,0:T(8,128)(2,1)}), bf16[128,768]{1,0:T(8,128)(2,1)}) %all-reduce.5.cloned.1.call-update) | async-done | bytes 196624 | tf_op jit(solution)/shard_map/psum | solution.py:155
  297.3 1.4 fusion.92
  299.2 8.7 %fusion.90 = (f32[128]{0:T(128)}, f32[128,768]{1,0:T(8,128)}) fusion(bf16[128,1,768]{2,0,1:T(8,128)(2,1)} %param.15, f32[128]{0:T(128)S(1)} %copy-done.24, f32[768]{0:T(1024)S(1)} %copy-done.27, bf16[768,3072]{1,0:T(8,128)(2,1)} %param.17, f32[128,3072]{1,0:T(8,128)} %copy-done.5, bf16[3072,768]{1,0:T(8,128)(2,1)} %param.18, ...), kind=kOutput, calls=%fused_computation.120 | convolution fusion | flops 1217298304 | bytes 11804672 | tf_op jit(solution)/shard_map/transpose(jvp())/dot_general | solution.py:32
  308.6 1.3 fusion.126
  310.0 2.1 fusion.97
  (111 shorter events, 32.1 us)
Async XLA Ops:
  7.2 127.4 %copy-start = (bf16[768,2304]{1,0:T(8,128)(2,1)S(1)}, bf16[768,2304]{1,0:T(8,128)(2,1)}, u32[]{:S(2)}) copy-start(bf16[768,2304]{1,0:T(8,128)(2,1)} %param.22) | copy-start | bytes 10616836
  7.2 45.3 %all-gather.7.cloned.1.call-start = ((), (), s32[]{:S(2)}) async-start(), calls=%async_computation.4 | async-start | bytes 3538944 | tf_op jit(solution)/shard_map/all_gather | solution.py:14
  8.4 1.7 copy-start.23
  9.6 0.6 copy-start.31
  10.1 0.5 copy-start.25
  10.7 3.4 %copy-start.3 = (bf16[128,1,768]{2,0,1:T(8,128)(2,1)S(1)}, bf16[128,1,768]{2,0,1:T(8,128)(2,1)}, u32[]{:S(2)}) copy-start(bf16[128,1,768]{2,0,1:T(8,128)(2,1)} %param.15) | copy-start | bytes 589828
  10.7 3.5 %copy-start.28 = (f32[768]{0:T(1024)S(1)}, f32[768]{0:T(1024)}, u32[]{:S(2)}) copy-start(f32[768]{0:T(1024)} %param.19) | copy-start | bytes 9220
  10.7 4.0 %copy-start.32 = (bf16[3072,768]{1,0:T(8,128)(2,1)S(1)}, bf16[3072,768]{1,0:T(8,128)(2,1)}, u32[]{:S(2)}) copy-start(bf16[3072,768]{1,0:T(8,128)(2,1)} %param.18) | copy-start | bytes 14155780
  14.7 1.2 copy-start.5
  14.7 32.6 %copy-start.7 = (s32[16,50]{1,0:T(8,128)S(1)}, s32[16,50]{1,0:T(8,128)}, u32[]{:S(2)}) copy-start(s32[16,50]{1,0:T(8,128)} %param.25) | copy-start | bytes 9604
  15.9 0.6 copy-start.30
  15.9 1.1 copy-start.4
  17.8 30.8 %all-to-all-start = ((s32[16,1,64]{2,1,0:T(1,128)}), s32[16,1,64]{2,1,0:T(1,128)S(1)}, u32[]{:S(2)}, u32[]{:S(2)}) async-start(s32[16,1,64]{2,1,0:T(1,128)} %bitcast.100), calls=%async_computation | async-start | bytes 16384 | tf_op jit(solution)/shard_map/all_to_all | solution.py:128
  37.9 8.3 %copy-start.19 = (f32[8,1,128]{2,1,0:T(1,128)}, f32[8,1,128]{2,1,0:T(1,128)S(1)}, u32[]{:S(2)}) copy-start(f32[8,1,128]{2,1,0:T(1,128)S(1)} %all-gather.4) | copy-start | bytes 12292
  46.1 0.6 copy-start.20
  88.3 31.7 %all-to-all-start.1 = ((bf16[16,64,768]{2,1,0:T(8,128)(2,1)}), bf16[16,64,768]{2,1,0:T(8,128)(2,1)}, u32[]{:S(2)}, u32[]{:S(2)}) async-start(bf16[16,64,768]{2,1,0:T(8,128)(2,1)} %broadcast_select_fusion), calls=%async_computation.1 | async-start | bytes 3145728 | tf_op jit(solution)/shard_map/all_to_all | solution.py:130
  113.5 3.0 copy-start.18
  113.5 4.2 %copy-start.14 = (s32[800]{0:T(1024)S(1)}, s32[800]{0:T(1024)}, u32[]{:S(2)}) copy-start(s32[800]{0:T(1024)} %reshape.417) | copy-start | bytes 9604
  126.4 2.3 copy-start.21
  128.7 2.8 copy-start.1
  128.7 3.1 copy-start.2
  128.7 3.1 copy-start.22
  133.9 0.6 copy-start.17
  149.1 0.8 copy-start.6
  150.7 0.6 copy-start.8
  182.6 0.6 copy-start.13
  186.6 3.0 copy-start.16
  200.2 3.0 copy-start.15
  211.5 27.6 %all-to-all-start.2 = ((bf16[16,64,768]{2,1,0:T(8,128)(2,1)}), bf16[16,64,768]{2,1,0:T(8,128)(2,1)}, u32[]{:S(2)}, u32[]{:S(2)}) async-start(bf16[16,64,768]{2,1,0:T(8,128)(2,1)} %fusion.15), calls=%async_computation.2 | async-start | bytes 3145728 | tf_op jit(solution)/shard_map/all_to_all | solution.py:146
  216.5 25.1 %copy-start.9 = (f32[16,50]{1,0:T(8,128)S(1)}, f32[16,50]{1,0:T(8,128)}, u32[]{:S(2)}) copy-start(f32[16,50]{1,0:T(8,128)} %copy-done.8) | copy-start | bytes 9604
  216.5 80.7 %all-reduce.5.cloned.1.call-start = ((), (), s32[]{:S(2)}) async-start(), calls=%async_computation.3 | async-start | bytes 393216 | tf_op jit(solution)/shard_map/psum | solution.py:155
  218.6 23.0 %copy-start.11 = (pred[16,50]{1,0:T(8,128)(4,1)S(1)}, pred[16,50]{1,0:T(8,128)(4,1)}, u32[]{:S(2)}) copy-start(pred[16,50]{1,0:T(8,128)(4,1)} %get-tuple-element.229) | copy-start | bytes 2404
  218.6 23.0 %copy-start.12 = (pred[16,50]{1,0:T(8,128)(4,1)S(1)}, pred[16,50]{1,0:T(8,128)(4,1)}, u32[]{:S(2)}) copy-start(pred[16,50]{1,0:T(8,128)(4,1)} %get-tuple-element.228) | copy-start | bytes 2404
  247.0 50.2 %copy-start.10 = (f32[128]{0:T(128)S(1)}, f32[128]{0:T(128)}, u32[]{:S(2)}) copy-start(f32[128]{0:T(128)} %get-tuple-element.181) | copy-start | bytes 1540
  247.0 52.2 %copy-start.24 = (f32[128]{0:T(128)S(1)}, f32[128]{0:T(128)}, u32[]{:S(2)}) copy-start(f32[128]{0:T(128)} %copy-done.23) | copy-start | bytes 1540
  247.0 52.2 %copy-start.27 = (f32[768]{0:T(1024)S(1)}, f32[768]{0:T(1024)}, u32[]{:S(2)}) copy-start(f32[768]{0:T(1024)} %param.16) | copy-start | bytes 9220
  247.0 52.2 %copy-start.29 = (f32[768]{0:T(1024)S(1)}, f32[768]{0:T(1024)}, u32[]{:S(2)}) copy-start(f32[768]{0:T(1024)} %param.19) | copy-start | bytes 9220
  299.2 9.4 %copy-start.26 = (f32[128]{0:T(128)S(1)}, f32[128]{0:T(128)}, u32[]{:S(2)}) copy-start(f32[128]{0:T(128)} %copy-done.25) | copy-start | bytes 1540
Sparse Core Ops, SparseCore 0:
  17.9 31.3 all-gather.6
  241.8 55.4 all-reduce.4
where the time goes:
time: 322 us; the launch traced here: 319 us
  other arithmetic  71.2 us (22%)
  waiting for transfers between devices  65.9 us (20%)
  matrix products  64.5 us (20%)
  local copies, waits for them, and re-layouts  62.4 us (19%)
  starting transfers between devices  20.9 us (6%)
  blocking collectives  19.7 us (6%)
  between operations  14.3 us (4%)
    psum x1, waiting for transfers between devices, shards(): lax.psum(partial_grad.astype(jnp.bfloat16), 'frame').astype(jnp.float32)  47.6 us
    all_gather x2, blocking collectives, merged(): everything = jax.tree.map(lambda part: lax.all_gather(part, axis), x)  19.7 us
    all_to_all x1, waiting for transfers between devices, shards(): lax.all_to_all(d_slots.reshape(owner_count, slot_count, feature_width).as...  16.6 us
    dot_general x2, matrix products, user_encoder(): jnp.dot(normed, w_qkv, preferred_element_type=jnp.float32)  15 us
    add x7, other arithmetic, combine_softmax(): sum_a * scale_a[:, None] + sum_b * scale_b[:, None]  13.8 us
    dot_general x2, matrix products, frame_block(): jnp.dot(normed, w_up, preferred_element_type=jnp.float32)  12.2 us
    dot_general x2, matrix products, sum_by_index(): jnp.dot(table, values, precision=lax.Precision.HIGHEST, preferred_element...  10.8 us
    reshape x2, local copies, waits for them, and re-layouts, user_encoder(): packed = packed.reshape(user_count, seq_length, 3 * feature_width)  9.89 us
  transfers between devices with their start and end apart: 5, of which 3 were waited for; matrix products, arithmetic and copies ran while one was open for 13% of the time, Pallas kernels for 0%

commit v1 on v0

v1 whole, which is shorter than its diff:
```python
import functools
import math

import jax
import jax.numpy as jnp
from jax import lax
from jax.experimental import pallas as pl
from jax.experimental.pallas import tpu as pltpu
from jax.sharding import PartitionSpec as P

D = 768
HID = 3072
L = 50
LP = 56
USERS = 16
GROUP = 4
ROWS = GROUP * LP
OWNERS = 16
HALF = 64
CAP = 64
PAY = D + 128
EPS = 1e-6
ROOT = math.sqrt(D)
MASKED = -1e9
AXES = ("dp", "frame")
f32 = jnp.float32
bf16 = jnp.bfloat16
VMEM = pl.BlockSpec(memory_space=pltpu.VMEM)
SMEM = pl.BlockSpec(memory_space=pltpu.SMEM)


def dot_nn(a, b):
    return lax.dot_general(a, b, (((1,), (0,)), ((), ())), preferred_element_type=f32)


def dot_nt(a, b):
    return lax.dot_general(a, b, (((1,), (1,)), ((), ())), preferred_element_type=f32)


def dot_tn(a, b):
    return lax.dot_general(a, b, (((0,), (0,)), ((), ())), preferred_element_type=f32)


def params(megabytes):
    return pltpu.CompilerParams(vmem_limit_bytes=megabytes << 20)


def normalised(x):
    centred = x - jnp.mean(x, axis=-1, keepdims=True)
    rstd = lax.rsqrt(jnp.mean(centred * centred, axis=-1, keepdims=True) + EPS)
    return centred * rstd, rstd


def norm_back(d_normed, gain, xhat, rstd):
    d_hat = d_normed * gain
    along = jnp.mean(d_hat * xhat, axis=-1, keepdims=True)
    return rstd * (d_hat - jnp.mean(d_hat, axis=-1, keepdims=True) - xhat * along)


def frame_forward(core, frames, gain, w_up, w_down, mine, other, out, slope, normed, total):
    step = pl.program_id(0)

    @pl.when(step == 0)
    def _():
        x = frames[...].astype(f32)
        xhat, _ = normalised(x)
        normed[...] = (xhat * gain[...]).astype(bf16)
        total[...] = x

    a = dot_nn(normed[...], w_up[...])
    c0 = math.sqrt(2.0 / math.pi)
    square = a * a
    th = jnp.tanh(c0 * a * (1.0 + 0.044715 * square))
    half = 0.5 * (1.0 + th)
    hidden = (a * half).astype(bf16)
    slope[...] = (half + 0.5 * a * (1.0 - th * th) * c0 * (1.0 + 3 * 0.044715 * square)).astype(bf16)
    total[...] += dot_nn(hidden, w_down[...])

    @pl.when(step == pl.num_programs(0) - 1)
    def _():
        out[...] = total[...].astype(bf16)
        c = core[0]
        mine[...] = total[pl.ds(pl.multiple_of(c * HALF, HALF), HALF), :].astype(bf16)
        other[...] = total[pl.ds(pl.multiple_of((1 - c) * HALF, HALF), HALF), :].astype(bf16)


def run_frame_forward(core, frames, gain, w_up, w_down):
    steps = 4
    width = HID // steps
    rows = frames.shape[0]
    full = lambda r, w: pl.BlockSpec((r, w), lambda j: (0, 0))
    return pl.pallas_call(
        frame_forward,
        grid=(steps,),
        in_specs=[
            SMEM,
            full(rows, D),
            full(1, D),
            pl.BlockSpec((D, width), lambda j: (0, j)),
            pl.BlockSpec((width, D), lambda j: (j, 0)),
        ],
        out_specs=[full(HALF, D), full(HALF, D), full(rows, D), pl.BlockSpec((rows, width), lambda j: (0, j))],
        out_shape=[
            jax.ShapeDtypeStruct((HALF, D), bf16),
            jax.ShapeDtypeStruct((HALF, D), bf16),
            jax.ShapeDtypeStruct((rows, D), bf16),
            jax.ShapeDtypeStruct((rows, HID), bf16),
        ],
        scratch_shapes=[pltpu.VMEM((rows, D), bf16), pltpu.VMEM((rows, D), f32)],
        compiler_params=params(40),
        name="frame_forward",
    )(core, frames, gain, w_up, w_down)


def pieces(value):
    first = value.astype(bf16).astype(f32)
    rest = value - first
    second = rest.astype(bf16).astype(f32)
    return first, second, rest - second


def write_payload(out, mean, top, total):
    lane = lax.broadcasted_iota(jnp.int32, (HALF, 128), 1)
    stats = jnp.zeros((HALF, 128), f32)
    for at, piece in enumerate(pieces(top) + pieces(total)):
        stats = jnp.where(lane == at, piece, stats)
    out[:, :D] = mean.astype(bf16)
    out[:, D:] = stats.astype(bf16)


def read_stats(block):
    stats = block[:, D:].astype(f32)
    lane = lax.broadcasted_iota(jnp.int32, stats.shape, 1)
    top = jnp.sum(jnp.where(lane < 3, stats, 0.0), axis=-1, keepdims=True)
    total = jnp.sum(jnp.where((lane >= 3) & (lane < 6), stats, 0.0), axis=-1, keepdims=True)
    return top, total


def pool_pair(mine, theirs, query, out):
    a = mine[...].astype(f32)
    b = theirs[...].astype(f32)
    q = query[...]
    score_a = jnp.sum(a * q, axis=-1, keepdims=True) / ROOT
    score_b = jnp.sum(b * q, axis=-1, keepdims=True) / ROOT
    top = jnp.maximum(score_a, score_b)
    weight_a = jnp.exp(score_a - top)
    weight_b = jnp.exp(score_b - top)
    total = weight_a + weight_b
    write_payload(out, (weight_a * a + weight_b * b) / total, top, total)


def pool_all(p0, p1, p2, p3, spread, out):
    parts = (p0, p1, p2, p3)
    stats = [read_stats(p) for p in parts]
    top = functools.reduce(jnp.maximum, [s[0] for s in stats])
    weights = [jnp.exp(s[0] - top) * s[1] for s in stats]
    total = sum(weights)
    mean = sum(w * p[:, :D].astype(f32) for w, p in zip(weights, parts)) / total
    write_payload(out, mean, top, total)
    rows = mean.astype(bf16)
    for o in range(OWNERS):
        spread[o] = rows


def encoder(
    lens, own_index, other_index, own_table, other_table, pos, gain, w_qkv, w_out, d_encoded,
    encoded, d_inputs, d_wide, e_wide,
):
    step = pl.program_id(0)

    @pl.when(step == 0)
    def _():
        for j in range(D // 128):
            d_wide[j] = d_encoded[:, j * 128 : (j + 1) * 128].astype(f32)

    at = lax.broadcasted_iota(jnp.int32, (ROWS, OWNERS * HALF), 1)
    x = dot_nn((at == own_index[...]).astype(bf16), own_table[...])
    x = x + dot_nn((at == other_index[...]).astype(bf16), other_table[...])
    x = x + pos[...]
    xhat, rstd = normalised(x)
    g = gain[...]
    packed = dot_nn((xhat * g).astype(bf16), w_qkv[...]).astype(bf16)
    q, k, v = packed[:, :D], packed[:, D : 2 * D], packed[:, 2 * D :]

    place = lax.broadcasted_iota(jnp.int32, (ROWS, 1), 0)
    length = jnp.full((ROWS, 1), 0, jnp.int32)
    first = jnp.full((ROWS, 1), 0, jnp.int32)
    for u in range(GROUP):
        here = (place >= u * LP) & (place < (u + 1) * LP)
        length = jnp.where(here, lens[step * GROUP + u], length)
        first = jnp.where(here, u * LP, first)
    column = lax.broadcasted_iota(jnp.int32, (ROWS, ROWS), 1)
    allowed = (column >= first) & (column <= place) & (column < first + length)
    live = (place - first) < length

    scores = jnp.where(allowed, dot_nt(q, k) / ROOT, MASKED)
    raised = jnp.exp(scores - jnp.max(scores, axis=-1, keepdims=True))
    probs = raised / jnp.sum(raised, axis=-1, keepdims=True)
    probs16 = probs.astype(bf16)
    attended = dot_nn(probs16, v).astype(bf16)
    updated = jnp.where(live, x + dot_nn(attended, w_out[...]), 0.0)
    cotangent = []
    for u in range(GROUP):
        rows = pl.ds(step * GROUP + u, L, stride=USERS)
        for j in range(D // 128):
            e_wide[j, rows, :] = updated[u * LP : u * LP + L, j * 128 : (j + 1) * 128]

    for u in range(GROUP):
        rows = pl.ds(step * GROUP + u, L, stride=USERS)
        one = jnp.concatenate([d_wide[j, rows, :] for j in range(D // 128)], axis=1)
        cotangent.append(jnp.concatenate([one, jnp.zeros((LP - L, D), f32)], axis=0))
    d_out = jnp.where(live, jnp.concatenate(cotangent, axis=0), 0.0)
    d_attended = dot_nt(d_out.astype(bf16), w_out[...]).astype(bf16)
    d_probs = dot_nt(d_attended, v).astype(bf16).astype(f32)
    d_v = dot_tn(probs16, d_attended).astype(bf16)
    d_scores = probs * (d_probs - jnp.sum(d_probs * probs, axis=-1, keepdims=True)) / ROOT
    d_scores = d_scores.astype(bf16)
    d_q = dot_nn(d_scores, k).astype(bf16)
    d_k = dot_tn(d_scores, q).astype(bf16)
    d_normed = dot_nt(d_q, w_qkv[:, :D]) + dot_nt(d_k, w_qkv[:, D : 2 * D]) + dot_nt(d_v, w_qkv[:, 2 * D :])
    d_normed = d_normed.astype(bf16).astype(f32)
    d_inputs[...] = (d_out + norm_back(d_normed, g, xhat, rstd)).astype(bf16)

    @pl.when(step == pl.num_programs(0) - 1)
    def _():
        for j in range(D // 128):
            encoded[:, j * 128 : (j + 1) * 128] = e_wide[j].astype(bf16)


def run_encoder(lens, own_index, other_index, own_table, other_table, pos, gain, w_qkv, w_out, d_encoded):
    full = lambda r, w: pl.BlockSpec((r, w), lambda j: (0, 0))
    part = lambda w: pl.BlockSpec((ROWS, w), lambda j: (j, 0))
    count = USERS * L
    return pl.pallas_call(
        encoder,
        grid=(USERS // GROUP,),
        in_specs=[
            SMEM, part(1), part(1), full(OWNERS * HALF, D), full(OWNERS * HALF, D), full(ROWS, D), full(1, D),
            full(D, 3 * D), full(D, D), full(count, D),
        ],
        out_specs=[full(count, D), part(D)],
        out_shape=[
            jax.ShapeDtypeStruct((count, D), bf16),
            jax.ShapeDtypeStruct((USERS * LP, D), bf16),
        ],
        scratch_shapes=[pltpu.VMEM((D // 128, count, 128), f32)] * 2,
        compiler_params=params(56),
        name="user_encoder",
    )(lens, own_index, other_index, own_table, other_table, pos, gain, w_qkv, w_out, d_encoded)


def scatter(own_index, peer_index, own_rows, peer_rows, out):
    count = USERS * LP
    block = out.shape[0]
    row = lax.broadcasted_iota(jnp.int32, (block, count), 0) + pl.program_id(0) * block
    total = dot_nn((row == own_index[...]).astype(bf16), own_rows[...])
    total = total + dot_nn((row == peer_index[...]).astype(bf16), peer_rows[...])
    out[...] = total.astype(bf16)


def run_scatter(own_index, peer_index, own_rows, peer_rows):
    count = USERS * LP
    steps = 4
    full = lambda r, w: pl.BlockSpec((r, w), lambda j: (0, 0))
    return pl.pallas_call(
        scatter,
        grid=(steps,),
        in_specs=[full(1, count), full(1, count), full(count, D), full(count, D)],
        out_specs=pl.BlockSpec((OWNERS * HALF // steps, D), lambda j: (j, 0)),
        out_shape=jax.ShapeDtypeStruct((OWNERS * HALF, D), bf16),
        compiler_params=params(40),
        name="scatter",
    )(own_index, peer_index, own_rows, peer_rows)


def frame_backward(
    core, d_mine, d_other, pay_mine, pay_other, query, frames, framed, gain, slope, w_up, w_down,
    out, grad, grad16, total, d_pooled, pay,
):
    step = pl.program_id(0)

    @pl.when(step == 0)
    def _():
        c = core[0]
        here = pl.ds(pl.multiple_of(c * HALF, HALF), HALF)
        there = pl.ds(pl.multiple_of((1 - c) * HALF, HALF), HALF)
        d_pooled[here, :] = d_mine[...].astype(f32)
        d_pooled[there, :] = d_other[...].astype(f32)
        pay[here, :] = pay_mine[...].astype(f32)
        pay[there, :] = pay_other[...].astype(f32)
        x = framed[...].astype(f32)
        q = query[...]
        top, whole = read_stats(pay)
        weight = jnp.exp(jnp.sum(x * q, axis=-1, keepdims=True) / ROOT - top) / whole
        dp = d_pooled[...]
        cross = jnp.sum(dp * x, axis=-1, keepdims=True)
        own = jnp.sum(dp * pay[:, :D], axis=-1, keepdims=True)
        d_out = weight * (dp + ((cross - own) / ROOT) * q)
        grad[...] = d_out
        grad16[...] = d_out.astype(bf16)
        total[...] = jnp.zeros_like(total)

    d_hidden = dot_nt(grad16[...], w_down[...]).astype(bf16).astype(f32)
    d_a = (d_hidden * slope[...].astype(f32)).astype(bf16)
    total[...] += dot_nt(d_a, w_up[...])

    @pl.when(step == pl.num_programs(0) - 1)
    def _():
        xhat, rstd = normalised(frames[...].astype(f32))
        d_normed = total[...].astype(bf16).astype(f32)
        out[...] = (grad[...] + norm_back(d_normed, gain[...], xhat, rstd)).astype(bf16)


def run_frame_backward(core, d_mine, d_other, pay_mine, pay_other, query, frames, framed, gain, slope, w_up, w_down):
    steps = 4
    width = HID // steps
    rows = frames.shape[0]
    full = lambda r, w: pl.BlockSpec((r, w), lambda j: (0, 0))
    return pl.pallas_call(
        frame_backward,
        grid=(steps,),
        in_specs=[
            SMEM, full(HALF, D), full(HALF, D), full(HALF, PAY), full(HALF, PAY), full(1, D), full(rows, D),
            full(rows, D), full(1, D),
            pl.BlockSpec((rows, width), lambda j: (0, j)),
            pl.BlockSpec((D, width), lambda j: (0, j)),
            pl.BlockSpec((width, D), lambda j: (j, 0)),
        ],
        out_specs=full(rows, D),
        out_shape=jax.ShapeDtypeStruct((rows, D), bf16),
        scratch_shapes=[
            pltpu.VMEM((rows, D), f32), pltpu.VMEM((rows, D), bf16), pltpu.VMEM((rows, D), f32),
            pltpu.VMEM((rows, D), f32), pltpu.VMEM((rows, PAY), f32),
        ],
        compiler_params=params(40),
        name="frame_backward",
    )(core, d_mine, d_other, pay_mine, pay_other, query, frames, framed, gain, slope, w_up, w_down)


def swap_with(x, bits):
    pairs = [(i, i ^ bits) for i in range(8)]
    return lax.ppermute(x, "frame", pairs)


def spread_along_x(x):
    return [swap_with(x, 2 * k) for k in (1, 2, 3)]


def shards(
    frames, frame_gain, w_up, w_down, pool_query, pos_embed, user_gain, w_qkv, w_out,
    request_rows, hist_slot, hist_len, d_encoded,
):
    rows = frames.shape[0]
    c = lax.axis_index("frame") % 2
    core = c.astype(jnp.int32).reshape(1)
    flat_frames = frames.reshape(rows, D)
    gain = frame_gain.reshape(1, D)
    query = pool_query.reshape(1, D)

    mine, other, framed, slope = run_frame_forward(core, flat_frames, gain, w_up, w_down)
    theirs = swap_with(other, 1)
    payload = jax.ShapeDtypeStruct((HALF, PAY), bf16)
    pair = pl.pallas_call(
        pool_pair, in_specs=[VMEM] * 3, out_specs=VMEM, out_shape=payload, name="pool_pair",
    )(mine, theirs, query)
    spread, pay_mine = pl.pallas_call(
        pool_all, in_specs=[VMEM] * 4, out_specs=[VMEM] * 2,
        out_shape=[jax.ShapeDtypeStruct((OWNERS, HALF, D), bf16), payload], name="pool_all",
    )(pair, *spread_along_x(pair))
    table = lax.all_to_all(spread, "dp", split_axis=0, concat_axis=0, tiled=True).reshape(OWNERS * HALF, D)
    other_table = swap_with(table, 1)
    pay_other = swap_with(pay_mine, 1)

    slots = jnp.pad(hist_slot, ((0, 0), (0, LP - L)), constant_values=-1).reshape(USERS * LP, 1)
    known = jnp.arange(OWNERS * CAP, dtype=jnp.int32)[None, :]
    local = jnp.sum(jnp.where(slots == known, request_rows.reshape(1, OWNERS * CAP), 0), axis=1, keepdims=True)
    position = jnp.where(slots >= 0, (slots // CAP) * HALF + local % HALF, -1)
    own_index = jnp.where(local // HALF == c, position, -1)
    other_index = jnp.where(local // HALF == c, -1, position)
    peer_index = swap_with(other_index.reshape(1, USERS * LP), 1)

    pos = jnp.tile(jnp.pad(pos_embed.astype(f32), ((0, LP - L), (0, 0))), (GROUP, 1))
    cotangent = jnp.transpose(d_encoded, (1, 0, 2)).reshape(USERS * L, D)
    encoded, d_inputs = run_encoder(
        hist_len, own_index, other_index, table, other_table, pos, user_gain.reshape(1, D), w_qkv, w_out, cotangent
    )
    peer_rows = swap_with(d_inputs, 1)
    d_table = run_scatter(own_index.reshape(1, USERS * LP), peer_index, d_inputs, peer_rows)
    returned = lax.all_to_all(
        d_table.reshape(OWNERS, HALF, D), "dp", split_axis=0, concat_axis=0, tiled=True
    )
    partial = jnp.sum(returned.astype(f32), axis=0).astype(bf16)
    d_mine = sum(part.astype(f32) for part in [partial] + spread_along_x(partial)).astype(bf16)
    d_other = swap_with(d_mine, 1)
    d_frames = run_frame_backward(
        core, d_mine, d_other, pay_mine, pay_other, query, flat_frames, framed, gain, slope, w_up, w_down
    )
    encoded = jnp.transpose(encoded.reshape(L, USERS, D), (1, 0, 2))
    return encoded, d_frames.reshape(rows, 1, D)


def solution(mesh):
    in_specs = (
        P("dp", "frame", None),
        P(),
        P(),
        P(),
        P(),
        P(),
        P(),
        P(),
        P(),
        P(("dp", "frame"), None, None),
        P(("dp", "frame"), None),
        P(("dp", "frame")),
        P(("dp", "frame"), None, None),
    )
    out_specs = (P(("dp", "frame"), None, None), P("dp", "frame", None))
    return jax.shard_map(shards, mesh=mesh, in_specs=in_specs, out_specs=out_specs, check_vma=False)
```

time: 322 us -> 154 us (0.48)
  other arithmetic: 71.2 us -> 3.71 us
  matrix products: 64.5 us -> 0 us
  waiting for transfers between devices: 65.9 us -> 13.3 us
  Pallas kernels: 0 us -> 46.8 us
  local copies, waits for them, and re-layouts: 62.4 us -> 17.2 us
  blocking collectives: 19.7 us -> 54.7 us
  between operations: 14.3 us -> 0.76 us
  starting transfers between devices: 20.9 us -> 16.5 us
    dot_general x14 -> x0, matrix products: 64.5 us -> none  [the longest x2 15 us: user_encoder(): jnp.dot(normed, w_qkv, preferred_element_type=jnp.float32)]
    all_to_all x0 -> x2, blocking collectives: none -> 54.7 us  [the longest x1 29.8 us: shards(): lax.all_to_all(spread, 'dp', split_axis=0, concat_axis=0, tiled=True)]
    psum x1 -> x0, waiting for transfers between devices: 47.6 us -> none  [shards(): lax.psum(partial_grad.astype(jnp.bfloat16), 'frame').astype(jnp.float32)]
    pallas_call x0 -> x6, Pallas kernels: none -> 46.8 us  [the longest x1 29.3 us: run_encoder(): pl.pallas_call(encoder, grid=(USERS // GROUP,), in_specs=[SMEM, part(1),...]
    add x15 -> x0, other arithmetic: 23.3 us -> none  [the longest x7 13.8 us: combine_softmax(): sum_a * scale_a[:, None] + sum_b * scale_b[:, None]]
    all_to_all x3 -> x0, starting transfers between devices: 20.6 us -> none  [the longest x1 8.62 us: shards(): lax.all_to_all(wanted, 'dp', split_axis=0, concat_axis=0, tiled=True)]
    all_gather x2 -> x0, blocking collectives: 19.7 us -> none  [merged(): everything = jax.tree.map(lambda part: lax.all_gather(part, axis), x)]
    all_to_all x3 -> x0, waiting for transfers between devices: 18.2 us -> none  [the longest x1 16.6 us: shards(): lax.all_to_all(d_slots.reshape(owner_count, slot_count, feature_width).as...]
  transfers between devices with their start and end apart: 5 -> 12, of which waited for: 3 -> 8; matrix products, arithmetic and copies ran while one was open for 13% -> 3% of each run, Pallas kernels for 0% -> 0%
where the time goes in v1:
time: 154 us; the launch traced here: 153 us
  blocking collectives  54.7 us (36%)
  Pallas kernels  46.8 us (30%)
  local copies, waits for them, and re-layouts  17.2 us (11%)
  starting transfers between devices  16.5 us (11%)
  waiting for transfers between devices  13.3 us (9%)
  other arithmetic  3.71 us (2%)
    all_to_all x1, blocking collectives, shards(): lax.all_to_all(spread, 'dp', split_axis=0, concat_axis=0, tiled=True)  29.8 us
    pallas_call x1, Pallas kernels, run_encoder(): pl.pallas_call(encoder, grid=(USERS // GROUP,), in_specs=[SMEM, part(1),...  29.3 us
    all_to_all x1, blocking collectives, shards(): lax.all_to_all(d_table.reshape(OWNERS, HALF, D), 'dp', split_axis=0, conc...  24.9 us
    ppermute x12, starting transfers between devices, swap_with(): return lax.ppermute(x, 'frame', pairs)  16.5 us
    unnamed x40, local copies, waits for them, and re-layouts  14 us
    ppermute x12, waiting for transfers between devices, swap_with(): return lax.ppermute(x, 'frame', pairs)  13.3 us
    pallas_call x1, Pallas kernels, run_frame_backward(): pl.pallas_call(frame_backward, grid=(steps,), in_specs=[SMEM, full(HALF,...  5.6 us
    pallas_call x1, Pallas kernels, run_scatter(): pl.pallas_call(scatter, grid=(steps,), in_specs=[full(1, count), full(1,...  3.92 us
  transfers between devices with their start and end apart: 12, of which 8 were waited for; matrix products, arithmetic and copies ran while one was open for 3% of the time, Pallas kernels for 0%

profile of v1, /device:TPU:1, one launch (start us, length us, event | category | flops | bytes accessed | tf_op | source)
XLA Modules:
  0.0 153.0 jit_solution(5112236375745477252)
XLA Ops:
  0.6 0.7 reshape.506.gain
  1.3 2.3 %copy-done = bf16[768,3072]{1,0:T(8,128)(2,1)S(1)} copy-done((bf16[768,3072]{1,0:T(8,128)(2,1)S(1)}, bf16[768,3072]{1,0:T(8,128)(2,1)}, u32[]{:S(2)}) %copy-start) | copy-done | bytes 4718616
  3.7 2.3 %copy-done.2 = bf16[3072,768]{1,0:T(8,128)(2,1)S(1)} copy-done((bf16[3072,768]{1,0:T(8,128)(2,1)S(1)}, bf16[3072,768]{1,0:T(8,128)(2,1)}, u32[]{:S(2)}) %copy-start.2) | copy-done | bytes 4718616
  6.0 0.9 copy-done.5
  6.9 3.7 %frame_forward.1 = (bf16[64,768]{1,0:T(8,128)(2,1)S(1)}, bf16[64,768]{1,0:T(8,128)(2,1)S(1)}, bf16[128,768]{1,0:T(8,128)(2,1)S(1)}, bf16[128,3072]{1,0:T(8,128)(2,1)S(1)}) custom-call(s32[1]{0:T(128)} %bitcast.core, bf16[128,768]{1,0:T(8,128)(2,1)S(1)} %bitcast.13, f32[1,768]{1,0:T(1,128)S(1)} %reshape.506.gain, bf16[768,3072]{1,0:T(8,128)(2,1)S(1)} %copy-done, ...), custom_call_target="tpu_custom_call" | custom-call | tf_op jit(solution)/shard_map/frame_forward/pallas_call | solution.py:92
  10.6 0.0 copy-start.8
  10.6 0.6 copy-done.8
  11.2 1.4 collective-permute-start
  12.7 0.0 copy-done.18
  12.7 0.6 reshape.507.query
  13.3 0.3 collective-permute-done.theirs
  13.6 0.6 copy-done.14
  14.3 1.8 %pool_pair.1.p0 = bf16[64,896]{1,0:T(8,128)(2,1)} custom-call(bf16[64,768]{1,0:T(8,128)(2,1)} %copy-done.8, bf16[64,768]{1,0:T(8,128)(2,1)} %copy-done.14, f32[1,768]{1,0:T(1,128)} %reshape.507.query), custom_call_target="tpu_custom_call" | custom-call | tf_op jit(solution)/shard_map/pool_pair/pallas_call | solution.py:363
  16.0 1.3 collective-permute-start.1
  17.3 2.5 %collective-permute-start.2 = (bf16[64,896]{1,0:T(8,128)(2,1)}, bf16[64,896]{1,0:T(8,128)(2,1)S(1)}, u32[]{:S(2)}, u32[]{:S(2)}) collective-permute-start(bf16[64,896]{1,0:T(8,128)(2,1)} %pool_pair.1.p0), channel_id=1, source_target_pairs={{0,4},{1,5},{2,6},{3,7},{4,0},{5,1},{6,2},{7,3},{8,12},{9,13},{10,... | collective-permute-start | bytes 344072 | tf_op jit(solution)/shard_map/ppermute | solution.py:342
  19.8 0.1 collective-permute-start.3
  19.9 0.7 collective-permute-done.1.p1
  20.6 4.7 %collective-permute-done.2.p2 = bf16[64,896]{1,0:T(8,128)(2,1)S(1)} collective-permute-done((bf16[64,896]{1,0:T(8,128)(2,1)}, bf16[64,896]{1,0:T(8,128)(2,1)S(1)}, u32[]{:S(2)}, u32[]{:S(2)}) %collective-permute-start.2) | collective-permute-done | bytes 114720 | tf_op jit(solution)/shard_map/ppermute | solution.py:342
  25.3 2.5 %collective-permute-done.3.p3 = bf16[64,896]{1,0:T(8,128)(2,1)S(1)} collective-permute-done((bf16[64,896]{1,0:T(8,128)(2,1)}, bf16[64,896]{1,0:T(8,128)(2,1)S(1)}, u32[]{:S(2)}, u32[]{:S(2)}) %collective-permute-start.3) | collective-permute-done | bytes 114720 | tf_op jit(solution)/shard_map/ppermute | solution.py:342
  27.9 0.0 copy-done.11
  27.9 0.0 copy-done.12
  27.9 0.6 copy-done.13
  28.5 2.6 %pool_all.1 = (bf16[16,64,768]{2,1,0:T(8,128)(2,1)}, bf16[64,896]{1,0:T(8,128)(2,1)}) custom-call(bf16[64,896]{1,0:T(8,128)(2,1)} %pool_pair.1.p0, bf16[64,896]{1,0:T(8,128)(2,1)} %copy-done.11, bf16[64,896]{1,0:T(8,128)(2,1)} %copy-done.12, bf16[64,896]{1,0:T(8,128)(2,1)} %copy-done.13), custom_call_target="tpu_custom_call" | custom-call | tf_op jit(solution)/shard_map/pool_all/pallas_call | solution.py:366
  31.1 0.0 copy-start.15
  31.1 29.8 %all_to_all.10 = bf16[16,64,768]{2,1,0:T(8,128)(2,1)} all-to-all(bf16[16,64,768]{2,1,0:T(8,128)(2,1)} %get-tuple-element.12), channel_id=1, replica_groups=mesh['dp'=16,'frame'=8] {'dp'}, dimensions={0} | all-to-all | bytes 3145728 | tf_op jit(solution)/shard_map/all_to_all | solution.py:370
  60.9 2.0 %collective-permute-start.4 = (bf16[1024,768]{1,0:T(8,128)(2,1)}, bf16[1024,768]{1,0:T(8,128)(2,1)S(1)}, u32[]{:S(2)}, u32[]{:S(2)}) collective-permute-start(bf16[1024,768]{1,0:T(8,128)(2,1)} %bitcast.2.own_table), channel_id=1, source_target_pairs={{0,1},{1,0},{2,3},{3,2},{4,5},{5,4},{6,7},{7,6},{8,9},{9,8},{10,11... | collective-permute-start | bytes 4718600 | tf_op jit(solution)/shard_map/ppermute | solution.py:342
  62.9 0.0 copy-done.17
  62.9 0.1 eq.54
  63.0 0.2 reshape.515
  63.1 0.0 copy-done.16
  63.2 0.1 broadcast_in_dim.21
  63.2 0.6 reshape.509.gain
  63.8 0.0 copy-done.15
  63.8 0.7 select_reduce_fusion
  64.5 1.5 %broadcast_select_fusion.1 = (s32[896,1]{1,0:T(8,128)}, s32[896,1]{1,0:T(8,128)S(1)}) fusion(s32[]{:T(128)} %select_n.143, s32[896]{0:T(1024)S(1)} %select_reduce_fusion, s32[896,1]{1,0:T(8,128)S(1)} %reshape.515), kind=kLoop, calls=%fused_computation.29 | loop fusion | flops 35840 | bytes 14340 | tf_op jit(solution)/shard_map/jit(_where)/select_n | solution.py:379
  66.0 1.1 broadcast_select_fusion.own_index
  67.2 0.0 collective-permute-done.4.other_table
  67.2 0.9 tile.4
  68.1 0.4 copy-done.10
  68.6 29.3 %user_encoder.1 = (bf16[800,768]{1,0:T(8,128)(2,1)}, bf16[896,768]{1,0:T(8,128)(2,1)}) custom-call(s32[16]{0:T(128)} %lens.1, s32[896,1]{1,0:T(8,128)} %broadcast_select_fusion.own_index, s32[896,1]{1,0:T(8,128)} %get-tuple-element.20.other_index, bf16[1024,768]{1,0:T(8,128)(2,1)} %bitcast.2.own_table, bf16[1024,768]{1,0:T(8,128)(2,1)} %copy-done.10, ...), custom_call_target="tpu_custom_call" | custom-call | tf_op jit(solution)/shard_map/user_encoder/pallas_call | solution.py:234
  97.9 0.0 collective-permute-start.6
  97.9 0.1 reshape.512
  98.0 0.1 compare_select_fusion.7
  98.1 0.6 collective-permute-start.5
  98.7 2.4 %collective-permute-done.5.peer_index = s32[1,896]{1,0:T(1,128)S(1)} collective-permute-done((s32[1,896]{1,0:T(1,128)S(1)}, s32[1,896]{1,0:T(1,128)S(1)}, u32[]{:S(2)}, u32[]{:S(2)}) %collective-permute-start.5) | collective-permute-done | bytes 3616 | tf_op jit(solution)/shard_map/ppermute | solution.py:342
  101.0 0.2 collective-permute-done.6.peer_rows
  101.3 1.3 copy-done.4
  102.6 3.9 %scatter.1 = bf16[1024,768]{1,0:T(8,128)(2,1)S(1)} custom-call(s32[1,896]{1,0:T(1,128)S(1)} %compare_select_fusion.8.own_index, s32[1,896]{1,0:T(1,128)S(1)} %collective-permute-done.5.peer_index, bf16[896,768]{1,0:T(8,128)(2,1)S(1)} %copy-done.4, bf16[896,768]{1,0:T(8,128)(2,1)S(1)} %collective-permute-done.6.peer_rows), custom_call_target="tpu_custom_call" | custom-call | tf_op jit(solution)/shard_map/scatter/pallas_call | solution.py:265
  106.5 24.9 %all_to_all.11 = bf16[16,64,768]{2,1,0:T(8,128)(2,1)S(1)} all-to-all(bf16[16,64,768]{2,1,0:T(8,128)(2,1)S(1)} %bitcast.12), channel_id=1, replica_groups=mesh['dp'=16,'frame'=8] {'dp'}, dimensions={0} | all-to-all | bytes 3145728 | tf_op jit(solution)/shard_map/all_to_all | solution.py:389
  131.4 0.2 reduce_sum.28
  131.7 0.1 collective-permute-start.7
  131.7 1.9 %collective-permute-start.8 = (bf16[64,768]{1,0:T(8,128)(2,1)S(1)}, bf16[64,768]{1,0:T(8,128)(2,1)S(1)}, u32[]{:S(2)}, u32[]{:S(2)}) collective-permute-start(bf16[64,768]{1,0:T(8,128)(2,1)S(1)} %reduce_sum.28), channel_id=1, source_target_pairs={{0,4},{1,5},{2,6},{3,7},{4,0},{5,1},{6,2},{7,3},{8,12},{9,13},{10,... | collective-permute-start | bytes 294920 | tf_op jit(solution)/shard_map/ppermute | solution.py:342
  133.7 1.9 %collective-permute-start.9 = (bf16[64,768]{1,0:T(8,128)(2,1)S(1)}, bf16[64,768]{1,0:T(8,128)(2,1)S(1)}, u32[]{:S(2)}, u32[]{:S(2)}) collective-permute-start(bf16[64,768]{1,0:T(8,128)(2,1)S(1)} %reduce_sum.28), channel_id=1, source_target_pairs={{0,6},{1,7},{2,4},{3,5},{4,2},{5,3},{6,0},{7,1},{8,14},{9,15},{10,... | collective-permute-start | bytes 294920 | tf_op jit(solution)/shard_map/ppermute | solution.py:342
  135.6 2.4 %collective-permute-start.11 = (bf16[64,896]{1,0:T(8,128)(2,1)S(1)}, bf16[64,896]{1,0:T(8,128)(2,1)S(1)}, u32[]{:S(2)}, u32[]{:S(2)}) collective-permute-start(bf16[64,896]{1,0:T(8,128)(2,1)S(1)} %copy-done.7), channel_id=1, source_target_pairs={{0,1},{1,0},{2,3},{3,2},{4,5},{5,4},{6,7},{7,6},{8,9},{9,8},{10,11... | collective-permute-start | bytes 344072 | tf_op jit(solution)/shard_map/ppermute | solution.py:342
  138.0 0.0 collective-permute-done.7
  138.0 0.0 collective-permute-done.8
  138.0 1.4 collective-permute-done.9
  139.4 0.1 add_convert_fusion.d_mine
  139.5 2.3 %collective-permute-start.10 = (bf16[64,768]{1,0:T(8,128)(2,1)S(1)}, bf16[64,768]{1,0:T(8,128)(2,1)S(1)}, u32[]{:S(2)}, u32[]{:S(2)}) collective-permute-start(bf16[64,768]{1,0:T(8,128)(2,1)S(1)} %add_convert_fusion.d_mine), channel_id=1, source_target_pairs={{0,1},{1,0},{2,3},{3,2},{4,5},{5,4},{6,7},{7,6},{8,9},{9,8},{10,11... | collective-permute-start | bytes 294920 | tf_op jit(solution)/shard_map/ppermute | solution.py:342
  141.8 0.0 collective-permute-done.11.pay_other
  141.8 0.9 collective-permute-done.10.d_other
  142.7 2.3 %copy-done.1 = bf16[768,3072]{1,0:T(8,128)(2,1)S(1)} copy-done((bf16[768,3072]{1,0:T(8,128)(2,1)S(1)}, bf16[768,3072]{1,0:T(8,128)(2,1)}, u32[]{:S(2)}) %copy-start.1) | copy-done | bytes 4718616
  145.1 2.3 %copy-done.3 = bf16[3072,768]{1,0:T(8,128)(2,1)S(1)} copy-done((bf16[3072,768]{1,0:T(8,128)(2,1)S(1)}, bf16[3072,768]{1,0:T(8,128)(2,1)}, u32[]{:S(2)}) %copy-start.3) | copy-done | bytes 4718616
  147.4 5.6 %frame_backward.1 = bf16[128,768]{1,0:T(8,128)(2,1)} custom-call(s32[1]{0:T(128)} %bitcast.core, bf16[64,768]{1,0:T(8,128)(2,1)S(1)} %add_convert_fusion.d_mine, bf16[64,768]{1,0:T(8,128)(2,1)S(1)} %collective-permute-done.10.d_other, bf16[64,896]{1,0:T(8,128)(2,1)S(1)} %copy-done.7, bf16[64,896]{1,0:T(8,128)(2,1)S(1)} %collective-permute-done.11.pay_other, ...), custom_call_target="tpu_custom_call" | custom-call | tf_op jit(solution)/shard_map/frame_backward/pallas_call | solution.py:319
  (25 shorter events, 0.1 us)
Async XLA Ops:
  1.3 2.3 %copy-start = (bf16[768,3072]{1,0:T(8,128)(2,1)S(1)}, bf16[768,3072]{1,0:T(8,128)(2,1)}, u32[]{:S(2)}) copy-start(bf16[768,3072]{1,0:T(8,128)(2,1)} %w_up.3) | copy-start | bytes 14155780
  3.7 2.3 %copy-start.2 = (bf16[3072,768]{1,0:T(8,128)(2,1)S(1)}, bf16[3072,768]{1,0:T(8,128)(2,1)}, u32[]{:S(2)}) copy-start(bf16[3072,768]{1,0:T(8,128)(2,1)} %w_down.3) | copy-start | bytes 14155780
  6.0 0.9 copy-start.5
  6.9 5.7 %copy-start.18 = (f32[768]{0:T(1024)S(1)}, f32[768]{0:T(1024)}, u32[]{:S(2)}) copy-start(f32[768]{0:T(1024)} %param.17) | copy-start | bytes 9220
  10.6 0.6 copy-start.8
  11.2 2.4 %collective-permute-start = (bf16[64,768]{1,0:T(8,128)(2,1)S(1)}, bf16[64,768]{1,0:T(8,128)(2,1)S(1)}, u32[]{:S(2)}, u32[]{:S(2)}) collective-permute-start(bf16[64,768]{1,0:T(8,128)(2,1)S(1)} %get-tuple-element.11), channel_id=1, source_target_pairs={{0,1},{1,0},{2,3},{3,2},{4,5},{5,4},{6,7},{7,6},{8,9},{9,8},{10,11... | collective-permute-start | bytes 294920 | tf_op jit(solution)/shard_map/ppermute | solution.py:342
  13.6 0.6 copy-start.14
  16.0 4.6 %collective-permute-start.1 = (bf16[64,896]{1,0:T(8,128)(2,1)}, bf16[64,896]{1,0:T(8,128)(2,1)S(1)}, u32[]{:S(2)}, u32[]{:S(2)}) collective-permute-start(bf16[64,896]{1,0:T(8,128)(2,1)} %pool_pair.1.p0), channel_id=1, source_target_pairs={{0,2},{1,3},{2,0},{3,1},{4,6},{5,7},{6,4},{7,5},{8,10},{9,11},{10,... | collective-permute-start | bytes 344072 | tf_op jit(solution)/shard_map/ppermute | solution.py:342
  17.3 8.0 %collective-permute-start.2 = (bf16[64,896]{1,0:T(8,128)(2,1)}, bf16[64,896]{1,0:T(8,128)(2,1)S(1)}, u32[]{:S(2)}, u32[]{:S(2)}) collective-permute-start(bf16[64,896]{1,0:T(8,128)(2,1)} %pool_pair.1.p0), channel_id=1, source_target_pairs={{0,4},{1,5},{2,6},{3,7},{4,0},{5,1},{6,2},{7,3},{8,12},{9,13},{10,... | collective-permute-start | bytes 344072 | tf_op jit(solution)/shard_map/ppermute | solution.py:342
  19.8 8.1 %collective-permute-start.3 = (bf16[64,896]{1,0:T(8,128)(2,1)}, bf16[64,896]{1,0:T(8,128)(2,1)S(1)}, u32[]{:S(2)}, u32[]{:S(2)}) collective-permute-start(bf16[64,896]{1,0:T(8,128)(2,1)} %pool_pair.1.p0), channel_id=1, source_target_pairs={{0,6},{1,7},{2,4},{3,5},{4,2},{5,3},{6,0},{7,1},{8,14},{9,15},{10,... | collective-permute-start | bytes 344072 | tf_op jit(solution)/shard_map/ppermute | solution.py:342
  20.6 7.3 %copy-start.11 = (bf16[64,896]{1,0:T(8,128)(2,1)}, bf16[64,896]{1,0:T(8,128)(2,1)S(1)}, u32[]{:S(2)}) copy-start(bf16[64,896]{1,0:T(8,128)(2,1)S(1)} %collective-permute-done.1.p1) | copy-start | bytes 344068
  25.3 2.5 %copy-start.12 = (bf16[64,896]{1,0:T(8,128)(2,1)}, bf16[64,896]{1,0:T(8,128)(2,1)S(1)}, u32[]{:S(2)}) copy-start(bf16[64,896]{1,0:T(8,128)(2,1)S(1)} %collective-permute-done.2.p2) | copy-start | bytes 344068
  27.9 0.6 copy-start.13
  31.1 31.8 %copy-start.17 = (s32[16,50]{1,0:T(8,128)S(1)}, s32[16,50]{1,0:T(8,128)}, u32[]{:S(2)}) copy-start(s32[16,50]{1,0:T(8,128)} %param.23) | copy-start | bytes 9604
  31.1 32.1 %copy-start.16 = (s32[1,16,64]{2,1,0:T(8,128)S(1)}, s32[1,16,64]{2,1,0:T(8,128)}, u32[]{:S(2)}) copy-start(s32[1,16,64]{2,1,0:T(8,128)} %param.22) | copy-start | bytes 12292
  31.1 32.1 %copy-start.19 = (f32[768]{0:T(1024)S(1)}, f32[768]{0:T(1024)}, u32[]{:S(2)}) copy-start(f32[768]{0:T(1024)} %param.19) | copy-start | bytes 9220
  31.1 32.7 %copy-start.15 = (bf16[50,768]{1,0:T(8,128)(2,1)S(1)}, bf16[50,768]{1,0:T(8,128)(2,1)}, u32[]{:S(2)}) copy-start(bf16[50,768]{1,0:T(8,128)(2,1)} %param.18) | copy-start | bytes 230404
  60.9 6.3 %collective-permute-start.4 = (bf16[1024,768]{1,0:T(8,128)(2,1)}, bf16[1024,768]{1,0:T(8,128)(2,1)S(1)}, u32[]{:S(2)}, u32[]{:S(2)}) collective-permute-start(bf16[1024,768]{1,0:T(8,128)(2,1)} %bitcast.2.own_table), channel_id=1, source_target_pairs={{0,1},{1,0},{2,3},{3,2},{4,5},{5,4},{6,7},{7,6},{8,9},{9,8},{10,11... | collective-permute-start | bytes 4718600 | tf_op jit(solution)/shard_map/ppermute | solution.py:342
  67.2 1.4 copy-start.10
  97.9 3.3 %collective-permute-start.6 = (bf16[896,768]{1,0:T(8,128)(2,1)}, bf16[896,768]{1,0:T(8,128)(2,1)S(1)}, u32[]{:S(2)}, u32[]{:S(2)}) collective-permute-start(bf16[896,768]{1,0:T(8,128)(2,1)} %get-tuple-element.14.own_rows), channel_id=1, source_target_pairs={{0,1},{1,0},{2,3},{3,2},{4,5},{5,4},{6,7},{7,6},{8,9},{9,8},{10,11... | collective-permute-start | bytes 4128776 | tf_op jit(solution)/shard_map/ppermute | solution.py:342
  98.1 3.0 %collective-permute-start.5 = (s32[1,896]{1,0:T(1,128)S(1)}, s32[1,896]{1,0:T(1,128)S(1)}, u32[]{:S(2)}, u32[]{:S(2)}) collective-permute-start(s32[1,896]{1,0:T(1,128)S(1)} %get-tuple-element.18), channel_id=1, source_target_pairs={{0,1},{1,0},{2,3},{3,2},{4,5},{5,4},{6,7},{7,6},{8,9},{9,8},{10,11... | collective-permute-start | bytes 10760 | tf_op jit(solution)/shard_map/ppermute | solution.py:342
  101.2 1.3 copy-start.4
  131.4 4.2 %copy-start.7 = (bf16[64,896]{1,0:T(8,128)(2,1)S(1)}, bf16[64,896]{1,0:T(8,128)(2,1)}, u32[]{:S(2)}) copy-start(bf16[64,896]{1,0:T(8,128)(2,1)} %get-tuple-element.15.pay_mine) | copy-start | bytes 344068
  131.4 11.3 %copy-start.6 = (bf16[128,1,768]{2,0,1:T(8,128)(2,1)S(1)}, bf16[128,1,768]{2,0,1:T(8,128)(2,1)}, u32[]{:S(2)}) copy-start(bf16[128,1,768]{2,0,1:T(8,128)(2,1)} %param.13) | copy-start | bytes 589828
  131.4 11.3 %copy-start.9 = (f32[1,768]{1,0:T(1,128)S(1)}, f32[1,768]{1,0:T(1,128)}, u32[]{:S(2)}) copy-start(f32[1,768]{1,0:T(1,128)} %reshape.507.query) | copy-start | bytes 9220
  131.7 6.4 %collective-permute-start.7 = (bf16[64,768]{1,0:T(8,128)(2,1)S(1)}, bf16[64,768]{1,0:T(8,128)(2,1)S(1)}, u32[]{:S(2)}, u32[]{:S(2)}) collective-permute-start(bf16[64,768]{1,0:T(8,128)(2,1)S(1)} %reduce_sum.28), channel_id=1, source_target_pairs={{0,2},{1,3},{2,0},{3,1},{4,6},{5,7},{6,4},{7,5},{8,10},{9,11},{10,... | collective-permute-start | bytes 294920 | tf_op jit(solution)/shard_map/ppermute | solution.py:342
  131.7 6.3 %collective-permute-start.8 = (bf16[64,768]{1,0:T(8,128)(2,1)S(1)}, bf16[64,768]{1,0:T(8,128)(2,1)S(1)}, u32[]{:S(2)}, u32[]{:S(2)}) collective-permute-start(bf16[64,768]{1,0:T(8,128)(2,1)S(1)} %reduce_sum.28), channel_id=1, source_target_pairs={{0,4},{1,5},{2,6},{3,7},{4,0},{5,1},{6,2},{7,3},{8,12},{9,13},{10,... | collective-permute-start | bytes 294920 | tf_op jit(solution)/shard_map/ppermute | solution.py:342
  133.7 5.7 %collective-permute-start.9 = (bf16[64,768]{1,0:T(8,128)(2,1)S(1)}, bf16[64,768]{1,0:T(8,128)(2,1)S(1)}, u32[]{:S(2)}, u32[]{:S(2)}) collective-permute-start(bf16[64,768]{1,0:T(8,128)(2,1)S(1)} %reduce_sum.28), channel_id=1, source_target_pairs={{0,6},{1,7},{2,4},{3,5},{4,2},{5,3},{6,0},{7,1},{8,14},{9,15},{10,... | collective-permute-start | bytes 294920 | tf_op jit(solution)/shard_map/ppermute | solution.py:342
  135.6 6.2 %collective-permute-start.11 = (bf16[64,896]{1,0:T(8,128)(2,1)S(1)}, bf16[64,896]{1,0:T(8,128)(2,1)S(1)}, u32[]{:S(2)}, u32[]{:S(2)}) collective-permute-start(bf16[64,896]{1,0:T(8,128)(2,1)S(1)} %copy-done.7), channel_id=1, source_target_pairs={{0,1},{1,0},{2,3},{3,2},{4,5},{5,4},{6,7},{7,6},{8,9},{9,8},{10,11... | collective-permute-start | bytes 344072 | tf_op jit(solution)/shard_map/ppermute | solution.py:342
  139.5 3.2 %collective-permute-start.10 = (bf16[64,768]{1,0:T(8,128)(2,1)S(1)}, bf16[64,768]{1,0:T(8,128)(2,1)S(1)}, u32[]{:S(2)}, u32[]{:S(2)}) collective-permute-start(bf16[64,768]{1,0:T(8,128)(2,1)S(1)} %add_convert_fusion.d_mine), channel_id=1, source_target_pairs={{0,1},{1,0},{2,3},{3,2},{4,5},{5,4},{6,7},{7,6},{8,9},{9,8},{10,11... | collective-permute-start | bytes 294920 | tf_op jit(solution)/shard_map/ppermute | solution.py:342
  142.7 2.3 %copy-start.1 = (bf16[768,3072]{1,0:T(8,128)(2,1)S(1)}, bf16[768,3072]{1,0:T(8,128)(2,1)}, u32[]{:S(2)}) copy-start(bf16[768,3072]{1,0:T(8,128)(2,1)} %w_up.3) | copy-start | bytes 14155780
  145.1 2.3 %copy-start.3 = (bf16[3072,768]{1,0:T(8,128)(2,1)S(1)}, bf16[3072,768]{1,0:T(8,128)(2,1)}, u32[]{:S(2)}) copy-start(bf16[3072,768]{1,0:T(8,128)(2,1)} %w_down.3) | copy-start | bytes 14155780

commit v2 on v1

v2 whole, which is shorter than its diff:
```python
import functools
import math

import jax
import jax.numpy as jnp
from jax import lax
from jax.experimental import pallas as pl
from jax.experimental.pallas import tpu as pltpu
from jax.sharding import PartitionSpec as P

D = 768
HID = 3072
L = 50
LP = 56
USERS = 16
GROUP = 8
ROWS = GROUP * LP
SUB = 4
SUB_ROWS = SUB * LP
ENC_MB = 28
OWNERS = 16
HALF = 64
CAP = 64
PAY = D + 128
EPS = 1e-6
ROOT = math.sqrt(D)
MASKED = -1e9
AXES = ("dp", "frame")
f32 = jnp.float32
bf16 = jnp.bfloat16
VMEM = pl.BlockSpec(memory_space=pltpu.VMEM)
SMEM = pl.BlockSpec(memory_space=pltpu.SMEM)
ANY = pl.BlockSpec(memory_space=pl.ANY)
HBM = pl.BlockSpec(memory_space=pltpu.HBM)
PARTS = 4
FRAME_MB = 16


def dot_nn(a, b):
    return lax.dot_general(a, b, (((1,), (0,)), ((), ())), preferred_element_type=f32)


def dot_nt(a, b):
    return lax.dot_general(a, b, (((1,), (1,)), ((), ())), preferred_element_type=f32)


def dot_tn(a, b):
    return lax.dot_general(a, b, (((0,), (0,)), ((), ())), preferred_element_type=f32)


def in_vmem(x):
    return pltpu.with_memory_space_constraint(x, pltpu.VMEM)


def in_hbm(x):
    return pltpu.with_memory_space_constraint(x, pltpu.HBM)


def params(megabytes):
    return pltpu.CompilerParams(vmem_limit_bytes=megabytes << 20)


def cost(flops, moved):
    return pl.CostEstimate(flops=int(flops), bytes_accessed=int(moved), transcendentals=0)


def normalised(x):
    centred = x - jnp.mean(x, axis=-1, keepdims=True)
    rstd = lax.rsqrt(jnp.mean(centred * centred, axis=-1, keepdims=True) + EPS)
    return centred * rstd, rstd


def norm_back(d_normed, gain, xhat, rstd):
    d_hat = d_normed * gain
    along = jnp.mean(d_hat * xhat, axis=-1, keepdims=True)
    return rstd * (d_hat - jnp.mean(d_hat, axis=-1, keepdims=True) - xhat * along)


def fetch(source, target, sems, axis, parts):
    width = source.shape[axis] // parts
    copies = []
    for p in range(parts):
        cut = pl.ds(p * width, width)
        where = (cut, slice(None)) if axis == 0 else (slice(None), cut)
        copies.append(pltpu.make_async_copy(source.at[where], target.at[where], sems.at[p]))
    return copies


def frame_forward(
    core, frames_in, gain_in, w_up, w_down, mine, other, out, slope, up, down, frames, gain, sems, up_sems, down_sems
):
    first = [pltpu.make_async_copy(frames_in, frames, sems.at[0]), pltpu.make_async_copy(gain_in, gain, sems.at[1])]
    for one in first:
        one.start()
    ups = fetch(w_up, up, up_sems, 1, PARTS)
    downs = fetch(w_down, down, down_sems, 0, PARTS)
    for one, two in zip(ups, downs):
        one.start()
        two.start()
    for one in first:
        one.wait()
    x = frames[...].astype(f32)
    xhat, _ = normalised(x)
    normed = (xhat * gain[...][None, :]).astype(bf16)
    total = x
    width = HID // PARTS
    c0 = math.sqrt(2.0 / math.pi)
    for p in range(PARTS):
        cut = pl.ds(p * width, width)
        ups[p].wait()
        a = dot_nn(normed, up[:, cut])
        square = a * a
        th = jnp.tanh(c0 * a * (1.0 + 0.044715 * square))
        half = 0.5 * (1.0 + th)
        hidden = (a * half).astype(bf16)
        slope[:, cut] = (half + 0.5 * a * (1.0 - th * th) * c0 * (1.0 + 3 * 0.044715 * square)).astype(bf16)
        downs[p].wait()
        total = total + dot_nn(hidden, down[cut, :])
    stored = total.astype(bf16)
    out[...] = stored
    upper = core[0] == 1
    mine[...] = jnp.where(upper, stored[HALF:], stored[:HALF])
    other[...] = jnp.where(upper, stored[:HALF], stored[HALF:])


def run_frame_forward(core, frames, gain, w_up, w_down):
    rows = frames.shape[0]
    return pl.pallas_call(
        frame_forward,
        in_specs=[SMEM, HBM, HBM, HBM, HBM],
        out_specs=[VMEM] * 6,
        out_shape=[
            jax.ShapeDtypeStruct((HALF, D), bf16),
            jax.ShapeDtypeStruct((HALF, D), bf16),
            jax.ShapeDtypeStruct((rows, D), bf16),
            jax.ShapeDtypeStruct((rows, HID), bf16),
            pltpu.VMEM((D, HID), bf16),
            pltpu.VMEM((HID, D), bf16),
        ],
        scratch_shapes=[
            pltpu.VMEM((rows, D), bf16), pltpu.VMEM((D,), f32), pltpu.SemaphoreType.DMA((2,)),
            pltpu.SemaphoreType.DMA((PARTS,)), pltpu.SemaphoreType.DMA((PARTS,)),
        ],
        compiler_params=params(FRAME_MB),
        name="frame_forward",
    )(core, in_hbm(frames), in_hbm(gain), in_hbm(w_up), in_hbm(w_down))


def pieces(value):
    first = value.astype(bf16).astype(f32)
    rest = value - first
    second = rest.astype(bf16).astype(f32)
    return first, second, rest - second


def write_payload(out, mean, top, total):
    lane = lax.broadcasted_iota(jnp.int32, (HALF, 128), 1)
    stats = jnp.zeros((HALF, 128), f32)
    for at, piece in enumerate(pieces(top) + pieces(total)):
        stats = jnp.where(lane == at, piece, stats)
    out[:, :D] = mean.astype(bf16)
    out[:, D:] = stats.astype(bf16)


def read_stats(block):
    stats = block[:, D:].astype(f32)
    lane = lax.broadcasted_iota(jnp.int32, stats.shape, 1)
    top = jnp.sum(jnp.where(lane < 3, stats, 0.0), axis=-1, keepdims=True)
    total = jnp.sum(jnp.where((lane >= 3) & (lane < 6), stats, 0.0), axis=-1, keepdims=True)
    return top, total


def pool_pair(mine, theirs, query, out):
    a = mine[...].astype(f32)
    b = theirs[...].astype(f32)
    q = query[...][None, :]
    score_a = jnp.sum(a * q, axis=-1, keepdims=True) / ROOT
    score_b = jnp.sum(b * q, axis=-1, keepdims=True) / ROOT
    top = jnp.maximum(score_a, score_b)
    weight_a = jnp.exp(score_a - top)
    weight_b = jnp.exp(score_b - top)
    total = weight_a + weight_b
    write_payload(out, (weight_a * a + weight_b * b) / total, top, total)


def pool_all(p0, p1, p2, p3, *rest):
    spread, out = rest[-2:]
    parts = (p0, p1, p2, p3)
    stats = [read_stats(p) for p in parts]
    top = functools.reduce(jnp.maximum, [s[0] for s in stats])
    weights = [jnp.exp(s[0] - top) * s[1] for s in stats]
    total = sum(weights)
    mean = sum(w * p[:, :D].astype(f32) for w, p in zip(weights, parts)) / total
    write_payload(out, mean, top, total)
    rows = mean.astype(bf16)
    for o in range(OWNERS):
        spread[o] = rows


def prepare(
    core, lens, slots, requests, d_encoded, w_out, w_qkv, after,
    d_out, d_attended, own_column, other_column, own_row, other_row, qkv, d_wide, sem,
):
    load = pltpu.make_async_copy(w_qkv, qkv, sem)
    load.start()
    c = core[0]
    lane = lax.broadcasted_iota(jnp.int32, (LP, L), 1)
    diagonal = lane == lax.broadcasted_iota(jnp.int32, (LP, L), 0)
    inside = lax.broadcasted_iota(jnp.int32, (LP, 1), 0) < L
    owner_lane = lax.broadcasted_iota(jnp.int32, (LP, OWNERS), 1)
    cap_lane = lax.broadcasted_iota(jnp.int32, (LP, CAP), 1)
    asked = requests[0].astype(f32).astype(bf16)
    for u in range(USERS):
        slot = jnp.sum(jnp.where(diagonal, slots[u : u + 1, :].astype(f32), 0.0), axis=1, keepdims=True)
        slot = slot.astype(jnp.int32)
        owner = slot >> 6
        lists = dot_nn((owner_lane == owner).astype(bf16), asked)
        local = jnp.sum(jnp.where(cap_lane == (slot & (CAP - 1)), lists, 0.0), axis=1, keepdims=True)
        local = local.astype(jnp.int32)
        position = jnp.where(inside, owner * HALF + (local & (HALF - 1)), -1)
        own = (local >> 6) == c
        here = pl.ds(u * LP, LP)
        own_column[here, :] = jnp.where(own, position, -1)
        other_column[here, :] = jnp.where(own, -1, position)
    square = (128, 128)
    same = lax.broadcasted_iota(jnp.int32, square, 0) == lax.broadcasted_iota(jnp.int32, square, 1)
    for part in range(USERS * LP // 128):
        here = pl.ds(part * 128, 128)
        for column, row in ((own_column, own_row), (other_column, other_row)):
            value = jnp.where(same, column[here, :].astype(f32), 0.0)
            row[:, here] = jnp.sum(value, axis=0, keepdims=True).astype(jnp.int32)

    for j in range(D // 128):
        d_wide[j] = d_encoded[:, j * 128 : (j + 1) * 128].astype(f32)
    place = lax.broadcasted_iota(jnp.int32, (LP, 1), 0)
    for first in range(0, USERS, 2):
        pair = []
        for u in (first, first + 1):
            rows = pl.ds(u, L, stride=USERS)
            one = jnp.concatenate([d_wide[j, rows, :] for j in range(D // 128)], axis=1)
            one = jnp.concatenate([one, jnp.zeros((LP - L, D), f32)], axis=0)
            pair.append(jnp.where(place < lens[u], one, 0.0))
        d_out[pl.ds(first * LP, 2 * LP), :] = jnp.concatenate(pair, axis=0).astype(bf16)
    for part in range(USERS // SUB):
        here = pl.ds(part * SUB_ROWS, SUB_ROWS)
        d_attended[here, :] = dot_nt(d_out[here, :], w_out[...]).astype(bf16)
    load.wait()


def run_prepare(core, lens, slots, requests, d_encoded, w_out, w_qkv, after):
    count = USERS * LP
    whole = lambda r, w, t: jax.ShapeDtypeStruct((r, w), t)
    return pl.pallas_call(
        prepare,
        in_specs=[SMEM, SMEM] + [VMEM] * 4 + [HBM, ANY],
        out_specs=[VMEM] * 7,
        out_shape=[
            pltpu.VMEM((count, D), bf16), pltpu.VMEM((count, D), bf16), whole(count, 1, jnp.int32), whole(count, 1, jnp.int32),
            whole(1, count, jnp.int32), whole(1, count, jnp.int32), pltpu.VMEM((D, 3 * D), bf16),
        ],
        scratch_shapes=[pltpu.VMEM((D // 128, USERS * L, 128), f32), pltpu.SemaphoreType.DMA],
        compiler_params=params(16),
        cost_estimate=cost(2 * count * D * D, 8 * count * D),
        name="prepare",
    )(core, lens, slots, requests, d_encoded, w_out, in_hbm(w_qkv), after)


def gather_own(index, table, out):
    at = lax.broadcasted_iota(jnp.int32, (ROWS, OWNERS * HALF), 1)
    out[...] = dot_nn((at == index[...]).astype(bf16), table[...]).astype(bf16)


def run_gather_own(index, table):
    part = lambda w: pl.BlockSpec((ROWS, w), lambda j: (j, 0))
    count = USERS * LP
    return pl.pallas_call(
        gather_own,
        grid=(USERS // GROUP,),
        in_specs=[part(1), VMEM],
        out_specs=part(D),
        out_shape=jax.ShapeDtypeStruct((count, D), bf16),
        compiler_params=params(12),
        cost_estimate=cost(2 * count * OWNERS * HALF * D, 6 * count * D),
        name="gather_own",
    )(index, table)


def encoder(lens, index, own_rows, table, pos, gain, w_qkv, w_out, d_out, d_attended, encoded, d_inputs):
    step = pl.program_id(0)
    at = lax.broadcasted_iota(jnp.int32, (ROWS, OWNERS * HALF), 1)
    x = dot_nn((at == index[...]).astype(bf16), table[...])
    x = x + own_rows[...].astype(f32)
    places = jnp.concatenate([pos[...].astype(f32), jnp.zeros((LP - L, D), f32)], axis=0)
    x = (x.reshape(GROUP, LP, D) + places[None]).reshape(ROWS, D)
    xhat, rstd = normalised(x)
    g = gain[...][None, :]
    packed = dot_nn((xhat * g).astype(bf16), w_qkv[...]).astype(bf16)

    subs = range(GROUP // SUB)
    cut = lambda value, sub: value[sub * SUB_ROWS : (sub + 1) * SUB_ROWS]
    join = lambda values: jnp.concatenate(values, axis=0)
    d_att = d_attended[...]
    q = [cut(packed[:, :D], sub) for sub in subs]
    k = [cut(packed[:, D : 2 * D], sub) for sub in subs]
    v = [cut(packed[:, 2 * D :], sub) for sub in subs]
    place = lax.broadcasted_iota(jnp.int32, (SUB_ROWS, 1), 0)
    column = lax.broadcasted_iota(jnp.int32, (SUB_ROWS, SUB_ROWS), 1)
    raw = [dot_nt(q[sub], k[sub]) for sub in subs]
    d_raw = [dot_nt(cut(d_att, sub), v[sub]) for sub in subs]
    live, probs16, d_scores = [], [], []
    for sub in subs:
        length = jnp.full((SUB_ROWS, 1), 0, jnp.int32)
        first = jnp.full((SUB_ROWS, 1), 0, jnp.int32)
        for u in range(SUB):
            here = (place >= u * LP) & (place < (u + 1) * LP)
            length = jnp.where(here, lens[step * GROUP + sub * SUB + u], length)
            first = jnp.where(here, u * LP, first)
        allowed = (column >= first) & (column <= place) & (column < first + length)
        live.append((place - first) < length)
        scores = jnp.where(allowed, raw[sub] / ROOT, MASKED)
        raised = jnp.exp(scores - jnp.max(scores, axis=-1, keepdims=True))
        probs = raised / jnp.sum(raised, axis=-1, keepdims=True)
        probs16.append(probs.astype(bf16))
        d_probs = d_raw[sub].astype(bf16).astype(f32)
        d_scores.append(
            (probs * (d_probs - jnp.sum(d_probs * probs, axis=-1, keepdims=True)) / ROOT).astype(bf16)
        )
    attended = join([dot_nn(probs16[sub], v[sub]).astype(bf16) for sub in subs])
    d_q = join([dot_nn(d_scores[sub], k[sub]).astype(bf16) for sub in subs])
    d_k = join([dot_tn(d_scores[sub], q[sub]).astype(bf16) for sub in subs])
    d_v = join([dot_tn(probs16[sub], cut(d_att, sub)).astype(bf16) for sub in subs])
    encoded[...] = jnp.where(join(live), x + dot_nn(attended, w_out[...]), 0.0).astype(bf16)
    d_normed = dot_nt(jnp.concatenate([d_q, d_k, d_v], axis=1), w_qkv[...]).astype(bf16).astype(f32)
    d_inputs[...] = (d_out[...].astype(f32) + norm_back(d_normed, g, xhat, rstd)).astype(bf16)


def run_encoder(lens, index, own_rows, table, pos, gain, w_qkv, w_out, d_out, d_attended):
    part = lambda w: pl.BlockSpec((ROWS, w), lambda j: (j, 0))
    count = USERS * LP
    return pl.pallas_call(
        encoder,
        grid=(USERS // GROUP,),
        in_specs=[
            SMEM, part(1), part(D), VMEM, VMEM, VMEM, VMEM, VMEM, part(D), part(D),
        ],
        out_specs=[part(D), part(D)],
        out_shape=[jax.ShapeDtypeStruct((count, D), bf16)] * 2,
        compiler_params=params(ENC_MB),
        name="user_encoder",
    )(lens, index, own_rows, table, pos, gain, in_vmem(w_qkv), w_out, in_vmem(d_out), in_vmem(d_attended))


def reorder(by_user, after, by_place, wide):
    for first in range(0, USERS, 2):
        pair = by_user[pl.ds(first * LP, 2 * LP), :].astype(f32)
        for k in range(2):
            for j in range(D // 128):
                one = pair[k * LP : k * LP + L, j * 128 : (j + 1) * 128]
                wide[j, pl.ds(first + k, L, stride=USERS), :] = one
    for j in range(D // 128):
        by_place[:, j * 128 : (j + 1) * 128] = wide[j].astype(bf16)


def run_reorder(by_user, after):
    return pl.pallas_call(
        reorder,
        in_specs=[VMEM, ANY],
        out_specs=VMEM,
        out_shape=jax.ShapeDtypeStruct((USERS * L, D), bf16),
        scratch_shapes=[pltpu.VMEM((D // 128, USERS * L, 128), f32)],
        compiler_params=params(12),
        cost_estimate=cost(USERS * L * D, 6 * USERS * L * D),
        name="reorder",
    )(by_user, after)


def add_owners(parts, out):
    total = parts[0].astype(f32)
    for o in range(1, OWNERS):
        total = total + parts[o].astype(f32)
    out[...] = total.astype(bf16)


def add_parts(a, b, c, d, after, out):
    out[...] = sum(part[...].astype(f32) for part in (a, b, c, d)).astype(bf16)


def scatter(index, rows, out):
    block = out.shape[0]
    row = lax.broadcasted_iota(jnp.int32, (block, USERS * LP), 0) + pl.program_id(0) * block
    out[...] = dot_nn((row == index[...]).astype(bf16), rows[...]).astype(bf16)


def scatter_more(index, rows, so_far, out):
    block = out.shape[0]
    row = lax.broadcasted_iota(jnp.int32, (block, USERS * LP), 0) + pl.program_id(0) * block
    total = dot_nn((row == index[...]).astype(bf16), rows[...])
    out[...] = (total + so_far[...].astype(f32)).astype(bf16)


def run_scatter(body, *operands):
    count = USERS * LP
    steps = 2
    part = pl.BlockSpec((OWNERS * HALF // steps, D), lambda j: (j, 0))
    return pl.pallas_call(
        body,
        grid=(steps,),
        in_specs=[VMEM, VMEM, part][: len(operands)],
        out_specs=part,
        out_shape=jax.ShapeDtypeStruct((OWNERS * HALF, D), bf16),
        compiler_params=params(12),
        cost_estimate=cost(2 * count * OWNERS * HALF * D, 6 * count * D),
        name=body.__name__,
    )(*operands)


def turn(up, down, after, up_t, down_t):
    for p in range(PARTS):
        cut = pl.ds(p * (HID // PARTS), HID // PARTS)
        up_t[cut, :] = up[:, cut].T
        down_t[:, cut] = down[cut, :].T


def run_turn(up, down, after):
    return pl.pallas_call(
        turn,
        in_specs=[VMEM, VMEM, ANY],
        out_specs=[VMEM] * 2,
        out_shape=[pltpu.VMEM((HID, D), bf16), pltpu.VMEM((D, HID), bf16)],
        compiler_params=params(8),
        cost_estimate=cost(HID * D, 8 * HID * D),
        name="turn",
    )(in_vmem(up), in_vmem(down), after)


def frame_backward(
    core, d_mine, d_other, pay_mine, pay_other, query, frames, framed, gain, slope, up, down,
    out,
):
    upper = core[0] == 1
    order = lambda a, b: jnp.concatenate([jnp.where(upper, b, a), jnp.where(upper, a, b)], axis=0)
    dp = order(d_mine[...], d_other[...]).astype(f32)
    pay = order(pay_mine[...], pay_other[...]).astype(f32)
    x = framed[...].astype(f32)
    q = query[...][None, :]
    top, whole = read_stats(pay)
    weight = jnp.exp(jnp.sum(x * q, axis=-1, keepdims=True) / ROOT - top) / whole
    cross = jnp.sum(dp * x, axis=-1, keepdims=True)
    own = jnp.sum(dp * pay[:, :D], axis=-1, keepdims=True)
    grad = weight * (dp + ((cross - own) / ROOT) * q)
    grad16 = grad.astype(bf16)
    width = HID // PARTS
    total = jnp.zeros(grad.shape, f32)
    for p in range(PARTS):
        cut = pl.ds(p * width, width)
        d_hidden = dot_nn(grad16, down[:, cut]).astype(bf16).astype(f32)
        d_a = (d_hidden * slope[:, cut].astype(f32)).astype(bf16)
        total = total + dot_nn(d_a, up[cut, :])
    xhat, rstd = normalised(frames[...].astype(f32))
    d_normed = total.astype(bf16).astype(f32)
    out[...] = (grad + norm_back(d_normed, gain[...][None, :], xhat, rstd)).astype(bf16)


def run_frame_backward(core, d_mine, d_other, pay_mine, pay_other, query, frames, framed, gain, slope, w_up, w_down):
    rows = frames.shape[0]
    return pl.pallas_call(
        frame_backward,
        in_specs=[SMEM] + [VMEM] * 11,
        out_specs=VMEM,
        out_shape=jax.ShapeDtypeStruct((rows, D), bf16),
        compiler_params=params(FRAME_MB),
        name="frame_backward",
    )(core, d_mine, d_other, pay_mine, pay_other, query, frames, framed, gain, slope, in_vmem(w_up), in_vmem(w_down))


def swap_with(x, bits):
    pairs = [(i, i ^ bits) for i in range(8)]
    return lax.ppermute(x, "frame", pairs)


def spread_along_x(x):
    return [swap_with(x, 2 * k) for k in (1, 2, 3)]


def shards(
    frames, frame_gain, w_up, w_down, pool_query, pos_embed, user_gain, w_qkv, w_out,
    request_rows, hist_slot, hist_len, d_encoded,
):
    rows = frames.shape[0]
    c = lax.axis_index("frame") % 2
    core = c.astype(jnp.int32).reshape(1)
    flat_frames = frames.reshape(rows, D)
    gain = frame_gain
    query = pool_query

    mine, other, framed, slope, up, down = run_frame_forward(core, flat_frames, gain, w_up, w_down)
    theirs = swap_with(other, 1)
    payload = jax.ShapeDtypeStruct((HALF, PAY), bf16)
    pair = pl.pallas_call(
        pool_pair, in_specs=[VMEM] * 3, out_specs=VMEM, out_shape=payload, compiler_params=params(8), name="pool_pair",
    )(mine, theirs, query)
    cotangent = jnp.transpose(d_encoded, (1, 0, 2)).reshape(USERS * L, D)
    d_out, d_attended, own_column, other_column, own_row, other_row, qkv = run_prepare(
        core, hist_len, hist_slot, request_rows, cotangent, w_out, w_qkv, pair
    )
    up_turned, down_turned = run_turn(up, down, pair)
    early = (in_vmem(d_out), in_vmem(up_turned))
    spread, pay_mine = pl.pallas_call(
        pool_all, in_specs=[VMEM] * 4 + [pl.BlockSpec(memory_space=pl.ANY)] * len(early), out_specs=[VMEM] * 2,
        out_shape=[jax.ShapeDtypeStruct((OWNERS, HALF, D), bf16), payload], compiler_params=params(8), name="pool_all",
    )(pair, *spread_along_x(pair), *early)
    table = lax.all_to_all(spread, "dp", split_axis=0, concat_axis=0, tiled=True).reshape(OWNERS * HALF, D)
    other_table = swap_with(table, 1)
    own_rows = run_gather_own(own_column, table)
    encoded, d_inputs = run_encoder(
        hist_len, other_column, own_rows, other_table, pos_embed, user_gain, qkv, w_out, d_out, d_attended
    )
    peer_rows = swap_with(d_inputs, 1)
    peer_index = swap_with(other_row, 1)
    pay_other = swap_with(pay_mine, 1)
    d_table = run_scatter(scatter, own_row, d_inputs)
    d_table = run_scatter(scatter_more, peer_index, peer_rows, d_table)
    returned = lax.all_to_all(
        d_table.reshape(OWNERS, HALF, D), "dp", split_axis=0, concat_axis=0, tiled=True
    )
    partial = pl.pallas_call(
        add_owners, in_specs=[VMEM], out_specs=VMEM, out_shape=jax.ShapeDtypeStruct((HALF, D), bf16),
        compiler_params=params(8), name="add_owners",
    )(returned)
    encoded = run_reorder(encoded, partial)
    d_mine = pl.pallas_call(
        add_parts, in_specs=[VMEM] * 4 + [ANY], out_specs=VMEM, out_shape=jax.ShapeDtypeStruct((HALF, D), bf16),
        compiler_params=params(8), name="add_parts",
    )(partial, *spread_along_x(partial), in_hbm(encoded))
    d_other = swap_with(d_mine, 1)
    d_frames = run_frame_backward(
        core, d_mine, d_other, pay_mine, pay_other, query, flat_frames, framed, gain, slope, up_turned, down_turned
    )
    encoded = jnp.transpose(encoded.reshape(L, USERS, D), (1, 0, 2))
    return encoded, d_frames.reshape(rows, 1, D)


def solution(mesh):
    in_specs = (
        P("dp", "frame", None),
        P(),
        P(),
        P(),
        P(),
        P(),
        P(),
        P(),
        P(),
        P(("dp", "frame"), None, None),
        P(("dp", "frame"), None),
        P(("dp", "frame")),
        P(("dp", "frame"), None, None),
    )
    out_specs = (P(("dp", "frame"), None, None), P("dp", "frame", None))
    return jax.shard_map(shards, mesh=mesh, in_specs=in_specs, out_specs=out_specs, check_vma=False)
```

time: 154 us -> 117 us (0.76)
  local copies, waits for them, and re-layouts: 17.2 us -> 0.04 us
  waiting for transfers between devices: 13.3 us -> 5.5 us
  Pallas kernels: 46.8 us -> 40.5 us
  other arithmetic: 3.71 us -> 0 us
    unnamed x40 -> x20, local copies, waits for them, and re-layouts: 14 us -> 0.04 us
    pallas_call x1, Pallas kernels: 29.3 us -> 16.5 us  [run_encoder(): pl.pallas_call(encoder, grid=(USERS // GROUP,), in_specs=[SMEM, part(1),...]
    pallas_call x4 -> x11, Pallas kernels: 15.7 us -> 23.9 us  [the longest x1 6.3 us: run_frame_forward(): pl.pallas_call(frame_forward, in_specs=[SMEM, HBM, HBM, HBM, HBM], out_sp...]
    ppermute x12, waiting for transfers between devices: 13.3 us -> 5.5 us  [swap_with(): return lax.ppermute(x, 'frame', pairs)]
    select_n x4 -> x0, other arithmetic: 2.75 us -> none  [the longest x2 1.58 us: shards(): other_index = jnp.where(local // HALF == c, -1, position)]
    reshape x5 -> x0, local copies, waits for them, and re-layouts: 2.13 us -> none  [the longest x1 0.69 us: shards(): gain = frame_gain.reshape(1, D)]
    pallas_call x1, Pallas kernels: 1.76 us -> 0.17 us  [shards(): pl.pallas_call(pool_pair, in_specs=[VMEM] * 3, out_specs=VMEM, out_shape=...]
  transfers between devices with their start and end apart: 12 -> 12, of which waited for: 8 -> 5; matrix products, arithmetic and copies ran while one was open for 3% -> 0% of each run, Pallas kernels for 0% -> 11%
where the time goes in v2:
time: 117 us
  blocking collectives  53.9 us (46%)
  Pallas kernels  40.5 us (35%)
  starting transfers between devices  15.7 us (13%)
  waiting for transfers between devices  5.5 us (5%)
    all_to_all x1, blocking collectives, shards(): lax.all_to_all(spread, 'dp', split_axis=0, concat_axis=0, tiled=True)  29.3 us
    all_to_all x1, blocking collectives, shards(): lax.all_to_all(d_table.reshape(OWNERS, HALF, D), 'dp', split_axis=0, conc...  24.6 us
    pallas_call x1, Pallas kernels, run_encoder(): pl.pallas_call(encoder, grid=(USERS // GROUP,), in_specs=[SMEM, part(1),...  16.5 us
    ppermute x12, starting transfers between devices, swap_with(): return lax.ppermute(x, 'frame', pairs)  15.7 us
    pallas_call x1, Pallas kernels, run_frame_forward(): pl.pallas_call(frame_forward, in_specs=[SMEM, HBM, HBM, HBM, HBM], out_sp...  6.3 us
    ppermute x12, waiting for transfers between devices, swap_with(): return lax.ppermute(x, 'frame', pairs)  5.5 us
    pallas_call x2, Pallas kernels, run_scatter(): pl.pallas_call(body, grid=(steps,), in_specs=[VMEM, VMEM, part][:len(oper...  4 us
    pallas_call x1, Pallas kernels, run_prepare(): pl.pallas_call(prepare, in_specs=[SMEM, SMEM] + [VMEM] * 4 + [HBM, ANY],...  3.1 us
  transfers between devices with their start and end apart: 12, of which 5 were waited for; matrix products, arithmetic and copies ran while one was open for 0% of the time, Pallas kernels for 11%

profile of v2, /device:TPU:1, one launch (start us, length us, event | category | flops | bytes accessed | tf_op | source)
XLA Modules:
  0.0 116.6 jit_solution(7770634841481718215)
XLA Ops:
  0.6 0.0 copy-start.5
  0.7 6.3 %frame_forward.1 = (bf16[64,768]{1,0:T(8,128)(2,1)S(1)}, bf16[64,768]{1,0:T(8,128)(2,1)S(1)}, bf16[128,768]{1,0:T(8,128)(2,1)S(1)}, bf16[128,3072]{1,0:T(8,128)(...) custom-call(s32[1]{0:T(128)} %bitcast.core, bf16[128,768]{1,0:T(8,128)(2,1)} %bitcast.15, ...), custom_call_target="tpu_custom_call" | custom-call | tf_op jit(solution)/shard_map/frame_forward/pallas_call | solution.py:128
  7.0 1.5 %collective-permute-start = (bf16[64,768]{1,0:T(8,128)(2,1)S(1)}, bf16[64,768]{1,0:T(8,128)(2,1)S(1)}, u32[]{:S(2)}, u32[]{:S(2)}) collective-permute-start(bf16[64,768]{1,0:T(8,128)(2,1)S(1)} %get-tuple-element.22), channel_id=1, source_target_pairs={{0,1},{1,0},{2,3},{3,2},{4,5},{5,4},{6,7},{7,6},{8,9},{9,8},{10,11... | collective-permute-start | bytes 294920 | tf_op jit(solution)/shard_map/ppermute | solution.py:478
  8.5 0.9 collective-permute-done.theirs
  9.4 0.0 copy-done.5
  9.4 0.2 pool_pair.1.after.p0
  9.6 1.4 %collective-permute-start.1 = (bf16[64,896]{1,0:T(8,128)(2,1)S(1)}, bf16[64,896]{1,0:T(8,128)(2,1)S(1)}, u32[]{:S(2)}, u32[]{:S(2)}) collective-permute-start(bf16[64,896]{1,0:T(8,128)(2,1)S(1)} %pool_pair.1.after.p0), channel_id=1, source_target_pairs={{0,2},{1,3},{2,0},{3,1},{4,6},{5,7},{6,4},{7,5},{8,10},{9,11},{10,... | collective-permute-start | bytes 344072 | tf_op jit(solution)/shard_map/ppermute | solution.py:478
  11.0 2.4 %collective-permute-start.2 = (bf16[64,896]{1,0:T(8,128)(2,1)S(1)}, bf16[64,896]{1,0:T(8,128)(2,1)S(1)}, u32[]{:S(2)}, u32[]{:S(2)}) collective-permute-start(bf16[64,896]{1,0:T(8,128)(2,1)S(1)} %pool_pair.1.after.p0), channel_id=1, source_target_pairs={{0,4},{1,5},{2,6},{3,7},{4,0},{5,1},{6,2},{7,3},{8,12},{9,13},{10,... | collective-permute-start | bytes 344072 | tf_op jit(solution)/shard_map/ppermute | solution.py:478
  13.4 0.1 collective-permute-start.3
  13.5 0.0 copy-start
  13.5 0.0 copy-start.1
  13.5 0.0 copy-start.6
  13.5 0.0 copy-start.7
  13.5 0.0 copy-start.9
  13.6 2.6 %turn.1 = (bf16[3072,768]{1,0:T(8,128)(2,1)S(1)}, bf16[768,3072]{1,0:T(8,128)(2,1)S(1)}) custom-call(bf16[768,3072]{1,0:T(8,128)(2,1)S(1)} %get-tuple-element.26.up, bf16[3072,768]{1,0:T(8,128)(2,1)S(1)} %get-tuple-element.27.down, bf16[64,896]{1,0:T(8,128)(2,1)S(1)} %pool_pair.1.after.p0), custom_call_target="tpu_custom_call" | custom-call | flops 2359296 | bytes 18874368 | tf_op jit(solution)/shard_map/turn/pallas_call | solution.py:425
  16.1 0.0 copy-done
  16.2 0.0 copy-done.1
  16.2 0.0 copy-done.6
  16.2 0.0 copy-done.7
  16.2 0.0 copy-done.9
  16.2 3.1 %prepare.1 = (bf16[896,768]{1,0:T(8,128)(2,1)S(1)}, bf16[896,768]{1,0:T(8,128)(2,1)S(1)}, s32[896,1]{1,0:T(8,128)S(1)}, s32[896,1]{1,0:T(8,128)S(1)}, s32[1,896]...) custom-call(s32[1]{0:T(128)} %bitcast.core, s32[16]{0:T(128)S(1)} %copy-done.9, ...), custom_call_target="tpu_custom_call" | custom-call | flops 1056964608 | bytes 5505024 | tf_op jit(solution)/shard_map/prepare/pallas_call | solution.py:253
  19.3 0.0 collective-permute-done.1.p1
  19.3 0.0 collective-permute-done.2.p2
  19.3 2.0 %collective-permute-done.3.p3 = bf16[64,896]{1,0:T(8,128)(2,1)S(1)} collective-permute-done((bf16[64,896]{1,0:T(8,128)(2,1)S(1)}, bf16[64,896]{1,0:T(8,128)(2,1)S(1)}, u32[]{:S(2)}, u32[]{:S(2)}) %collective-permute-start.3) | collective-permute-done | bytes 114720 | tf_op jit(solution)/shard_map/ppermute | solution.py:478
  21.3 0.3 pool_all.1
  21.6 29.3 %all_to_all.10 = bf16[16,64,768]{2,1,0:T(8,128)(2,1)S(1)} all-to-all(bf16[16,64,768]{2,1,0:T(8,128)(2,1)S(1)} %get-tuple-element.29), channel_id=1, replica_groups=mesh['dp'=16,'frame'=8] {'dp'}, dimensions={0} | all-to-all | bytes 3145728 | tf_op jit(solution)/shard_map/all_to_all | solution.py:512
  51.0 2.0 %collective-permute-start.4 = (bf16[1024,768]{1,0:T(8,128)(2,1)S(1)}, bf16[1024,768]{1,0:T(8,128)(2,1)S(1)}, u32[]{:S(2)}, u32[]{:S(2)}) collective-permute-start(bf16[1024,768]{1,0:T(8,128)(2,1)S(1)} %bitcast.11), channel_id=1, source_target_pairs={{0,1},{1,0},{2,3},{3,2},{4,5},{5,4},{6,7},{7,6},{8,9},{9,8},{10,11... | collective-permute-start | bytes 4718600 | tf_op jit(solution)/shard_map/ppermute | solution.py:478
  52.9 0.0 copy-start.3
  52.9 0.0 copy-start.8
  52.9 2.0 %gather_own.1.own_rows = bf16[896,768]{1,0:T(8,128)(2,1)S(1)} custom-call(s32[896,1]{1,0:T(8,128)S(1)} %get-tuple-element.24.index, bf16[1024,768]{1,0:T(8,128)(2,1)S(1)} %bitcast.12), custom_call_target="tpu_custom_call" | custom-call | flops 1409286144 | bytes 4128768 | tf_op jit(solution)/shard_map/gather_own/pallas_call | solution.py:276
  55.0 1.0 collective-permute-done.4.table
  56.0 0.0 copy-done.3
  56.0 0.0 copy-done.8
  56.0 16.5 %user_encoder.1 = (bf16[896,768]{1,0:T(8,128)(2,1)S(1)}, bf16[896,768]{1,0:T(8,128)(2,1)S(1)}) custom-call(s32[16]{0:T(128)S(1)} %copy-done.9, s32[896,1]{1,0:T(8,128)S(1)} %get-tuple-element.23.index, bf16[896,768]{1,0:T(8,128)(2,1)S(1)} %gather_own.1.own_rows, bf16[1024,768]{1,0:T(8,128)(2,1)S(1)} %collective-permute-done.4.table, ...), custom_call_target="tpu_custom_call" | custom-call | tf_op jit(solution)/shard_map/user_encoder/pallas_call | solution.py:340
  72.5 0.5 collective-permute-start.6
  72.9 0.1 collective-permute-start.5
  73.1 2.0 %scatter.1.so_far = bf16[1024,768]{1,0:T(8,128)(2,1)S(1)} custom-call(s32[1,896]{1,0:T(1,128)S(1)} %get-tuple-element.35.index, bf16[896,768]{1,0:T(8,128)(2,1)S(1)} %get-tuple-element.34.rows), custom_call_target="tpu_custom_call" | custom-call | flops 1409286144 | bytes 4128768 | tf_op jit(solution)/shard_map/scatter/pallas_call | solution.py:405
  75.1 0.6 collective-permute-done.5.index
  75.7 0.0 collective-permute-done.6.rows
  75.7 2.0 %scatter_more.1 = bf16[1024,768]{1,0:T(8,128)(2,1)S(1)} custom-call(s32[1,896]{1,0:T(1,128)S(1)} %collective-permute-done.5.index, bf16[896,768]{1,0:T(8,128)(2,1)S(1)} %collective-permute-done.6.rows, bf16[1024,768]{1,0:T(8,128)(2,1)S(1)} %scatter.1.so_far), custom_call_target="tpu_custom_call" | custom-call | flops 1409286144 | bytes 4128768 | tf_op jit(solution)/shard_map/scatter_more/pallas_call | solution.py:405
  77.7 24.6 %all_to_all.11.parts = bf16[16,64,768]{2,1,0:T(8,128)(2,1)S(1)} all-to-all(bf16[16,64,768]{2,1,0:T(8,128)(2,1)S(1)} %bitcast.13), channel_id=1, replica_groups=mesh['dp'=16,'frame'=8] {'dp'}, dimensions={0} | all-to-all | bytes 3145728 | tf_op jit(solution)/shard_map/all_to_all | solution.py:523
  102.3 0.2 add_owners.1.after.a
  102.5 0.1 collective-permute-start.7
  102.6 1.9 %collective-permute-start.8 = (bf16[64,768]{1,0:T(8,128)(2,1)S(1)}, bf16[64,768]{1,0:T(8,128)(2,1)S(1)}, u32[]{:S(2)}, u32[]{:S(2)}) collective-permute-start(bf16[64,768]{1,0:T(8,128)(2,1)S(1)} %add_owners.1.after.a), channel_id=1, source_target_pairs={{0,4},{1,5},{2,6},{3,7},{4,0},{5,1},{6,2},{7,3},{8,12},{9,13},{10,... | collective-permute-start | bytes 294920 | tf_op jit(solution)/shard_map/ppermute | solution.py:478
  104.5 1.9 %collective-permute-start.9 = (bf16[64,768]{1,0:T(8,128)(2,1)S(1)}, bf16[64,768]{1,0:T(8,128)(2,1)S(1)}, u32[]{:S(2)}, u32[]{:S(2)}) collective-permute-start(bf16[64,768]{1,0:T(8,128)(2,1)S(1)} %add_owners.1.after.a), channel_id=1, source_target_pairs={{0,6},{1,7},{2,4},{3,5},{4,2},{5,3},{6,0},{7,1},{8,14},{9,15},{10,... | collective-permute-start | bytes 294920 | tf_op jit(solution)/shard_map/ppermute | solution.py:478
  106.5 2.6 %collective-permute-start.11 = (bf16[64,896]{1,0:T(8,128)(2,1)S(1)}, bf16[64,896]{1,0:T(8,128)(2,1)S(1)}, u32[]{:S(2)}, u32[]{:S(2)}) collective-permute-start(bf16[64,896]{1,0:T(8,128)(2,1)S(1)} %get-tuple-element.36.pay_mine), channel_id=1, source_target_pairs={{0,1},{1,0},{2,3},{3,2},{4,5},{5,4},{6,7},{7,6},{8,9},{9,8},{10,11... | collective-permute-start | bytes 344072 | tf_op jit(solution)/shard_map/ppermute | solution.py:478
  109.1 0.0 copy-start.2
  109.1 0.0 copy-start.4
  109.1 2.5 %reorder.1.after = bf16[800,768]{1,0:T(8,128)(2,1)} custom-call(bf16[896,768]{1,0:T(8,128)(2,1)S(1)} %get-tuple-element.32.by_user, bf16[64,768]{1,0:T(8,128)(2,1)S(1)} %add_owners.1.after.a), custom_call_target="tpu_custom_call" | custom-call | flops 614400 | bytes 3686400 | tf_op jit(solution)/shard_map/reorder/pallas_call | solution.py:365
  111.6 0.0 collective-permute-done.7.b
  111.6 0.0 collective-permute-done.8.c
  111.6 0.0 collective-permute-done.9.d
  111.6 0.1 add_parts.1.d_mine
  111.6 1.2 %collective-permute-start.10 = (bf16[64,768]{1,0:T(8,128)(2,1)S(1)}, bf16[64,768]{1,0:T(8,128)(2,1)S(1)}, u32[]{:S(2)}, u32[]{:S(2)}) collective-permute-start(bf16[64,768]{1,0:T(8,128)(2,1)S(1)} %add_parts.1.d_mine), channel_id=1, source_target_pairs={{0,1},{1,0},{2,3},{3,2},{4,5},{5,4},{6,7},{7,6},{8,9},{9,8},{10,11... | collective-permute-start | bytes 294920 | tf_op jit(solution)/shard_map/ppermute | solution.py:478
  112.8 0.0 collective-permute-done.11.pay_other
  112.8 0.9 collective-permute-done.10.d_other
  113.8 0.0 copy-done.2
  113.8 0.0 copy-done.4
  113.8 2.8 %frame_backward.1 = bf16[128,768]{1,0:T(8,128)(2,1)} custom-call(s32[1]{0:T(128)} %bitcast.core, bf16[64,768]{1,0:T(8,128)(2,1)S(1)} %add_parts.1.d_mine, bf16[64,768]{1,0:T(8,128)(2,1)S(1)} %collective-permute-done.10.d_other, bf16[64,896]{1,0:T(8,128)(2,1)S(1)} %get-tuple-element.36.pay_mine, bf16[64,896]{1,0:T(8,128)(2,1)S(1)} %collective-permute-done.11.pay_other, ...), custom_call_target="tpu_custom_call" | custom-call | tf_op jit(solution)/shard_map/frame_backward/pallas_call | solution.py:466
Async XLA Ops:
  0.6 8.8 %copy-start.5 = (f32[768]{0:T(1024)S(1)}, f32[768]{0:T(1024)}, u32[]{:S(2)}) copy-start(f32[768]{0:T(1024)} %query.3) | copy-start | bytes 9220
  7.0 2.4 %collective-permute-start = (bf16[64,768]{1,0:T(8,128)(2,1)S(1)}, bf16[64,768]{1,0:T(8,128)(2,1)S(1)}, u32[]{:S(2)}, u32[]{:S(2)}) collective-permute-start(bf16[64,768]{1,0:T(8,128)(2,1)S(1)} %get-tuple-element.22), channel_id=1, source_target_pairs={{0,1},{1,0},{2,3},{3,2},{4,5},{5,4},{6,7},{7,6},{8,9},{9,8},{10,11... | collective-permute-start | bytes 294920 | tf_op jit(solution)/shard_map/ppermute | solution.py:478
  9.6 9.7 %collective-permute-start.1 = (bf16[64,896]{1,0:T(8,128)(2,1)S(1)}, bf16[64,896]{1,0:T(8,128)(2,1)S(1)}, u32[]{:S(2)}, u32[]{:S(2)}) collective-permute-start(bf16[64,896]{1,0:T(8,128)(2,1)S(1)} %pool_pair.1.after.p0), channel_id=1, source_target_pairs={{0,2},{1,3},{2,0},{3,1},{4,6},{5,7},{6,4},{7,5},{8,10},{9,11},{10,... | collective-permute-start | bytes 344072 | tf_op jit(solution)/shard_map/ppermute | solution.py:478
  11.0 8.3 %collective-permute-start.2 = (bf16[64,896]{1,0:T(8,128)(2,1)S(1)}, bf16[64,896]{1,0:T(8,128)(2,1)S(1)}, u32[]{:S(2)}, u32[]{:S(2)}) collective-permute-start(bf16[64,896]{1,0:T(8,128)(2,1)S(1)} %pool_pair.1.after.p0), channel_id=1, source_target_pairs={{0,4},{1,5},{2,6},{3,7},{4,0},{5,1},{6,2},{7,3},{8,12},{9,13},{10,... | collective-permute-start | bytes 344072 | tf_op jit(solution)/shard_map/ppermute | solution.py:478
  13.4 7.9 %collective-permute-start.3 = (bf16[64,896]{1,0:T(8,128)(2,1)S(1)}, bf16[64,896]{1,0:T(8,128)(2,1)S(1)}, u32[]{:S(2)}, u32[]{:S(2)}) collective-permute-start(bf16[64,896]{1,0:T(8,128)(2,1)S(1)} %pool_pair.1.after.p0), channel_id=1, source_target_pairs={{0,6},{1,7},{2,4},{3,5},{4,2},{5,3},{6,0},{7,1},{8,14},{9,15},{10,... | collective-permute-start | bytes 344072 | tf_op jit(solution)/shard_map/ppermute | solution.py:478
  13.5 2.6 %copy-start = (bf16[768,768]{1,0:T(8,128)(2,1)S(1)}, bf16[768,768]{1,0:T(8,128)(2,1)}, u32[]{:S(2)}) copy-start(bf16[768,768]{1,0:T(8,128)(2,1)} %w_out.3) | copy-start | bytes 3538948
  13.5 2.6 %copy-start.1 = (bf16[16,50,768]{2,0,1:T(8,128)(2,1)S(1)}, bf16[16,50,768]{2,0,1:T(8,128)(2,1)}, u32[]{:S(2)}) copy-start(bf16[16,50,768]{2,0,1:T(8,128)(2,1)} %param.25) | copy-start | bytes 3686404
  13.5 2.6 %copy-start.6 = (s32[16,50]{1,0:T(8,128)S(1)}, s32[16,50]{1,0:T(8,128)}, u32[]{:S(2)}) copy-start(s32[16,50]{1,0:T(8,128)} %slots.1) | copy-start | bytes 9604
  13.5 2.6 %copy-start.7 = (s32[1,16,64]{2,1,0:T(8,128)S(1)}, s32[1,16,64]{2,1,0:T(8,128)}, u32[]{:S(2)}) copy-start(s32[1,16,64]{2,1,0:T(8,128)} %requests.1) | copy-start | bytes 12292
  13.5 2.6 %copy-start.9 = (s32[16]{0:T(128)S(1)}, s32[16]{0:T(128)}, u32[]{:S(2)}) copy-start(s32[16]{0:T(128)} %lens.3) | copy-start | bytes 196
  51.0 5.0 %collective-permute-start.4 = (bf16[1024,768]{1,0:T(8,128)(2,1)S(1)}, bf16[1024,768]{1,0:T(8,128)(2,1)S(1)}, u32[]{:S(2)}, u32[]{:S(2)}) collective-permute-start(bf16[1024,768]{1,0:T(8,128)(2,1)S(1)} %bitcast.11), channel_id=1, source_target_pairs={{0,1},{1,0},{2,3},{3,2},{4,5},{5,4},{6,7},{7,6},{8,9},{9,8},{10,11... | collective-permute-start | bytes 4718600 | tf_op jit(solution)/shard_map/ppermute | solution.py:478
  52.9 3.0 %copy-start.3 = (bf16[50,768]{1,0:T(8,128)(2,1)S(1)}, bf16[50,768]{1,0:T(8,128)(2,1)}, u32[]{:S(2)}) copy-start(bf16[50,768]{1,0:T(8,128)(2,1)} %pos.1) | copy-start | bytes 230404
  52.9 3.0 %copy-start.8 = (f32[768]{0:T(1024)S(1)}, f32[768]{0:T(1024)}, u32[]{:S(2)}) copy-start(f32[768]{0:T(1024)} %gain.2) | copy-start | bytes 9220
  72.5 3.2 %collective-permute-start.6 = (bf16[896,768]{1,0:T(8,128)(2,1)S(1)}, bf16[896,768]{1,0:T(8,128)(2,1)S(1)}, u32[]{:S(2)}, u32[]{:S(2)}) collective-permute-start(bf16[896,768]{1,0:T(8,128)(2,1)S(1)} %get-tuple-element.34.rows), channel_id=1, source_target_pairs={{0,1},{1,0},{2,3},{3,2},{4,5},{5,4},{6,7},{7,6},{8,9},{9,8},{10,11... | collective-permute-start | bytes 4128776 | tf_op jit(solution)/shard_map/ppermute | solution.py:478
  72.9 2.8 %collective-permute-start.5 = (s32[1,896]{1,0:T(1,128)S(1)}, s32[1,896]{1,0:T(1,128)S(1)}, u32[]{:S(2)}, u32[]{:S(2)}) collective-permute-start(s32[1,896]{1,0:T(1,128)S(1)} %get-tuple-element.33), channel_id=1, source_target_pairs={{0,1},{1,0},{2,3},{3,2},{4,5},{5,4},{6,7},{7,6},{8,9},{9,8},{10,11... | collective-permute-start | bytes 10760 | tf_op jit(solution)/shard_map/ppermute | solution.py:478
  102.5 9.0 %collective-permute-start.7 = (bf16[64,768]{1,0:T(8,128)(2,1)S(1)}, bf16[64,768]{1,0:T(8,128)(2,1)S(1)}, u32[]{:S(2)}, u32[]{:S(2)}) collective-permute-start(bf16[64,768]{1,0:T(8,128)(2,1)S(1)} %add_owners.1.after.a), channel_id=1, source_target_pairs={{0,2},{1,3},{2,0},{3,1},{4,6},{5,7},{6,4},{7,5},{8,10},{9,11},{10,... | collective-permute-start | bytes 294920 | tf_op jit(solution)/shard_map/ppermute | solution.py:478
  102.6 8.9 %collective-permute-start.8 = (bf16[64,768]{1,0:T(8,128)(2,1)S(1)}, bf16[64,768]{1,0:T(8,128)(2,1)S(1)}, u32[]{:S(2)}, u32[]{:S(2)}) collective-permute-start(bf16[64,768]{1,0:T(8,128)(2,1)S(1)} %add_owners.1.after.a), channel_id=1, source_target_pairs={{0,4},{1,5},{2,6},{3,7},{4,0},{5,1},{6,2},{7,3},{8,12},{9,13},{10,... | collective-permute-start | bytes 294920 | tf_op jit(solution)/shard_map/ppermute | solution.py:478
  104.5 7.0 %collective-permute-start.9 = (bf16[64,768]{1,0:T(8,128)(2,1)S(1)}, bf16[64,768]{1,0:T(8,128)(2,1)S(1)}, u32[]{:S(2)}, u32[]{:S(2)}) collective-permute-start(bf16[64,768]{1,0:T(8,128)(2,1)S(1)} %add_owners.1.after.a), channel_id=1, source_target_pairs={{0,6},{1,7},{2,4},{3,5},{4,2},{5,3},{6,0},{7,1},{8,14},{9,15},{10,... | collective-permute-start | bytes 294920 | tf_op jit(solution)/shard_map/ppermute | solution.py:478
  106.5 6.4 %collective-permute-start.11 = (bf16[64,896]{1,0:T(8,128)(2,1)S(1)}, bf16[64,896]{1,0:T(8,128)(2,1)S(1)}, u32[]{:S(2)}, u32[]{:S(2)}) collective-permute-start(bf16[64,896]{1,0:T(8,128)(2,1)S(1)} %get-tuple-element.36.pay_mine), channel_id=1, source_target_pairs={{0,1},{1,0},{2,3},{3,2},{4,5},{5,4},{6,7},{7,6},{8,9},{9,8},{10,11... | collective-permute-start | bytes 344072 | tf_op jit(solution)/shard_map/ppermute | solution.py:478
  109.1 4.7 %copy-start.2 = (bf16[128,1,768]{2,0,1:T(8,128)(2,1)S(1)}, bf16[128,1,768]{2,0,1:T(8,128)(2,1)}, u32[]{:S(2)}) copy-start(bf16[128,1,768]{2,0,1:T(8,128)(2,1)} %param.13) | copy-start | bytes 589828
  109.1 4.7 %copy-start.4 = (f32[768]{0:T(1024)S(1)}, f32[768]{0:T(1024)}, u32[]{:S(2)}) copy-start(f32[768]{0:T(1024)} %gain.3) | copy-start | bytes 9220
  111.6 2.1 %collective-permute-start.10 = (bf16[64,768]{1,0:T(8,128)(2,1)S(1)}, bf16[64,768]{1,0:T(8,128)(2,1)S(1)}, u32[]{:S(2)}, u32[]{:S(2)}) collective-permute-start(bf16[64,768]{1,0:T(8,128)(2,1)S(1)} %add_parts.1.d_mine), channel_id=1, source_target_pairs={{0,1},{1,0},{2,3},{3,2},{4,5},{5,4},{6,7},{7,6},{8,9},{9,8},{10,11... | collective-permute-start | bytes 294920 | tf_op jit(solution)/shard_map/ppermute | solution.py:478

commit v3 on v2

--- a/solution.py
+++ b/solution.py
@@ -13,11 +13,11 @@
 L = 50
 LP = 56
 USERS = 16
-GROUP = 8
+GROUP = 16
 ROWS = GROUP * LP
 SUB = 4
 SUB_ROWS = SUB * LP
-ENC_MB = 28
+ENC_MB = 36
 OWNERS = 16
 HALF = 64
 CAP = 64
@@ -285,16 +285,28 @@
     )(index, table)
 
 
-def encoder(lens, index, own_rows, table, pos, gain, w_qkv, w_out, d_out, d_attended, encoded, d_inputs):
+def encoder(
+    lens, index, own_rows, table, pos, gain, w_qkv, w_out, d_out, d_attended, *rest
+):
+    encoded, d_inputs = rest[-2:]
     step = pl.program_id(0)
-    at = lax.broadcasted_iota(jnp.int32, (ROWS, OWNERS * HALF), 1)
-    x = dot_nn((at == index[...]).astype(bf16), table[...])
-    x = x + own_rows[...].astype(f32)
+    some = ROWS // 2
+    at = lax.broadcasted_iota(jnp.int32, (some, OWNERS * HALF), 1)
     places = jnp.concatenate([pos[...].astype(f32), jnp.zeros((LP - L, D), f32)], axis=0)
-    x = (x.reshape(GROUP, LP, D) + places[None]).reshape(ROWS, D)
-    xhat, rstd = normalised(x)
     g = gain[...][None, :]
-    packed = dot_nn((xhat * g).astype(bf16), w_qkv[...]).astype(bf16)
+    xs, xhats, rstds, packs = [], [], [], []
+    for part in range(2):
+        here = pl.ds(part * some, some)
+        x = dot_nn((at == index[here, :]).astype(bf16), table[...])
+        x = x + own_rows[here, :].astype(f32)
+        x = (x.reshape(some // LP, LP, D) + places[None]).reshape(some, D)
+        xs.append(x)
+    for x in xs:
+        xhat, rstd = normalised(x)
+        xhats.append(xhat)
+        rstds.append(rstd)
+        packs.append(dot_nn((xhat * g).astype(bf16), w_qkv[...]).astype(bf16))
+    x, xhat, rstd, packed = [jnp.concatenate(v, axis=0) for v in (xs, xhats, rstds, packs)]
 
     subs = range(GROUP // SUB)
     cut = lambda value, sub: value[sub * SUB_ROWS : (sub + 1) * SUB_ROWS]
@@ -330,11 +342,16 @@
     d_k = join([dot_tn(d_scores[sub], q[sub]).astype(bf16) for sub in subs])
     d_v = join([dot_tn(probs16[sub], cut(d_att, sub)).astype(bf16) for sub in subs])
     encoded[...] = jnp.where(join(live), x + dot_nn(attended, w_out[...]), 0.0).astype(bf16)
-    d_normed = dot_nt(jnp.concatenate([d_q, d_k, d_v], axis=1), w_qkv[...]).astype(bf16).astype(f32)
-    d_inputs[...] = (d_out[...].astype(f32) + norm_back(d_normed, g, xhat, rstd)).astype(bf16)
-
-
-def run_encoder(lens, index, own_rows, table, pos, gain, w_qkv, w_out, d_out, d_attended):
+    joined = jnp.concatenate([d_q, d_k, d_v], axis=1)
+    step_rows = ROWS // 2
+    for part in range(2):
+        lo, hi = part * step_rows, (part + 1) * step_rows
+        d_normed = dot_nt(joined[lo:hi], w_qkv[...]).astype(bf16).astype(f32)
+        back = norm_back(d_normed, g, xhat[lo:hi], rstd[lo:hi])
+        d_inputs[lo:hi, :] = (d_out[lo:hi, :].astype(f32) + back).astype(bf16)
+
+
+def run_encoder(lens, index, own_rows, table, pos, gain, w_qkv, w_out, d_out, d_attended, early):
     part = lambda w: pl.BlockSpec((ROWS, w), lambda j: (j, 0))
     count = USERS * LP
     return pl.pallas_call(
@@ -342,12 +359,13 @@
         grid=(USERS // GROUP,),
         in_specs=[
             SMEM, part(1), part(D), VMEM, VMEM, VMEM, VMEM, VMEM, part(D), part(D),
+            *[ANY] * len(early),
         ],
         out_specs=[part(D), part(D)],
         out_shape=[jax.ShapeDtypeStruct((count, D), bf16)] * 2,
         compiler_params=params(ENC_MB),
         name="user_encoder",
-    )(lens, index, own_rows, table, pos, gain, in_vmem(w_qkv), w_out, in_vmem(d_out), in_vmem(d_attended))
+    )(lens, index, own_rows, table, pos, gain, in_vmem(w_qkv), w_out, in_vmem(d_out), in_vmem(d_attended), *[in_vmem(x) for x in early])
 
 
 def reorder(by_user, after, by_place, wide):
@@ -512,12 +530,13 @@
     table = lax.all_to_all(spread, "dp", split_axis=0, concat_axis=0, tiled=True).reshape(OWNERS * HALF, D)
     other_table = swap_with(table, 1)
     own_rows = run_gather_own(own_column, table)
+    peer_index = swap_with(other_row, 1)
+    pay_other = swap_with(pay_mine, 1)
     encoded, d_inputs = run_encoder(
-        hist_len, other_column, own_rows, other_table, pos_embed, user_gain, qkv, w_out, d_out, d_attended
+        hist_len, other_column, own_rows, other_table, pos_embed, user_gain, qkv, w_out, d_out, d_attended,
+        (peer_index, pay_other),
     )
     peer_rows = swap_with(d_inputs, 1)
-    peer_index = swap_with(other_row, 1)
-    pay_other = swap_with(pay_mine, 1)
     d_table = run_scatter(scatter, own_row, d_inputs)
     d_table = run_scatter(scatter_more, peer_index, peer_rows, d_table)
     returned = lax.all_to_all(

time: 117 us -> 112 us (0.957)
  Pallas kernels: 40.5 us -> 36.9 us
    pallas_call x1, Pallas kernels: 16.5 us -> 13.3 us  [run_encoder(): pl.pallas_call(encoder, grid=(USERS // GROUP,), in_specs=[SMEM, part(1),...]
  transfers between devices with their start and end apart: 12 -> 12, of which waited for: 5 -> 6; matrix products, arithmetic and copies ran while one was open for 0% -> 0% of each run, Pallas kernels for 11% -> 11%
where the time goes in v3:
time: 112 us
  blocking collectives  53.3 us (48%)
  Pallas kernels  36.9 us (33%)
  starting transfers between devices  15.1 us (13%)
  waiting for transfers between devices  5.41 us (5%)
    all_to_all x1, blocking collectives, shards(): lax.all_to_all(spread, 'dp', split_axis=0, concat_axis=0, tiled=True)  28.7 us
    all_to_all x1, blocking collectives, shards(): lax.all_to_all(d_table.reshape(OWNERS, HALF, D), 'dp', split_axis=0, conc...  24.6 us
    ppermute x12, starting transfers between devices, swap_with(): return lax.ppermute(x, 'frame', pairs)  15.1 us
    pallas_call x1, Pallas kernels, run_encoder(): pl.pallas_call(encoder, grid=(USERS // GROUP,), in_specs=[SMEM, part(1),...  13.3 us
    pallas_call x1, Pallas kernels, run_frame_forward(): pl.pallas_call(frame_forward, in_specs=[SMEM, HBM, HBM, HBM, HBM], out_sp...  6.3 us
    ppermute x12, waiting for transfers between devices, swap_with(): return lax.ppermute(x, 'frame', pairs)  5.41 us
    pallas_call x2, Pallas kernels, run_scatter(): pl.pallas_call(body, grid=(steps,), in_specs=[VMEM, VMEM, part][:len(oper...  3.99 us
    pallas_call x1, Pallas kernels, run_prepare(): pl.pallas_call(prepare, in_specs=[SMEM, SMEM] + [VMEM] * 4 + [HBM, ANY],...  3.08 us
  transfers between devices with their start and end apart: 12, of which 6 were waited for; matrix products, arithmetic and copies ran while one was open for 0% of the time, Pallas kernels for 11%

profile of v3, /device:TPU:1, one launch (start us, length us, event | category | flops | bytes accessed | tf_op | source)
XLA Modules:
  0.0 111.6 jit_solution(8556259860871349199)
XLA Ops:
  0.6 0.0 copy-start.5
  0.7 6.3 %frame_forward.1 = (bf16[64,768]{1,0:T(8,128)(2,1)S(1)}, bf16[64,768]{1,0:T(8,128)(2,1)S(1)}, bf16[128,768]{1,0:T(8,128)(2,1)S(1)}, bf16[128,3072]{1,0:T(8,128)(...) custom-call(s32[1]{0:T(128)} %bitcast.core, bf16[128,768]{1,0:T(8,128)(2,1)} %bitcast.15, ...), custom_call_target="tpu_custom_call" | custom-call | tf_op jit(solution)/shard_map/frame_forward/pallas_call | solution.py:128
  7.0 1.5 %collective-permute-start = (bf16[64,768]{1,0:T(8,128)(2,1)S(1)}, bf16[64,768]{1,0:T(8,128)(2,1)S(1)}, u32[]{:S(2)}, u32[]{:S(2)}) collective-permute-start(bf16[64,768]{1,0:T(8,128)(2,1)S(1)} %get-tuple-element.22), channel_id=1, source_target_pairs={{0,1},{1,0},{2,3},{3,2},{4,5},{5,4},{6,7},{7,6},{8,9},{9,8},{10,11... | collective-permute-start | bytes 294920 | tf_op jit(solution)/shard_map/ppermute | solution.py:496
  8.5 0.9 collective-permute-done.theirs
  9.4 0.0 copy-done.5
  9.4 0.2 pool_pair.1.after.p0
  9.6 2.6 %collective-permute-start.3 = (bf16[64,896]{1,0:T(8,128)(2,1)S(1)}, bf16[64,896]{1,0:T(8,128)(2,1)S(1)}, u32[]{:S(2)}, u32[]{:S(2)}) collective-permute-start(bf16[64,896]{1,0:T(8,128)(2,1)S(1)} %pool_pair.1.after.p0), channel_id=1, source_target_pairs={{0,6},{1,7},{2,4},{3,5},{4,2},{5,3},{6,0},{7,1},{8,14},{9,15},{10,... | collective-permute-start | bytes 344072 | tf_op jit(solution)/shard_map/ppermute | solution.py:496
  12.2 0.5 collective-permute-start.2
  12.8 0.2 collective-permute-start.1
  12.9 0.0 copy-start
  12.9 0.0 copy-start.1
  12.9 0.0 copy-start.6
  12.9 0.0 copy-start.7
  12.9 0.0 copy-start.9
  12.9 2.6 %turn.1 = (bf16[3072,768]{1,0:T(8,128)(2,1)S(1)}, bf16[768,3072]{1,0:T(8,128)(2,1)S(1)}) custom-call(bf16[768,3072]{1,0:T(8,128)(2,1)S(1)} %get-tuple-element.26.up, bf16[3072,768]{1,0:T(8,128)(2,1)S(1)} %get-tuple-element.27.down, bf16[64,896]{1,0:T(8,128)(2,1)S(1)} %pool_pair.1.after.p0), custom_call_target="tpu_custom_call" | custom-call | flops 2359296 | bytes 18874368 | tf_op jit(solution)/shard_map/turn/pallas_call | solution.py:443
  15.5 0.0 copy-done
  15.5 0.0 copy-done.1
  15.6 0.0 copy-done.6
  15.6 0.0 copy-done.7
  15.6 0.0 copy-done.9
  15.6 3.1 %prepare.1 = (bf16[896,768]{1,0:T(8,128)(2,1)S(1)}, bf16[896,768]{1,0:T(8,128)(2,1)S(1)}, s32[896,1]{1,0:T(8,128)S(1)}, s32[896,1]{1,0:T(8,128)S(1)}, s32[1,896]...) custom-call(s32[1]{0:T(128)} %bitcast.core, s32[16]{0:T(128)S(1)} %copy-done.9, ...), custom_call_target="tpu_custom_call" | custom-call | flops 1056964608 | bytes 5505024 | tf_op jit(solution)/shard_map/prepare/pallas_call | solution.py:253
  18.7 0.0 collective-permute-done.3.p3
  18.7 0.0 collective-permute-done.2.p2
  18.7 0.0 collective-permute-done.1.p1
  18.7 0.3 pool_all.1
  19.0 28.7 %all_to_all.10 = bf16[16,64,768]{2,1,0:T(8,128)(2,1)S(1)} all-to-all(bf16[16,64,768]{2,1,0:T(8,128)(2,1)S(1)} %get-tuple-element.29), channel_id=1, replica_groups=mesh['dp'=16,'frame'=8] {'dp'}, dimensions={0} | all-to-all | bytes 3145728 | tf_op jit(solution)/shard_map/all_to_all | solution.py:530
  47.7 2.8 %collective-permute-start.4 = (bf16[1024,768]{1,0:T(8,128)(2,1)S(1)}, bf16[1024,768]{1,0:T(8,128)(2,1)S(1)}, u32[]{:S(2)}, u32[]{:S(2)}) collective-permute-start(bf16[1024,768]{1,0:T(8,128)(2,1)S(1)} %bitcast.11), channel_id=1, source_target_pairs={{0,1},{1,0},{2,3},{3,2},{4,5},{5,4},{6,7},{7,6},{8,9},{9,8},{10,11... | collective-permute-start | bytes 4718600 | tf_op jit(solution)/shard_map/ppermute | solution.py:496
  50.6 0.0 collective-permute-start.5
  50.6 0.5 collective-permute-start.6
  51.1 0.0 copy-start.3
  51.1 0.0 copy-start.8
  51.1 1.6 %gather_own.1.own_rows = bf16[896,768]{1,0:T(8,128)(2,1)S(1)} custom-call(s32[896,1]{1,0:T(8,128)S(1)} %get-tuple-element.24.index, bf16[1024,768]{1,0:T(8,128)(2,1)S(1)} %bitcast.12), custom_call_target="tpu_custom_call" | custom-call | flops 1409286144 | bytes 4128768 | tf_op jit(solution)/shard_map/gather_own/pallas_call | solution.py:276
  52.7 0.9 collective-permute-done.5.rest_0_.index
  53.6 0.2 collective-permute-done.6.rest_1_.pay_other
  53.8 0.0 collective-permute-done.4.table
  53.8 0.0 copy-done.3
  53.8 0.0 copy-done.8
  53.8 13.3 %user_encoder.1 = (bf16[896,768]{1,0:T(8,128)(2,1)S(1)}, bf16[896,768]{1,0:T(8,128)(2,1)S(1)}) custom-call(s32[16]{0:T(128)S(1)} %copy-done.9, s32[896,1]{1,0:T(8,128)S(1)} %get-tuple-element.23.index, bf16[896,768]{1,0:T(8,128)(2,1)S(1)} %gather_own.1.own_rows, bf16[1024,768]{1,0:T(8,128)(2,1)S(1)} %collective-permute-done.4.table, ...), custom_call_target="tpu_custom_call" | custom-call | tf_op jit(solution)/shard_map/user_encoder/pallas_call | solution.py:357
  67.1 0.5 collective-permute-start.7
  67.5 2.0 %scatter.1.so_far = bf16[1024,768]{1,0:T(8,128)(2,1)S(1)} custom-call(s32[1,896]{1,0:T(1,128)S(1)} %get-tuple-element.36.index, bf16[896,768]{1,0:T(8,128)(2,1)S(1)} %get-tuple-element.35.rows), custom_call_target="tpu_custom_call" | custom-call | flops 1409286144 | bytes 4128768 | tf_op jit(solution)/shard_map/scatter/pallas_call | solution.py:423
  69.5 0.8 collective-permute-done.7.rows
  70.3 2.0 %scatter_more.1 = bf16[1024,768]{1,0:T(8,128)(2,1)S(1)} custom-call(s32[1,896]{1,0:T(1,128)S(1)} %collective-permute-done.5.rest_0_.index, bf16[896,768]{1,0:T(8,128)(2,1)S(1)} %collective-permute-done.7.rows, bf16[1024,768]{1,0:T(8,128)(2,1)S(1)} %scatter.1.so_far), custom_call_target="tpu_custom_call" | custom-call | flops 1409286144 | bytes 4128768 | tf_op jit(solution)/shard_map/scatter_more/pallas_call | solution.py:423
  72.3 24.6 %all_to_all.11.parts = bf16[16,64,768]{2,1,0:T(8,128)(2,1)S(1)} all-to-all(bf16[16,64,768]{2,1,0:T(8,128)(2,1)S(1)} %bitcast.13), channel_id=1, replica_groups=mesh['dp'=16,'frame'=8] {'dp'}, dimensions={0} | all-to-all | bytes 3145728 | tf_op jit(solution)/shard_map/all_to_all | solution.py:542
  96.9 0.2 add_owners.1.after.a
  97.1 2.4 %collective-permute-start.10 = (bf16[64,768]{1,0:T(8,128)(2,1)S(1)}, bf16[64,768]{1,0:T(8,128)(2,1)S(1)}, u32[]{:S(2)}, u32[]{:S(2)}) collective-permute-start(bf16[64,768]{1,0:T(8,128)(2,1)S(1)} %add_owners.1.after.a), channel_id=1, source_target_pairs={{0,6},{1,7},{2,4},{3,5},{4,2},{5,3},{6,0},{7,1},{8,14},{9,15},{10,... | collective-permute-start | bytes 294920 | tf_op jit(solution)/shard_map/ppermute | solution.py:496
  99.5 0.5 collective-permute-start.9
  100.1 0.3 collective-permute-start.8
  100.4 0.0 copy-start.2
  100.4 0.0 copy-start.4
  100.4 2.5 %reorder.1.after = bf16[800,768]{1,0:T(8,128)(2,1)} custom-call(bf16[896,768]{1,0:T(8,128)(2,1)S(1)} %get-tuple-element.34.by_user, bf16[64,768]{1,0:T(8,128)(2,1)S(1)} %add_owners.1.after.a), custom_call_target="tpu_custom_call" | custom-call | flops 614400 | bytes 3686400 | tf_op jit(solution)/shard_map/reorder/pallas_call | solution.py:383
  102.9 0.0 collective-permute-done.10.d
  102.9 1.7 %collective-permute-done.9.c = bf16[64,768]{1,0:T(8,128)(2,1)S(1)} collective-permute-done((bf16[64,768]{1,0:T(8,128)(2,1)S(1)}, bf16[64,768]{1,0:T(8,128)(2,1)S(1)}, u32[]{:S(2)}, u32[]{:S(2)}) %collective-permute-start.9) | collective-permute-done | bytes 98336 | tf_op jit(solution)/shard_map/ppermute | solution.py:496
  104.6 0.0 collective-permute-done.8.b
  104.6 0.1 add_parts.1.d_mine
  104.7 3.2 %collective-permute-start.11 = (bf16[64,768]{1,0:T(8,128)(2,1)S(1)}, bf16[64,768]{1,0:T(8,128)(2,1)S(1)}, u32[]{:S(2)}, u32[]{:S(2)}) collective-permute-start(bf16[64,768]{1,0:T(8,128)(2,1)S(1)} %add_parts.1.d_mine), channel_id=1, source_target_pairs={{0,1},{1,0},{2,3},{3,2},{4,5},{5,4},{6,7},{7,6},{8,9},{9,8},{10,11... | collective-permute-start | bytes 294920 | tf_op jit(solution)/shard_map/ppermute | solution.py:496
  107.8 0.9 collective-permute-done.11.d_other
  108.8 0.0 copy-done.2
  108.8 0.0 copy-done.4
  108.8 2.8 %frame_backward.1 = bf16[128,768]{1,0:T(8,128)(2,1)} custom-call(s32[1]{0:T(128)} %bitcast.core, bf16[64,768]{1,0:T(8,128)(2,1)S(1)} %add_parts.1.d_mine, bf16[64,768]{1,0:T(8,128)(2,1)S(1)} %collective-permute-done.11.d_other, bf16[64,896]{1,0:T(8,128)(2,1)S(1)} %get-tuple-element.33.pay_mine, bf16[64,896]{1,0:T(8,128)(2,1)S(1)} %collective-permute-done.6.rest_1_.pay_other, ...), custom_call_target="tpu_custom_call" | custom-call | tf_op jit(solution)/shard_map/frame_backward/pallas_call | solution.py:484
Async XLA Ops:
  0.6 8.8 %copy-start.5 = (f32[768]{0:T(1024)S(1)}, f32[768]{0:T(1024)}, u32[]{:S(2)}) copy-start(f32[768]{0:T(1024)} %query.3) | copy-start | bytes 9220
  7.0 2.4 %collective-permute-start = (bf16[64,768]{1,0:T(8,128)(2,1)S(1)}, bf16[64,768]{1,0:T(8,128)(2,1)S(1)}, u32[]{:S(2)}, u32[]{:S(2)}) collective-permute-start(bf16[64,768]{1,0:T(8,128)(2,1)S(1)} %get-tuple-element.22), channel_id=1, source_target_pairs={{0,1},{1,0},{2,3},{3,2},{4,5},{5,4},{6,7},{7,6},{8,9},{9,8},{10,11... | collective-permute-start | bytes 294920 | tf_op jit(solution)/shard_map/ppermute | solution.py:496
  9.6 9.1 %collective-permute-start.3 = (bf16[64,896]{1,0:T(8,128)(2,1)S(1)}, bf16[64,896]{1,0:T(8,128)(2,1)S(1)}, u32[]{:S(2)}, u32[]{:S(2)}) collective-permute-start(bf16[64,896]{1,0:T(8,128)(2,1)S(1)} %pool_pair.1.after.p0), channel_id=1, source_target_pairs={{0,6},{1,7},{2,4},{3,5},{4,2},{5,3},{6,0},{7,1},{8,14},{9,15},{10,... | collective-permute-start | bytes 344072 | tf_op jit(solution)/shard_map/ppermute | solution.py:496
  12.2 6.5 %collective-permute-start.2 = (bf16[64,896]{1,0:T(8,128)(2,1)S(1)}, bf16[64,896]{1,0:T(8,128)(2,1)S(1)}, u32[]{:S(2)}, u32[]{:S(2)}) collective-permute-start(bf16[64,896]{1,0:T(8,128)(2,1)S(1)} %pool_pair.1.after.p0), channel_id=1, source_target_pairs={{0,4},{1,5},{2,6},{3,7},{4,0},{5,1},{6,2},{7,3},{8,12},{9,13},{10,... | collective-permute-start | bytes 344072 | tf_op jit(solution)/shard_map/ppermute | solution.py:496
  12.8 5.9 %collective-permute-start.1 = (bf16[64,896]{1,0:T(8,128)(2,1)S(1)}, bf16[64,896]{1,0:T(8,128)(2,1)S(1)}, u32[]{:S(2)}, u32[]{:S(2)}) collective-permute-start(bf16[64,896]{1,0:T(8,128)(2,1)S(1)} %pool_pair.1.after.p0), channel_id=1, source_target_pairs={{0,2},{1,3},{2,0},{3,1},{4,6},{5,7},{6,4},{7,5},{8,10},{9,11},{10,... | collective-permute-start | bytes 344072 | tf_op jit(solution)/shard_map/ppermute | solution.py:496
  12.9 2.6 %copy-start = (bf16[768,768]{1,0:T(8,128)(2,1)S(1)}, bf16[768,768]{1,0:T(8,128)(2,1)}, u32[]{:S(2)}) copy-start(bf16[768,768]{1,0:T(8,128)(2,1)} %w_out.3) | copy-start | bytes 3538948
  12.9 2.6 %copy-start.1 = (bf16[16,50,768]{2,0,1:T(8,128)(2,1)S(1)}, bf16[16,50,768]{2,0,1:T(8,128)(2,1)}, u32[]{:S(2)}) copy-start(bf16[16,50,768]{2,0,1:T(8,128)(2,1)} %param.25) | copy-start | bytes 3686404
  12.9 2.6 %copy-start.6 = (s32[16,50]{1,0:T(8,128)S(1)}, s32[16,50]{1,0:T(8,128)}, u32[]{:S(2)}) copy-start(s32[16,50]{1,0:T(8,128)} %slots.1) | copy-start | bytes 9604
  12.9 2.6 %copy-start.7 = (s32[1,16,64]{2,1,0:T(8,128)S(1)}, s32[1,16,64]{2,1,0:T(8,128)}, u32[]{:S(2)}) copy-start(s32[1,16,64]{2,1,0:T(8,128)} %requests.1) | copy-start | bytes 12292
  12.9 2.6 %copy-start.9 = (s32[16]{0:T(128)S(1)}, s32[16]{0:T(128)}, u32[]{:S(2)}) copy-start(s32[16]{0:T(128)} %lens.3) | copy-start | bytes 196
  47.7 6.0 %collective-permute-start.4 = (bf16[1024,768]{1,0:T(8,128)(2,1)S(1)}, bf16[1024,768]{1,0:T(8,128)(2,1)S(1)}, u32[]{:S(2)}, u32[]{:S(2)}) collective-permute-start(bf16[1024,768]{1,0:T(8,128)(2,1)S(1)} %bitcast.11), channel_id=1, source_target_pairs={{0,1},{1,0},{2,3},{3,2},{4,5},{5,4},{6,7},{7,6},{8,9},{9,8},{10,11... | collective-permute-start | bytes 4718600 | tf_op jit(solution)/shard_map/ppermute | solution.py:496
  50.6 3.0 %collective-permute-start.5 = (s32[1,896]{1,0:T(1,128)S(1)}, s32[1,896]{1,0:T(1,128)S(1)}, u32[]{:S(2)}, u32[]{:S(2)}) collective-permute-start(s32[1,896]{1,0:T(1,128)S(1)} %get-tuple-element.32), channel_id=1, source_target_pairs={{0,1},{1,0},{2,3},{3,2},{4,5},{5,4},{6,7},{7,6},{8,9},{9,8},{10,11... | collective-permute-start | bytes 10760 | tf_op jit(solution)/shard_map/ppermute | solution.py:496
  50.6 3.2 %collective-permute-start.6 = (bf16[64,896]{1,0:T(8,128)(2,1)S(1)}, bf16[64,896]{1,0:T(8,128)(2,1)S(1)}, u32[]{:S(2)}, u32[]{:S(2)}) collective-permute-start(bf16[64,896]{1,0:T(8,128)(2,1)S(1)} %get-tuple-element.33.pay_mine), channel_id=1, source_target_pairs={{0,1},{1,0},{2,3},{3,2},{4,5},{5,4},{6,7},{7,6},{8,9},{9,8},{10,11... | collective-permute-start | bytes 344072 | tf_op jit(solution)/shard_map/ppermute | solution.py:496
  51.1 2.7 %copy-start.3 = (bf16[50,768]{1,0:T(8,128)(2,1)S(1)}, bf16[50,768]{1,0:T(8,128)(2,1)}, u32[]{:S(2)}) copy-start(bf16[50,768]{1,0:T(8,128)(2,1)} %pos.1) | copy-start | bytes 230404
  51.1 2.7 %copy-start.8 = (f32[768]{0:T(1024)S(1)}, f32[768]{0:T(1024)}, u32[]{:S(2)}) copy-start(f32[768]{0:T(1024)} %gain.2) | copy-start | bytes 9220
  67.1 3.2 %collective-permute-start.7 = (bf16[896,768]{1,0:T(8,128)(2,1)S(1)}, bf16[896,768]{1,0:T(8,128)(2,1)S(1)}, u32[]{:S(2)}, u32[]{:S(2)}) collective-permute-start(bf16[896,768]{1,0:T(8,128)(2,1)S(1)} %get-tuple-element.35.rows), channel_id=1, source_target_pairs={{0,1},{1,0},{2,3},{3,2},{4,5},{5,4},{6,7},{7,6},{8,9},{9,8},{10,11... | collective-permute-start | bytes 4128776 | tf_op jit(solution)/shard_map/ppermute | solution.py:496
  97.1 5.8 %collective-permute-start.10 = (bf16[64,768]{1,0:T(8,128)(2,1)S(1)}, bf16[64,768]{1,0:T(8,128)(2,1)S(1)}, u32[]{:S(2)}, u32[]{:S(2)}) collective-permute-start(bf16[64,768]{1,0:T(8,128)(2,1)S(1)} %add_owners.1.after.a), channel_id=1, source_target_pairs={{0,6},{1,7},{2,4},{3,5},{4,2},{5,3},{6,0},{7,1},{8,14},{9,15},{10,... | collective-permute-start | bytes 294920 | tf_op jit(solution)/shard_map/ppermute | solution.py:496
  99.5 5.1 %collective-permute-start.9 = (bf16[64,768]{1,0:T(8,128)(2,1)S(1)}, bf16[64,768]{1,0:T(8,128)(2,1)S(1)}, u32[]{:S(2)}, u32[]{:S(2)}) collective-permute-start(bf16[64,768]{1,0:T(8,128)(2,1)S(1)} %add_owners.1.after.a), channel_id=1, source_target_pairs={{0,4},{1,5},{2,6},{3,7},{4,0},{5,1},{6,2},{7,3},{8,12},{9,13},{10,... | collective-permute-start | bytes 294920 | tf_op jit(solution)/shard_map/ppermute | solution.py:496
  100.1 4.5 %collective-permute-start.8 = (bf16[64,768]{1,0:T(8,128)(2,1)S(1)}, bf16[64,768]{1,0:T(8,128)(2,1)S(1)}, u32[]{:S(2)}, u32[]{:S(2)}) collective-permute-start(bf16[64,768]{1,0:T(8,128)(2,1)S(1)} %add_owners.1.after.a), channel_id=1, source_target_pairs={{0,2},{1,3},{2,0},{3,1},{4,6},{5,7},{6,4},{7,5},{8,10},{9,11},{10,... | collective-permute-start | bytes 294920 | tf_op jit(solution)/shard_map/ppermute | solution.py:496
  100.4 8.4 %copy-start.2 = (bf16[128,1,768]{2,0,1:T(8,128)(2,1)S(1)}, bf16[128,1,768]{2,0,1:T(8,128)(2,1)}, u32[]{:S(2)}) copy-start(bf16[128,1,768]{2,0,1:T(8,128)(2,1)} %param.13) | copy-start | bytes 589828
  100.4 8.4 %copy-start.4 = (f32[768]{0:T(1024)S(1)}, f32[768]{0:T(1024)}, u32[]{:S(2)}) copy-start(f32[768]{0:T(1024)} %gain.3) | copy-start | bytes 9220
  104.7 4.1 %collective-permute-start.11 = (bf16[64,768]{1,0:T(8,128)(2,1)S(1)}, bf16[64,768]{1,0:T(8,128)(2,1)S(1)}, u32[]{:S(2)}, u32[]{:S(2)}) collective-permute-start(bf16[64,768]{1,0:T(8,128)(2,1)S(1)} %add_parts.1.d_mine), channel_id=1, source_target_pairs={{0,1},{1,0},{2,3},{3,2},{4,5},{5,4},{6,7},{7,6},{8,9},{9,8},{10,11... | collective-permute-start | bytes 294920 | tf_op jit(solution)/shard_map/ppermute | solution.py:496

commit v4 on v3

--- a/solution.py
+++ b/solution.py
@@ -18,6 +18,8 @@
 SUB = 4
 SUB_ROWS = SUB * LP
 ENC_MB = 36
+PART = USERS * LP // 2
+LANES = 512
 OWNERS = 16
 HALF = 64
 CAP = 64
@@ -224,11 +226,15 @@
         other_column[here, :] = jnp.where(own, -1, position)
     square = (128, 128)
     same = lax.broadcasted_iota(jnp.int32, square, 0) == lax.broadcasted_iota(jnp.int32, square, 1)
-    for part in range(USERS * LP // 128):
-        here = pl.ds(part * 128, 128)
-        for column, row in ((own_column, own_row), (other_column, other_row)):
-            value = jnp.where(same, column[here, :].astype(f32), 0.0)
-            row[:, here] = jnp.sum(value, axis=0, keepdims=True).astype(jnp.int32)
+    for column, row in ((own_column, own_row), (other_column, other_row)):
+        for first in range(0, PART, 128):
+            for half in range(2):
+                size = min(128, PART - first)
+                value = column[pl.ds(half * PART + first, size), :].astype(f32)
+                if size < 128:
+                    value = jnp.concatenate([value, jnp.full((128 - size, 1), -1.0, f32)], axis=0)
+                value = jnp.sum(jnp.where(same, value, 0.0), axis=0, keepdims=True)
+                row[:, pl.ds(half * LANES + first, 128)] = value.astype(jnp.int32)
 
     for j in range(D // 128):
         d_wide[j] = d_encoded[:, j * 128 : (j + 1) * 128].astype(f32)
@@ -255,41 +261,45 @@
         in_specs=[SMEM, SMEM] + [VMEM] * 4 + [HBM, ANY],
         out_specs=[VMEM] * 7,
         out_shape=[
-            pltpu.VMEM((count, D), bf16), pltpu.VMEM((count, D), bf16), whole(count, 1, jnp.int32), whole(count, 1, jnp.int32),
-            whole(1, count, jnp.int32), whole(1, count, jnp.int32), pltpu.VMEM((D, 3 * D), bf16),
+            pltpu.VMEM((count, D), bf16), pltpu.VMEM((count, D), bf16),
+            whole(count, 1, jnp.int32), whole(count, 1, jnp.int32),
+            whole(1, 2 * LANES, jnp.int32), whole(1, 2 * LANES, jnp.int32), pltpu.VMEM((D, 3 * D), bf16),
         ],
-        scratch_shapes=[pltpu.VMEM((D // 128, USERS * L, 128), f32), pltpu.SemaphoreType.DMA],
+        scratch_shapes=[
+            pltpu.VMEM((D // 128, USERS * L, 128), f32), pltpu.SemaphoreType.DMA,
+        ],
         compiler_params=params(16),
         cost_estimate=cost(2 * count * D * D, 8 * count * D),
         name="prepare",
     )(core, lens, slots, requests, d_encoded, w_out, in_hbm(w_qkv), after)
 
 
-def gather_own(index, table, out):
-    at = lax.broadcasted_iota(jnp.int32, (ROWS, OWNERS * HALF), 1)
-    out[...] = dot_nn((at == index[...]).astype(bf16), table[...]).astype(bf16)
-
-
-def run_gather_own(index, table):
-    part = lambda w: pl.BlockSpec((ROWS, w), lambda j: (j, 0))
-    count = USERS * LP
-    return pl.pallas_call(
-        gather_own,
-        grid=(USERS // GROUP,),
-        in_specs=[part(1), VMEM],
-        out_specs=part(D),
+def gather(index, table, *rest):
+    out = rest[-1]
+    at = lax.broadcasted_iota(jnp.int32, (PART, OWNERS * HALF), 1)
+    for half in range(2):
+        here = pl.ds(half * PART, PART)
+        chosen = (at == index[here, :]).astype(bf16)
+        out[here, :] = dot_nn(chosen, table[...]).astype(bf16)
+
+
+def run_gather(index, table, *after):
+    count = 2 * PART
+    return pl.pallas_call(
+        gather,
+        in_specs=[VMEM, VMEM] + [ANY] * len(after),
+        out_specs=VMEM,
         out_shape=jax.ShapeDtypeStruct((count, D), bf16),
         compiler_params=params(12),
         cost_estimate=cost(2 * count * OWNERS * HALF * D, 6 * count * D),
-        name="gather_own",
-    )(index, table)
+        name="gather",
+    )(index, table, *[in_vmem(x) for x in after])
 
 
 def encoder(
     lens, index, own_rows, table, pos, gain, w_qkv, w_out, d_out, d_attended, *rest
 ):
-    encoded, d_inputs = rest[-2:]
-    step = pl.program_id(0)
+    encoded, d_inputs_a, d_inputs_b = rest[-3:]
     some = ROWS // 2
     at = lax.broadcasted_iota(jnp.int32, (some, OWNERS * HALF), 1)
     places = jnp.concatenate([pos[...].astype(f32), jnp.zeros((LP - L, D), f32)], axis=0)
@@ -297,8 +307,8 @@
     xs, xhats, rstds, packs = [], [], [], []
     for part in range(2):
         here = pl.ds(part * some, some)
-        x = dot_nn((at == index[here, :]).astype(bf16), table[...])
-        x = x + own_rows[here, :].astype(f32)
+        chosen = (at == index[here, :]).astype(bf16)
+        x = dot_nn(chosen, table[...]) + own_rows[here, :].astype(f32)
         x = (x.reshape(some // LP, LP, D) + places[None]).reshape(some, D)
         xs.append(x)
     for x in xs:
@@ -325,7 +335,7 @@
         first = jnp.full((SUB_ROWS, 1), 0, jnp.int32)
         for u in range(SUB):
             here = (place >= u * LP) & (place < (u + 1) * LP)
-            length = jnp.where(here, lens[step * GROUP + sub * SUB + u], length)
+            length = jnp.where(here, lens[sub * SUB + u], length)
             first = jnp.where(here, u * LP, first)
         allowed = (column >= first) & (column <= place) & (column < first + length)
         live.append((place - first) < length)
@@ -348,21 +358,18 @@
         lo, hi = part * step_rows, (part + 1) * step_rows
         d_normed = dot_nt(joined[lo:hi], w_qkv[...]).astype(bf16).astype(f32)
         back = norm_back(d_normed, g, xhat[lo:hi], rstd[lo:hi])
-        d_inputs[lo:hi, :] = (d_out[lo:hi, :].astype(f32) + back).astype(bf16)
+        (d_inputs_a, d_inputs_b)[part][...] = (d_out[lo:hi, :].astype(f32) + back).astype(bf16)
 
 
 def run_encoder(lens, index, own_rows, table, pos, gain, w_qkv, w_out, d_out, d_attended, early):
-    part = lambda w: pl.BlockSpec((ROWS, w), lambda j: (j, 0))
     count = USERS * LP
     return pl.pallas_call(
         encoder,
-        grid=(USERS // GROUP,),
         in_specs=[
-            SMEM, part(1), part(D), VMEM, VMEM, VMEM, VMEM, VMEM, part(D), part(D),
-            *[ANY] * len(early),
+            SMEM, VMEM, VMEM, VMEM, VMEM, VMEM, VMEM, VMEM, VMEM, VMEM, *[ANY] * len(early),
         ],
-        out_specs=[part(D), part(D)],
-        out_shape=[jax.ShapeDtypeStruct((count, D), bf16)] * 2,
+        out_specs=[VMEM] * 3,
+        out_shape=[jax.ShapeDtypeStruct((rows, D), bf16) for rows in (count, PART, PART)],
         compiler_params=params(ENC_MB),
         name="user_encoder",
     )(lens, index, own_rows, table, pos, gain, in_vmem(w_qkv), w_out, in_vmem(d_out), in_vmem(d_attended), *[in_vmem(x) for x in early])
@@ -403,32 +410,31 @@
     out[...] = sum(part[...].astype(f32) for part in (a, b, c, d)).astype(bf16)
 
 
-def scatter(index, rows, out):
-    block = out.shape[0]
-    row = lax.broadcasted_iota(jnp.int32, (block, USERS * LP), 0) + pl.program_id(0) * block
-    out[...] = dot_nn((row == index[...]).astype(bf16), rows[...]).astype(bf16)
-
-
-def scatter_more(index, rows, so_far, out):
-    block = out.shape[0]
-    row = lax.broadcasted_iota(jnp.int32, (block, USERS * LP), 0) + pl.program_id(0) * block
-    total = dot_nn((row == index[...]).astype(bf16), rows[...])
-    out[...] = (total + so_far[...].astype(f32)).astype(bf16)
-
-
-def run_scatter(body, *operands):
-    count = USERS * LP
-    steps = 2
-    part = pl.BlockSpec((OWNERS * HALF // steps, D), lambda j: (j, 0))
-    return pl.pallas_call(
-        body,
-        grid=(steps,),
-        in_specs=[VMEM, VMEM, part][: len(operands)],
-        out_specs=part,
+def scatter(halves, own, index, *operands):
+    out = operands[-1]
+    rows = operands[: len(halves)]
+    block = OWNERS * HALF // 2
+    for k in range(2):
+        here = pl.ds(k * block, block)
+        row = lax.broadcasted_iota(jnp.int32, (block, PART), 0) + k * block
+        total = None if own else operands[len(halves)][here, :].astype(f32)
+        for half, part in zip(halves, rows):
+            chosen = (row == index[:, pl.ds(half * LANES, PART)]).astype(bf16)
+            more = dot_nn(chosen, part[...])
+            total = more if total is None else total + more
+        out[here, :] = total.astype(bf16)
+
+
+def run_scatter(halves, own, *operands):
+    count = PART * len(halves)
+    return pl.pallas_call(
+        functools.partial(scatter, halves, own),
+        in_specs=[VMEM] * len(operands),
+        out_specs=VMEM,
         out_shape=jax.ShapeDtypeStruct((OWNERS * HALF, D), bf16),
         compiler_params=params(12),
         cost_estimate=cost(2 * count * OWNERS * HALF * D, 6 * count * D),
-        name=body.__name__,
+        name="scatter",
     )(*operands)
 
 
@@ -529,16 +535,18 @@
     )(pair, *spread_along_x(pair), *early)
     table = lax.all_to_all(spread, "dp", split_axis=0, concat_axis=0, tiled=True).reshape(OWNERS * HALF, D)
     other_table = swap_with(table, 1)
-    own_rows = run_gather_own(own_column, table)
+    own_rows = run_gather(own_column, table)
     peer_index = swap_with(other_row, 1)
     pay_other = swap_with(pay_mine, 1)
-    encoded, d_inputs = run_encoder(
+    encoded, d_a, d_b = run_encoder(
         hist_len, other_column, own_rows, other_table, pos_embed, user_gain, qkv, w_out, d_out, d_attended,
         (peer_index, pay_other),
     )
-    peer_rows = swap_with(d_inputs, 1)
-    d_table = run_scatter(scatter, own_row, d_inputs)
-    d_table = run_scatter(scatter_more, peer_index, peer_rows, d_table)
+    back_a = swap_with(d_a, 1)
+    back_b = swap_with(d_b, 1)
+    d_table = run_scatter((0, 1), True, own_row, d_a, d_b)
+    d_table = run_scatter((0,), False, peer_index, back_a, d_table)
+    d_table = run_scatter((1,), False, peer_index, back_b, d_table)
     returned = lax.all_to_all(
         d_table.reshape(OWNERS, HALF, D), "dp", split_axis=0, concat_axis=0, tiled=True
     )

time: 112 us -> 111 us (level)
    ppermute x12 -> x13, waiting for transfers between devices: 5.41 us -> 4.57 us  [swap_with(): return lax.ppermute(x, 'frame', pairs)]
    pallas_call x4 -> x5, Pallas kernels: 18.9 us -> 18.7 us  [the longest x1 13.3 us: run_encoder(): pl.pallas_call(encoder, in_specs=[SMEM, VMEM, VMEM, VMEM, VMEM, VMEM, VME...]
    ppermute x12 -> x13, starting transfers between devices: 15.1 us -> 15.2 us  [swap_with(): return lax.ppermute(x, 'frame', pairs)]
  transfers between devices with their start and end apart: 12 -> 13, of which waited for: 6 -> 5; matrix products, arithmetic and copies ran while one was open for 0% -> 0% of each run, Pallas kernels for 11% -> 11%
where the time goes in v4:
time: 111 us
  blocking collectives  53.5 us (48%)
  Pallas kernels  36.8 us (33%)
  starting transfers between devices  15.2 us (14%)
  waiting for transfers between devices  4.57 us (4%)
    all_to_all x1, blocking collectives, shards(): lax.all_to_all(spread, 'dp', split_axis=0, concat_axis=0, tiled=True)  28.8 us
    all_to_all x1, blocking collectives, shards(): lax.all_to_all(d_table.reshape(OWNERS, HALF, D), 'dp', split_axis=0, conc...  24.7 us
    ppermute x13, starting transfers between devices, swap_with(): return lax.ppermute(x, 'frame', pairs)  15.2 us
    pallas_call x1, Pallas kernels, run_encoder(): pl.pallas_call(encoder, in_specs=[SMEM, VMEM, VMEM, VMEM, VMEM, VMEM, VME...  13.3 us
    pallas_call x1, Pallas kernels, run_frame_forward(): pl.pallas_call(frame_forward, in_specs=[SMEM, HBM, HBM, HBM, HBM], out_sp...  6.3 us
    ppermute x13, waiting for transfers between devices, swap_with(): return lax.ppermute(x, 'frame', pairs)  4.57 us
    pallas_call x3, Pallas kernels, run_scatter(): pl.pallas_call(functools.partial(scatter, halves, own), in_specs=[VMEM] *...  3.79 us
    pallas_call x1, Pallas kernels, run_prepare(): pl.pallas_call(prepare, in_specs=[SMEM, SMEM] + [VMEM] * 4 + [HBM, ANY],...  3.16 us
  transfers between devices with their start and end apart: 13, of which 5 were waited for; matrix products, arithmetic and copies ran while one was open for 0% of the time, Pallas kernels for 11%

profile of v4, /device:TPU:1, one launch (start us, length us, event | category | flops | bytes accessed | tf_op | source)
XLA Modules:
  0.0 110.8 jit_solution(7499270895378647389)
XLA Ops:
  0.6 0.0 copy-start.5
  0.7 6.3 %frame_forward.1 = (bf16[64,768]{1,0:T(8,128)(2,1)S(1)}, bf16[64,768]{1,0:T(8,128)(2,1)S(1)}, bf16[128,768]{1,0:T(8,128)(2,1)S(1)}, bf16[128,3072]{1,0:T(8,128)(...) custom-call(s32[1]{0:T(128)} %bitcast.core, bf16[128,768]{1,0:T(8,128)(2,1)} %bitcast.15, ...), custom_call_target="tpu_custom_call" | custom-call | tf_op jit(solution)/shard_map/frame_forward/pallas_call | solution.py:130
  7.0 1.5 %collective-permute-start = (bf16[64,768]{1,0:T(8,128)(2,1)S(1)}, bf16[64,768]{1,0:T(8,128)(2,1)S(1)}, u32[]{:S(2)}, u32[]{:S(2)}) collective-permute-start(bf16[64,768]{1,0:T(8,128)(2,1)S(1)} %get-tuple-element.23), channel_id=1, source_target_pairs={{0,1},{1,0},{2,3},{3,2},{4,5},{5,4},{6,7},{7,6},{8,9},{9,8},{10,11... | collective-permute-start | bytes 294920 | tf_op jit(solution)/shard_map/ppermute | solution.py:502
  8.5 0.9 collective-permute-done.theirs
  9.4 0.0 copy-done.5
  9.4 0.2 pool_pair.1.after.p0
  9.6 2.6 %collective-permute-start.3 = (bf16[64,896]{1,0:T(8,128)(2,1)S(1)}, bf16[64,896]{1,0:T(8,128)(2,1)S(1)}, u32[]{:S(2)}, u32[]{:S(2)}) collective-permute-start(bf16[64,896]{1,0:T(8,128)(2,1)S(1)} %pool_pair.1.after.p0), channel_id=1, source_target_pairs={{0,6},{1,7},{2,4},{3,5},{4,2},{5,3},{6,0},{7,1},{8,14},{9,15},{10,... | collective-permute-start | bytes 344072 | tf_op jit(solution)/shard_map/ppermute | solution.py:502
  12.2 0.5 collective-permute-start.2
  12.8 0.2 collective-permute-start.1
  12.9 0.0 copy-start
  12.9 0.0 copy-start.1
  12.9 0.0 copy-start.6
  12.9 0.0 copy-start.7
  12.9 0.0 copy-start.9
  12.9 2.6 %turn.1 = (bf16[3072,768]{1,0:T(8,128)(2,1)S(1)}, bf16[768,3072]{1,0:T(8,128)(2,1)S(1)}) custom-call(bf16[768,3072]{1,0:T(8,128)(2,1)S(1)} %get-tuple-element.27.up, bf16[3072,768]{1,0:T(8,128)(2,1)S(1)} %get-tuple-element.28.down, bf16[64,896]{1,0:T(8,128)(2,1)S(1)} %pool_pair.1.after.p0), custom_call_target="tpu_custom_call" | custom-call | flops 2359296 | bytes 18874368 | tf_op jit(solution)/shard_map/turn/pallas_call | solution.py:449
  15.5 0.0 copy-done
  15.5 0.0 copy-done.1
  15.6 0.0 copy-done.6
  15.6 0.0 copy-done.7
  15.6 0.0 copy-done.9
  15.6 3.2 %prepare.1 = (bf16[896,768]{1,0:T(8,128)(2,1)S(1)}, bf16[896,768]{1,0:T(8,128)(2,1)S(1)}, s32[896,1]{1,0:T(8,128)S(1)}, s32[896,1]{1,0:T(8,128)S(1)}, s32[1,1024...) custom-call(s32[1]{0:T(128)} %bitcast.core, s32[16]{0:T(128)S(1)} %copy-done.9, ...), custom_call_target="tpu_custom_call" | custom-call | flops 1056964608 | bytes 5505024 | tf_op jit(solution)/shard_map/prepare/pallas_call | solution.py:259
  18.8 0.0 collective-permute-done.3.p3
  18.8 0.0 collective-permute-done.2.p2
  18.8 0.0 collective-permute-done.1.p1
  18.8 0.3 pool_all.1
  19.1 28.8 %all_to_all.10 = bf16[16,64,768]{2,1,0:T(8,128)(2,1)S(1)} all-to-all(bf16[16,64,768]{2,1,0:T(8,128)(2,1)S(1)} %get-tuple-element.30), channel_id=1, replica_groups=mesh['dp'=16,'frame'=8] {'dp'}, dimensions={0} | all-to-all | bytes 3145728 | tf_op jit(solution)/shard_map/all_to_all | solution.py:536
  47.9 2.7 %collective-permute-start.4 = (bf16[1024,768]{1,0:T(8,128)(2,1)S(1)}, bf16[1024,768]{1,0:T(8,128)(2,1)S(1)}, u32[]{:S(2)}, u32[]{:S(2)}) collective-permute-start(bf16[1024,768]{1,0:T(8,128)(2,1)S(1)} %bitcast.12), channel_id=1, source_target_pairs={{0,1},{1,0},{2,3},{3,2},{4,5},{5,4},{6,7},{7,6},{8,9},{9,8},{10,11... | collective-permute-start | bytes 4718600 | tf_op jit(solution)/shard_map/ppermute | solution.py:502
  50.6 0.0 collective-permute-start.5
  50.6 0.5 collective-permute-start.6
  51.1 0.0 copy-start.3
  51.1 0.0 copy-start.8
  51.2 1.7 %gather.1.own_rows = bf16[896,768]{1,0:T(8,128)(2,1)S(1)} custom-call(s32[896,1]{1,0:T(8,128)S(1)} %get-tuple-element.25.index, bf16[1024,768]{1,0:T(8,128)(2,1)S(1)} %bitcast.13), custom_call_target="tpu_custom_call" | custom-call | flops 1409286144 | bytes 4128768 | tf_op jit(solution)/shard_map/gather/pallas_call | solution.py:288
  52.8 0.9 collective-permute-done.5.rest_0_.index
  53.7 0.2 collective-permute-done.6.rest_1_.pay_other
  53.8 0.0 collective-permute-done.4.table
  53.8 0.0 copy-done.3
  53.8 0.0 copy-done.8
  53.9 13.3 %user_encoder.1 = (bf16[896,768]{1,0:T(8,128)(2,1)S(1)}, bf16[448,768]{1,0:T(8,128)(2,1)S(1)}, bf16[448,768]{1,0:T(8,128)(2,1)S(1)}) custom-call(s32[16]{0:T(128)S(1)} %copy-done.9, s32[896,1]{1,0:T(8,128)S(1)} %get-tuple-element.24.index, bf16[896,768]{1,0:T(8,128)(2,1)S(1)} %gather.1.own_rows, bf16[1024,768]{1,0:T(8,128)(2,1)S(1)} %collective-permute-done.4.table, ...), custom_call_target="tpu_custom_call" | custom-call | tf_op jit(solution)/shard_map/user_encoder/pallas_call | solution.py:366
  67.1 0.5 collective-permute-start.8
  67.6 0.1 collective-permute-start.7
  67.7 1.8 %scatter.3.operands_1_ = bf16[1024,768]{1,0:T(8,128)(2,1)S(1)} custom-call(s32[1,1024]{1,0:T(1,128)S(1)} %get-tuple-element.38.index, bf16[448,768]{1,0:T(8,128)(2,1)S(1)} %get-tuple-element.37.operands_0_, bf16[448,768]{1,0:T(8,128)(2,1)S(1)} %get-tuple-element.36.operands_1_), custom_call_target="tpu_custom_call" | custom-call | flops 1409286144 | bytes 4128768 | tf_op jit(solution)/shard_map/scatter/pallas_call | solution.py:430
  69.5 0.0 collective-permute-done.8.operands_0_
  69.5 1.0 scatter.4.operands_1_
  70.5 0.0 collective-permute-done.7.operands_0_
  70.5 1.0 scatter.5
  71.5 24.7 %all_to_all.11.parts = bf16[16,64,768]{2,1,0:T(8,128)(2,1)S(1)} all-to-all(bf16[16,64,768]{2,1,0:T(8,128)(2,1)S(1)} %bitcast.11), channel_id=1, replica_groups=mesh['dp'=16,'frame'=8] {'dp'}, dimensions={0} | all-to-all | bytes 3145728 | tf_op jit(solution)/shard_map/all_to_all | solution.py:550
  96.2 0.2 add_owners.1.after.a
  96.4 2.4 %collective-permute-start.11 = (bf16[64,768]{1,0:T(8,128)(2,1)S(1)}, bf16[64,768]{1,0:T(8,128)(2,1)S(1)}, u32[]{:S(2)}, u32[]{:S(2)}) collective-permute-start(bf16[64,768]{1,0:T(8,128)(2,1)S(1)} %add_owners.1.after.a), channel_id=1, source_target_pairs={{0,6},{1,7},{2,4},{3,5},{4,2},{5,3},{6,0},{7,1},{8,14},{9,15},{10,... | collective-permute-start | bytes 294920 | tf_op jit(solution)/shard_map/ppermute | solution.py:502
  98.8 0.5 collective-permute-start.10
  99.3 0.5 collective-permute-start.9
  99.8 0.0 copy-start.2
  99.8 0.0 copy-start.4
  99.8 2.5 %reorder.1.after = bf16[800,768]{1,0:T(8,128)(2,1)} custom-call(bf16[896,768]{1,0:T(8,128)(2,1)S(1)} %get-tuple-element.35.by_user, bf16[64,768]{1,0:T(8,128)(2,1)S(1)} %add_owners.1.after.a), custom_call_target="tpu_custom_call" | custom-call | flops 614400 | bytes 3686400 | tf_op jit(solution)/shard_map/reorder/pallas_call | solution.py:390
  102.3 0.0 collective-permute-done.11.d
  102.3 1.6 %collective-permute-done.10.c = bf16[64,768]{1,0:T(8,128)(2,1)S(1)} collective-permute-done((bf16[64,768]{1,0:T(8,128)(2,1)S(1)}, bf16[64,768]{1,0:T(8,128)(2,1)S(1)}, u32[]{:S(2)}, u32[]{:S(2)}) %collective-permute-start.10) | collective-permute-done | bytes 98336 | tf_op jit(solution)/shard_map/ppermute | solution.py:502
  103.9 0.0 collective-permute-done.9.b
  103.9 0.1 add_parts.1.d_mine
  104.0 3.2 %collective-permute-start.12 = (bf16[64,768]{1,0:T(8,128)(2,1)S(1)}, bf16[64,768]{1,0:T(8,128)(2,1)S(1)}, u32[]{:S(2)}, u32[]{:S(2)}) collective-permute-start(bf16[64,768]{1,0:T(8,128)(2,1)S(1)} %add_parts.1.d_mine), channel_id=1, source_target_pairs={{0,1},{1,0},{2,3},{3,2},{4,5},{5,4},{6,7},{7,6},{8,9},{9,8},{10,11... | collective-permute-start | bytes 294920 | tf_op jit(solution)/shard_map/ppermute | solution.py:502
  107.1 0.9 collective-permute-done.12.d_other
  108.1 0.0 copy-done.2
  108.1 0.0 copy-done.4
  108.1 2.8 %frame_backward.1 = bf16[128,768]{1,0:T(8,128)(2,1)} custom-call(s32[1]{0:T(128)} %bitcast.core, bf16[64,768]{1,0:T(8,128)(2,1)S(1)} %add_parts.1.d_mine, bf16[64,768]{1,0:T(8,128)(2,1)S(1)} %collective-permute-done.12.d_other, bf16[64,896]{1,0:T(8,128)(2,1)S(1)} %get-tuple-element.34.pay_mine, bf16[64,896]{1,0:T(8,128)(2,1)S(1)} %collective-permute-done.6.rest_1_.pay_other, ...), custom_call_target="tpu_custom_call" | custom-call | tf_op jit(solution)/shard_map/frame_backward/pallas_call | solution.py:490
Async XLA Ops:
  0.6 8.8 %copy-start.5 = (f32[768]{0:T(1024)S(1)}, f32[768]{0:T(1024)}, u32[]{:S(2)}) copy-start(f32[768]{0:T(1024)} %query.3) | copy-start | bytes 9220
  7.0 2.4 %collective-permute-start = (bf16[64,768]{1,0:T(8,128)(2,1)S(1)}, bf16[64,768]{1,0:T(8,128)(2,1)S(1)}, u32[]{:S(2)}, u32[]{:S(2)}) collective-permute-start(bf16[64,768]{1,0:T(8,128)(2,1)S(1)} %get-tuple-element.23), channel_id=1, source_target_pairs={{0,1},{1,0},{2,3},{3,2},{4,5},{5,4},{6,7},{7,6},{8,9},{9,8},{10,11... | collective-permute-start | bytes 294920 | tf_op jit(solution)/shard_map/ppermute | solution.py:502
  9.6 9.2 %collective-permute-start.3 = (bf16[64,896]{1,0:T(8,128)(2,1)S(1)}, bf16[64,896]{1,0:T(8,128)(2,1)S(1)}, u32[]{:S(2)}, u32[]{:S(2)}) collective-permute-start(bf16[64,896]{1,0:T(8,128)(2,1)S(1)} %pool_pair.1.after.p0), channel_id=1, source_target_pairs={{0,6},{1,7},{2,4},{3,5},{4,2},{5,3},{6,0},{7,1},{8,14},{9,15},{10,... | collective-permute-start | bytes 344072 | tf_op jit(solution)/shard_map/ppermute | solution.py:502
  12.2 6.5 %collective-permute-start.2 = (bf16[64,896]{1,0:T(8,128)(2,1)S(1)}, bf16[64,896]{1,0:T(8,128)(2,1)S(1)}, u32[]{:S(2)}, u32[]{:S(2)}) collective-permute-start(bf16[64,896]{1,0:T(8,128)(2,1)S(1)} %pool_pair.1.after.p0), channel_id=1, source_target_pairs={{0,4},{1,5},{2,6},{3,7},{4,0},{5,1},{6,2},{7,3},{8,12},{9,13},{10,... | collective-permute-start | bytes 344072 | tf_op jit(solution)/shard_map/ppermute | solution.py:502
  12.8 6.0 %collective-permute-start.1 = (bf16[64,896]{1,0:T(8,128)(2,1)S(1)}, bf16[64,896]{1,0:T(8,128)(2,1)S(1)}, u32[]{:S(2)}, u32[]{:S(2)}) collective-permute-start(bf16[64,896]{1,0:T(8,128)(2,1)S(1)} %pool_pair.1.after.p0), channel_id=1, source_target_pairs={{0,2},{1,3},{2,0},{3,1},{4,6},{5,7},{6,4},{7,5},{8,10},{9,11},{10,... | collective-permute-start | bytes 344072 | tf_op jit(solution)/shard_map/ppermute | solution.py:502
  12.9 2.6 %copy-start = (bf16[768,768]{1,0:T(8,128)(2,1)S(1)}, bf16[768,768]{1,0:T(8,128)(2,1)}, u32[]{:S(2)}) copy-start(bf16[768,768]{1,0:T(8,128)(2,1)} %w_out.3) | copy-start | bytes 3538948
  12.9 2.6 %copy-start.1 = (bf16[16,50,768]{2,0,1:T(8,128)(2,1)S(1)}, bf16[16,50,768]{2,0,1:T(8,128)(2,1)}, u32[]{:S(2)}) copy-start(bf16[16,50,768]{2,0,1:T(8,128)(2,1)} %param.25) | copy-start | bytes 3686404
  12.9 2.6 %copy-start.6 = (s32[16,50]{1,0:T(8,128)S(1)}, s32[16,50]{1,0:T(8,128)}, u32[]{:S(2)}) copy-start(s32[16,50]{1,0:T(8,128)} %slots.1) | copy-start | bytes 9604
  12.9 2.6 %copy-start.7 = (s32[1,16,64]{2,1,0:T(8,128)S(1)}, s32[1,16,64]{2,1,0:T(8,128)}, u32[]{:S(2)}) copy-start(s32[1,16,64]{2,1,0:T(8,128)} %requests.1) | copy-start | bytes 12292
  12.9 2.6 %copy-start.9 = (s32[16]{0:T(128)S(1)}, s32[16]{0:T(128)}, u32[]{:S(2)}) copy-start(s32[16]{0:T(128)} %lens.3) | copy-start | bytes 196
  47.9 5.9 %collective-permute-start.4 = (bf16[1024,768]{1,0:T(8,128)(2,1)S(1)}, bf16[1024,768]{1,0:T(8,128)(2,1)S(1)}, u32[]{:S(2)}, u32[]{:S(2)}) collective-permute-start(bf16[1024,768]{1,0:T(8,128)(2,1)S(1)} %bitcast.12), channel_id=1, source_target_pairs={{0,1},{1,0},{2,3},{3,2},{4,5},{5,4},{6,7},{7,6},{8,9},{9,8},{10,11... | collective-permute-start | bytes 4718600 | tf_op jit(solution)/shard_map/ppermute | solution.py:502
  50.6 3.0 %collective-permute-start.5 = (s32[1,1024]{1,0:T(1,128)S(1)}, s32[1,1024]{1,0:T(1,128)S(1)}, u32[]{:S(2)}, u32[]{:S(2)}) collective-permute-start(s32[1,1024]{1,0:T(1,128)S(1)} %get-tuple-element.33), channel_id=1, source_target_pairs={{0,1},{1,0},{2,3},{3,2},{4,5},{5,4},{6,7},{7,6},{8,9},{9,8},{10,11... | collective-permute-start | bytes 12296 | tf_op jit(solution)/shard_map/ppermute | solution.py:502
  50.6 3.2 %collective-permute-start.6 = (bf16[64,896]{1,0:T(8,128)(2,1)S(1)}, bf16[64,896]{1,0:T(8,128)(2,1)S(1)}, u32[]{:S(2)}, u32[]{:S(2)}) collective-permute-start(bf16[64,896]{1,0:T(8,128)(2,1)S(1)} %get-tuple-element.34.pay_mine), channel_id=1, source_target_pairs={{0,1},{1,0},{2,3},{3,2},{4,5},{5,4},{6,7},{7,6},{8,9},{9,8},{10,11... | collective-permute-start | bytes 344072 | tf_op jit(solution)/shard_map/ppermute | solution.py:502
  51.1 2.7 %copy-start.3 = (bf16[50,768]{1,0:T(8,128)(2,1)S(1)}, bf16[50,768]{1,0:T(8,128)(2,1)}, u32[]{:S(2)}) copy-start(bf16[50,768]{1,0:T(8,128)(2,1)} %pos.1) | copy-start | bytes 230404
  51.1 2.7 %copy-start.8 = (f32[768]{0:T(1024)S(1)}, f32[768]{0:T(1024)}, u32[]{:S(2)}) copy-start(f32[768]{0:T(1024)} %gain.2) | copy-start | bytes 9220
  67.1 2.4 %collective-permute-start.8 = (bf16[448,768]{1,0:T(8,128)(2,1)S(1)}, bf16[448,768]{1,0:T(8,128)(2,1)S(1)}, u32[]{:S(2)}, u32[]{:S(2)}) collective-permute-start(bf16[448,768]{1,0:T(8,128)(2,1)S(1)} %get-tuple-element.37.operands_0_), channel_id=1, source_target_pairs={{0,1},{1,0},{2,3},{3,2},{4,5},{5,4},{6,7},{7,6},{8,9},{9,8},{10,11... | collective-permute-start | bytes 2064392 | tf_op jit(solution)/shard_map/ppermute | solution.py:502
  67.6 3.0 %collective-permute-start.7 = (bf16[448,768]{1,0:T(8,128)(2,1)S(1)}, bf16[448,768]{1,0:T(8,128)(2,1)S(1)}, u32[]{:S(2)}, u32[]{:S(2)}) collective-permute-start(bf16[448,768]{1,0:T(8,128)(2,1)S(1)} %get-tuple-element.36.operands_1_), channel_id=1, source_target_pairs={{0,1},{1,0},{2,3},{3,2},{4,5},{5,4},{6,7},{7,6},{8,9},{9,8},{10,11... | collective-permute-start | bytes 2064392 | tf_op jit(solution)/shard_map/ppermute | solution.py:502
  96.4 5.8 %collective-permute-start.11 = (bf16[64,768]{1,0:T(8,128)(2,1)S(1)}, bf16[64,768]{1,0:T(8,128)(2,1)S(1)}, u32[]{:S(2)}, u32[]{:S(2)}) collective-permute-start(bf16[64,768]{1,0:T(8,128)(2,1)S(1)} %add_owners.1.after.a), channel_id=1, source_target_pairs={{0,6},{1,7},{2,4},{3,5},{4,2},{5,3},{6,0},{7,1},{8,14},{9,15},{10,... | collective-permute-start | bytes 294920 | tf_op jit(solution)/shard_map/ppermute | solution.py:502
  98.8 5.1 %collective-permute-start.10 = (bf16[64,768]{1,0:T(8,128)(2,1)S(1)}, bf16[64,768]{1,0:T(8,128)(2,1)S(1)}, u32[]{:S(2)}, u32[]{:S(2)}) collective-permute-start(bf16[64,768]{1,0:T(8,128)(2,1)S(1)} %add_owners.1.after.a), channel_id=1, source_target_pairs={{0,4},{1,5},{2,6},{3,7},{4,0},{5,1},{6,2},{7,3},{8,12},{9,13},{10,... | collective-permute-start | bytes 294920 | tf_op jit(solution)/shard_map/ppermute | solution.py:502
  99.3 4.6 %collective-permute-start.9 = (bf16[64,768]{1,0:T(8,128)(2,1)S(1)}, bf16[64,768]{1,0:T(8,128)(2,1)S(1)}, u32[]{:S(2)}, u32[]{:S(2)}) collective-permute-start(bf16[64,768]{1,0:T(8,128)(2,1)S(1)} %add_owners.1.after.a), channel_id=1, source_target_pairs={{0,2},{1,3},{2,0},{3,1},{4,6},{5,7},{6,4},{7,5},{8,10},{9,11},{10,... | collective-permute-start | bytes 294920 | tf_op jit(solution)/shard_map/ppermute | solution.py:502
  99.8 8.3 %copy-start.2 = (bf16[128,1,768]{2,0,1:T(8,128)(2,1)S(1)}, bf16[128,1,768]{2,0,1:T(8,128)(2,1)}, u32[]{:S(2)}) copy-start(bf16[128,1,768]{2,0,1:T(8,128)(2,1)} %param.13) | copy-start | bytes 589828
  99.8 8.3 %copy-start.4 = (f32[768]{0:T(1024)S(1)}, f32[768]{0:T(1024)}, u32[]{:S(2)}) copy-start(f32[768]{0:T(1024)} %gain.3) | copy-start | bytes 9220
  104.0 4.1 %collective-permute-start.12 = (bf16[64,768]{1,0:T(8,128)(2,1)S(1)}, bf16[64,768]{1,0:T(8,128)(2,1)S(1)}, u32[]{:S(2)}, u32[]{:S(2)}) collective-permute-start(bf16[64,768]{1,0:T(8,128)(2,1)S(1)} %add_parts.1.d_mine), channel_id=1, source_target_pairs={{0,1},{1,0},{2,3},{3,2},{4,5},{5,4},{6,7},{7,6},{8,9},{9,8},{10,11... | collective-permute-start | bytes 294920 | tf_op jit(solution)/shard_map/ppermute | solution.py:502

commit v5 on v4

--- a/solution.py
+++ b/solution.py
@@ -98,7 +98,7 @@
     downs = fetch(w_down, down, down_sems, 0, PARTS)
     for one, two in zip(ups, downs):
         one.start()
-        two.start()
+        two.start(priority=1)
     for one in first:
         one.wait()
     x = frames[...].astype(f32)

time: 111 us -> 110 us (level)
  transfers between devices with their start and end apart: 13 -> 13, of which waited for: 5 -> 5; matrix products, arithmetic and copies ran while one was open for 0% -> 0% of each run, Pallas kernels for 11% -> 12%
where the time goes in v5:
time: 110 us
  blocking collectives  53.5 us (49%)
  Pallas kernels  36 us (33%)
  starting transfers between devices  15.2 us (14%)
  waiting for transfers between devices  4.56 us (4%)
    all_to_all x1, blocking collectives, shards(): lax.all_to_all(spread, 'dp', split_axis=0, concat_axis=0, tiled=True)  28.8 us
    all_to_all x1, blocking collectives, shards(): lax.all_to_all(d_table.reshape(OWNERS, HALF, D), 'dp', split_axis=0, conc...  24.7 us
    ppermute x13, starting transfers between devices, swap_with(): return lax.ppermute(x, 'frame', pairs)  15.2 us
    pallas_call x1, Pallas kernels, run_encoder(): pl.pallas_call(encoder, in_specs=[SMEM, VMEM, VMEM, VMEM, VMEM, VMEM, VME...  13.3 us
    pallas_call x1, Pallas kernels, run_frame_forward(): pl.pallas_call(frame_forward, in_specs=[SMEM, HBM, HBM, HBM, HBM], out_sp...  5.49 us
    ppermute x13, waiting for transfers between devices, swap_with(): return lax.ppermute(x, 'frame', pairs)  4.56 us
    pallas_call x3, Pallas kernels, run_scatter(): pl.pallas_call(functools.partial(scatter, halves, own), in_specs=[VMEM] *...  3.79 us
    pallas_call x1, Pallas kernels, run_prepare(): pl.pallas_call(prepare, in_specs=[SMEM, SMEM] + [VMEM] * 4 + [HBM, ANY],...  3.16 us
  transfers between devices with their start and end apart: 13, of which 5 were waited for; matrix products, arithmetic and copies ran while one was open for 0% of the time, Pallas kernels for 12%

profile of v5, /device:TPU:1, one launch (start us, length us, event | category | flops | bytes accessed | tf_op | source)
XLA Modules:
  0.0 110.0 jit_solution(17350853320736211451)
XLA Ops:
  0.6 0.0 copy-start.5
  0.7 5.5 %frame_forward.1 = (bf16[64,768]{1,0:T(8,128)(2,1)S(1)}, bf16[64,768]{1,0:T(8,128)(2,1)S(1)}, bf16[128,768]{1,0:T(8,128)(2,1)S(1)}, bf16[128,3072]{1,0:T(8,128)(...) custom-call(s32[1]{0:T(128)} %bitcast.core, bf16[128,768]{1,0:T(8,128)(2,1)} %bitcast.15, ...), custom_call_target="tpu_custom_call" | custom-call | tf_op jit(solution)/shard_map/frame_forward/pallas_call | solution.py:130
  6.1 1.5 %collective-permute-start = (bf16[64,768]{1,0:T(8,128)(2,1)S(1)}, bf16[64,768]{1,0:T(8,128)(2,1)S(1)}, u32[]{:S(2)}, u32[]{:S(2)}) collective-permute-start(bf16[64,768]{1,0:T(8,128)(2,1)S(1)} %get-tuple-element.23), channel_id=1, source_target_pairs={{0,1},{1,0},{2,3},{3,2},{4,5},{5,4},{6,7},{7,6},{8,9},{9,8},{10,11... | collective-permute-start | bytes 294920 | tf_op jit(solution)/shard_map/ppermute | solution.py:502
  7.6 0.9 collective-permute-done.theirs
  8.6 0.0 copy-done.5
  8.6 0.2 pool_pair.1.after.p0
  8.8 2.6 %collective-permute-start.3 = (bf16[64,896]{1,0:T(8,128)(2,1)S(1)}, bf16[64,896]{1,0:T(8,128)(2,1)S(1)}, u32[]{:S(2)}, u32[]{:S(2)}) collective-permute-start(bf16[64,896]{1,0:T(8,128)(2,1)S(1)} %pool_pair.1.after.p0), channel_id=1, source_target_pairs={{0,6},{1,7},{2,4},{3,5},{4,2},{5,3},{6,0},{7,1},{8,14},{9,15},{10,... | collective-permute-start | bytes 344072 | tf_op jit(solution)/shard_map/ppermute | solution.py:502
  11.4 0.5 collective-permute-start.2
  11.9 0.2 collective-permute-start.1
  12.1 0.0 copy-start
  12.1 0.0 copy-start.1
  12.1 0.0 copy-start.6
  12.1 0.0 copy-start.7
  12.1 0.0 copy-start.9
  12.1 2.6 %turn.1 = (bf16[3072,768]{1,0:T(8,128)(2,1)S(1)}, bf16[768,3072]{1,0:T(8,128)(2,1)S(1)}) custom-call(bf16[768,3072]{1,0:T(8,128)(2,1)S(1)} %get-tuple-element.27.up, bf16[3072,768]{1,0:T(8,128)(2,1)S(1)} %get-tuple-element.28.down, bf16[64,896]{1,0:T(8,128)(2,1)S(1)} %pool_pair.1.after.p0), custom_call_target="tpu_custom_call" | custom-call | flops 2359296 | bytes 18874368 | tf_op jit(solution)/shard_map/turn/pallas_call | solution.py:449
  14.7 0.0 copy-done
  14.7 0.0 copy-done.1
  14.7 0.0 copy-done.6
  14.8 0.0 copy-done.7
  14.8 0.0 copy-done.9
  14.8 3.2 %prepare.1 = (bf16[896,768]{1,0:T(8,128)(2,1)S(1)}, bf16[896,768]{1,0:T(8,128)(2,1)S(1)}, s32[896,1]{1,0:T(8,128)S(1)}, s32[896,1]{1,0:T(8,128)S(1)}, s32[1,1024...) custom-call(s32[1]{0:T(128)} %bitcast.core, s32[16]{0:T(128)S(1)} %copy-done.9, ...), custom_call_target="tpu_custom_call" | custom-call | flops 1056964608 | bytes 5505024 | tf_op jit(solution)/shard_map/prepare/pallas_call | solution.py:259
  17.9 0.0 collective-permute-done.3.p3
  17.9 0.0 collective-permute-done.2.p2
  18.0 0.0 collective-permute-done.1.p1
  18.0 0.3 pool_all.1
  18.3 28.8 %all_to_all.10 = bf16[16,64,768]{2,1,0:T(8,128)(2,1)S(1)} all-to-all(bf16[16,64,768]{2,1,0:T(8,128)(2,1)S(1)} %get-tuple-element.30), channel_id=1, replica_groups=mesh['dp'=16,'frame'=8] {'dp'}, dimensions={0} | all-to-all | bytes 3145728 | tf_op jit(solution)/shard_map/all_to_all | solution.py:536
  47.1 2.7 %collective-permute-start.4 = (bf16[1024,768]{1,0:T(8,128)(2,1)S(1)}, bf16[1024,768]{1,0:T(8,128)(2,1)S(1)}, u32[]{:S(2)}, u32[]{:S(2)}) collective-permute-start(bf16[1024,768]{1,0:T(8,128)(2,1)S(1)} %bitcast.12), channel_id=1, source_target_pairs={{0,1},{1,0},{2,3},{3,2},{4,5},{5,4},{6,7},{7,6},{8,9},{9,8},{10,11... | collective-permute-start | bytes 4718600 | tf_op jit(solution)/shard_map/ppermute | solution.py:502
  49.8 0.0 collective-permute-start.5
  49.8 0.5 collective-permute-start.6
  50.3 0.0 copy-start.3
  50.3 0.0 copy-start.8
  50.3 1.7 %gather.1.own_rows = bf16[896,768]{1,0:T(8,128)(2,1)S(1)} custom-call(s32[896,1]{1,0:T(8,128)S(1)} %get-tuple-element.25.index, bf16[1024,768]{1,0:T(8,128)(2,1)S(1)} %bitcast.13), custom_call_target="tpu_custom_call" | custom-call | flops 1409286144 | bytes 4128768 | tf_op jit(solution)/shard_map/gather/pallas_call | solution.py:288
  52.0 0.9 collective-permute-done.5.rest_0_.index
  52.9 0.2 collective-permute-done.6.rest_1_.pay_other
  53.0 0.0 collective-permute-done.4.table
  53.0 0.0 copy-done.3
  53.0 0.0 copy-done.8
  53.0 13.3 %user_encoder.1 = (bf16[896,768]{1,0:T(8,128)(2,1)S(1)}, bf16[448,768]{1,0:T(8,128)(2,1)S(1)}, bf16[448,768]{1,0:T(8,128)(2,1)S(1)}) custom-call(s32[16]{0:T(128)S(1)} %copy-done.9, s32[896,1]{1,0:T(8,128)S(1)} %get-tuple-element.24.index, bf16[896,768]{1,0:T(8,128)(2,1)S(1)} %gather.1.own_rows, bf16[1024,768]{1,0:T(8,128)(2,1)S(1)} %collective-permute-done.4.table, ...), custom_call_target="tpu_custom_call" | custom-call | tf_op jit(solution)/shard_map/user_encoder/pallas_call | solution.py:366
  66.3 0.5 collective-permute-start.8
  66.8 0.1 collective-permute-start.7
  66.9 1.8 %scatter.3.operands_1_ = bf16[1024,768]{1,0:T(8,128)(2,1)S(1)} custom-call(s32[1,1024]{1,0:T(1,128)S(1)} %get-tuple-element.38.index, bf16[448,768]{1,0:T(8,128)(2,1)S(1)} %get-tuple-element.37.operands_0_, bf16[448,768]{1,0:T(8,128)(2,1)S(1)} %get-tuple-element.36.operands_1_), custom_call_target="tpu_custom_call" | custom-call | flops 1409286144 | bytes 4128768 | tf_op jit(solution)/shard_map/scatter/pallas_call | solution.py:430
  68.7 0.0 collective-permute-done.8.operands_0_
  68.7 1.0 scatter.4.operands_1_
  69.7 0.0 collective-permute-done.7.operands_0_
  69.7 1.0 scatter.5
  70.7 24.7 %all_to_all.11.parts = bf16[16,64,768]{2,1,0:T(8,128)(2,1)S(1)} all-to-all(bf16[16,64,768]{2,1,0:T(8,128)(2,1)S(1)} %bitcast.11), channel_id=1, replica_groups=mesh['dp'=16,'frame'=8] {'dp'}, dimensions={0} | all-to-all | bytes 3145728 | tf_op jit(solution)/shard_map/all_to_all | solution.py:550
  95.4 0.2 add_owners.1.after.a
  95.6 2.4 %collective-permute-start.11 = (bf16[64,768]{1,0:T(8,128)(2,1)S(1)}, bf16[64,768]{1,0:T(8,128)(2,1)S(1)}, u32[]{:S(2)}, u32[]{:S(2)}) collective-permute-start(bf16[64,768]{1,0:T(8,128)(2,1)S(1)} %add_owners.1.after.a), channel_id=1, source_target_pairs={{0,6},{1,7},{2,4},{3,5},{4,2},{5,3},{6,0},{7,1},{8,14},{9,15},{10,... | collective-permute-start | bytes 294920 | tf_op jit(solution)/shard_map/ppermute | solution.py:502
  98.0 0.5 collective-permute-start.10
  98.5 0.5 collective-permute-start.9
  99.0 0.0 copy-start.2
  99.0 0.0 copy-start.4
  99.0 2.5 %reorder.1.after = bf16[800,768]{1,0:T(8,128)(2,1)} custom-call(bf16[896,768]{1,0:T(8,128)(2,1)S(1)} %get-tuple-element.35.by_user, bf16[64,768]{1,0:T(8,128)(2,1)S(1)} %add_owners.1.after.a), custom_call_target="tpu_custom_call" | custom-call | flops 614400 | bytes 3686400 | tf_op jit(solution)/shard_map/reorder/pallas_call | solution.py:390
  101.4 0.0 collective-permute-done.11.d
  101.4 1.6 %collective-permute-done.10.c = bf16[64,768]{1,0:T(8,128)(2,1)S(1)} collective-permute-done((bf16[64,768]{1,0:T(8,128)(2,1)S(1)}, bf16[64,768]{1,0:T(8,128)(2,1)S(1)}, u32[]{:S(2)}, u32[]{:S(2)}) %collective-permute-start.10) | collective-permute-done | bytes 98336 | tf_op jit(solution)/shard_map/ppermute | solution.py:502
  103.1 0.0 collective-permute-done.9.b
  103.1 0.1 add_parts.1.d_mine
  103.1 3.2 %collective-permute-start.12 = (bf16[64,768]{1,0:T(8,128)(2,1)S(1)}, bf16[64,768]{1,0:T(8,128)(2,1)S(1)}, u32[]{:S(2)}, u32[]{:S(2)}) collective-permute-start(bf16[64,768]{1,0:T(8,128)(2,1)S(1)} %add_parts.1.d_mine), channel_id=1, source_target_pairs={{0,1},{1,0},{2,3},{3,2},{4,5},{5,4},{6,7},{7,6},{8,9},{9,8},{10,11... | collective-permute-start | bytes 294920 | tf_op jit(solution)/shard_map/ppermute | solution.py:502
  106.3 0.9 collective-permute-done.12.d_other
  107.2 0.0 copy-done.2
  107.2 0.0 copy-done.4
  107.3 2.8 %frame_backward.1 = bf16[128,768]{1,0:T(8,128)(2,1)} custom-call(s32[1]{0:T(128)} %bitcast.core, bf16[64,768]{1,0:T(8,128)(2,1)S(1)} %add_parts.1.d_mine, bf16[64,768]{1,0:T(8,128)(2,1)S(1)} %collective-permute-done.12.d_other, bf16[64,896]{1,0:T(8,128)(2,1)S(1)} %get-tuple-element.34.pay_mine, bf16[64,896]{1,0:T(8,128)(2,1)S(1)} %collective-permute-done.6.rest_1_.pay_other, ...), custom_call_target="tpu_custom_call" | custom-call | tf_op jit(solution)/shard_map/frame_backward/pallas_call | solution.py:490
Async XLA Ops:
  0.6 8.0 %copy-start.5 = (f32[768]{0:T(1024)S(1)}, f32[768]{0:T(1024)}, u32[]{:S(2)}) copy-start(f32[768]{0:T(1024)} %query.3) | copy-start | bytes 9220
  6.1 2.4 %collective-permute-start = (bf16[64,768]{1,0:T(8,128)(2,1)S(1)}, bf16[64,768]{1,0:T(8,128)(2,1)S(1)}, u32[]{:S(2)}, u32[]{:S(2)}) collective-permute-start(bf16[64,768]{1,0:T(8,128)(2,1)S(1)} %get-tuple-element.23), channel_id=1, source_target_pairs={{0,1},{1,0},{2,3},{3,2},{4,5},{5,4},{6,7},{7,6},{8,9},{9,8},{10,11... | collective-permute-start | bytes 294920 | tf_op jit(solution)/shard_map/ppermute | solution.py:502
  8.8 9.2 %collective-permute-start.3 = (bf16[64,896]{1,0:T(8,128)(2,1)S(1)}, bf16[64,896]{1,0:T(8,128)(2,1)S(1)}, u32[]{:S(2)}, u32[]{:S(2)}) collective-permute-start(bf16[64,896]{1,0:T(8,128)(2,1)S(1)} %pool_pair.1.after.p0), channel_id=1, source_target_pairs={{0,6},{1,7},{2,4},{3,5},{4,2},{5,3},{6,0},{7,1},{8,14},{9,15},{10,... | collective-permute-start | bytes 344072 | tf_op jit(solution)/shard_map/ppermute | solution.py:502
  11.4 6.5 %collective-permute-start.2 = (bf16[64,896]{1,0:T(8,128)(2,1)S(1)}, bf16[64,896]{1,0:T(8,128)(2,1)S(1)}, u32[]{:S(2)}, u32[]{:S(2)}) collective-permute-start(bf16[64,896]{1,0:T(8,128)(2,1)S(1)} %pool_pair.1.after.p0), channel_id=1, source_target_pairs={{0,4},{1,5},{2,6},{3,7},{4,0},{5,1},{6,2},{7,3},{8,12},{9,13},{10,... | collective-permute-start | bytes 344072 | tf_op jit(solution)/shard_map/ppermute | solution.py:502
  11.9 6.0 %collective-permute-start.1 = (bf16[64,896]{1,0:T(8,128)(2,1)S(1)}, bf16[64,896]{1,0:T(8,128)(2,1)S(1)}, u32[]{:S(2)}, u32[]{:S(2)}) collective-permute-start(bf16[64,896]{1,0:T(8,128)(2,1)S(1)} %pool_pair.1.after.p0), channel_id=1, source_target_pairs={{0,2},{1,3},{2,0},{3,1},{4,6},{5,7},{6,4},{7,5},{8,10},{9,11},{10,... | collective-permute-start | bytes 344072 | tf_op jit(solution)/shard_map/ppermute | solution.py:502
  12.1 2.6 %copy-start = (bf16[768,768]{1,0:T(8,128)(2,1)S(1)}, bf16[768,768]{1,0:T(8,128)(2,1)}, u32[]{:S(2)}) copy-start(bf16[768,768]{1,0:T(8,128)(2,1)} %w_out.3) | copy-start | bytes 3538948
  12.1 2.6 %copy-start.1 = (bf16[16,50,768]{2,0,1:T(8,128)(2,1)S(1)}, bf16[16,50,768]{2,0,1:T(8,128)(2,1)}, u32[]{:S(2)}) copy-start(bf16[16,50,768]{2,0,1:T(8,128)(2,1)} %param.25) | copy-start | bytes 3686404
  12.1 2.6 %copy-start.6 = (s32[16,50]{1,0:T(8,128)S(1)}, s32[16,50]{1,0:T(8,128)}, u32[]{:S(2)}) copy-start(s32[16,50]{1,0:T(8,128)} %slots.1) | copy-start | bytes 9604
  12.1 2.6 %copy-start.7 = (s32[1,16,64]{2,1,0:T(8,128)S(1)}, s32[1,16,64]{2,1,0:T(8,128)}, u32[]{:S(2)}) copy-start(s32[1,16,64]{2,1,0:T(8,128)} %requests.1) | copy-start | bytes 12292
  12.1 2.6 %copy-start.9 = (s32[16]{0:T(128)S(1)}, s32[16]{0:T(128)}, u32[]{:S(2)}) copy-start(s32[16]{0:T(128)} %lens.3) | copy-start | bytes 196
  47.1 5.9 %collective-permute-start.4 = (bf16[1024,768]{1,0:T(8,128)(2,1)S(1)}, bf16[1024,768]{1,0:T(8,128)(2,1)S(1)}, u32[]{:S(2)}, u32[]{:S(2)}) collective-permute-start(bf16[1024,768]{1,0:T(8,128)(2,1)S(1)} %bitcast.12), channel_id=1, source_target_pairs={{0,1},{1,0},{2,3},{3,2},{4,5},{5,4},{6,7},{7,6},{8,9},{9,8},{10,11... | collective-permute-start | bytes 4718600 | tf_op jit(solution)/shard_map/ppermute | solution.py:502
  49.8 3.0 %collective-permute-start.5 = (s32[1,1024]{1,0:T(1,128)S(1)}, s32[1,1024]{1,0:T(1,128)S(1)}, u32[]{:S(2)}, u32[]{:S(2)}) collective-permute-start(s32[1,1024]{1,0:T(1,128)S(1)} %get-tuple-element.33), channel_id=1, source_target_pairs={{0,1},{1,0},{2,3},{3,2},{4,5},{5,4},{6,7},{7,6},{8,9},{9,8},{10,11... | collective-permute-start | bytes 12296 | tf_op jit(solution)/shard_map/ppermute | solution.py:502
  49.8 3.2 %collective-permute-start.6 = (bf16[64,896]{1,0:T(8,128)(2,1)S(1)}, bf16[64,896]{1,0:T(8,128)(2,1)S(1)}, u32[]{:S(2)}, u32[]{:S(2)}) collective-permute-start(bf16[64,896]{1,0:T(8,128)(2,1)S(1)} %get-tuple-element.34.pay_mine), channel_id=1, source_target_pairs={{0,1},{1,0},{2,3},{3,2},{4,5},{5,4},{6,7},{7,6},{8,9},{9,8},{10,11... | collective-permute-start | bytes 344072 | tf_op jit(solution)/shard_map/ppermute | solution.py:502
  50.3 2.7 %copy-start.3 = (bf16[50,768]{1,0:T(8,128)(2,1)S(1)}, bf16[50,768]{1,0:T(8,128)(2,1)}, u32[]{:S(2)}) copy-start(bf16[50,768]{1,0:T(8,128)(2,1)} %pos.1) | copy-start | bytes 230404
  50.3 2.7 %copy-start.8 = (f32[768]{0:T(1024)S(1)}, f32[768]{0:T(1024)}, u32[]{:S(2)}) copy-start(f32[768]{0:T(1024)} %gain.2) | copy-start | bytes 9220
  66.3 2.4 %collective-permute-start.8 = (bf16[448,768]{1,0:T(8,128)(2,1)S(1)}, bf16[448,768]{1,0:T(8,128)(2,1)S(1)}, u32[]{:S(2)}, u32[]{:S(2)}) collective-permute-start(bf16[448,768]{1,0:T(8,128)(2,1)S(1)} %get-tuple-element.37.operands_0_), channel_id=1, source_target_pairs={{0,1},{1,0},{2,3},{3,2},{4,5},{5,4},{6,7},{7,6},{8,9},{9,8},{10,11... | collective-permute-start | bytes 2064392 | tf_op jit(solution)/shard_map/ppermute | solution.py:502
  66.8 3.0 %collective-permute-start.7 = (bf16[448,768]{1,0:T(8,128)(2,1)S(1)}, bf16[448,768]{1,0:T(8,128)(2,1)S(1)}, u32[]{:S(2)}, u32[]{:S(2)}) collective-permute-start(bf16[448,768]{1,0:T(8,128)(2,1)S(1)} %get-tuple-element.36.operands_1_), channel_id=1, source_target_pairs={{0,1},{1,0},{2,3},{3,2},{4,5},{5,4},{6,7},{7,6},{8,9},{9,8},{10,11... | collective-permute-start | bytes 2064392 | tf_op jit(solution)/shard_map/ppermute | solution.py:502
  95.6 5.8 %collective-permute-start.11 = (bf16[64,768]{1,0:T(8,128)(2,1)S(1)}, bf16[64,768]{1,0:T(8,128)(2,1)S(1)}, u32[]{:S(2)}, u32[]{:S(2)}) collective-permute-start(bf16[64,768]{1,0:T(8,128)(2,1)S(1)} %add_owners.1.after.a), channel_id=1, source_target_pairs={{0,6},{1,7},{2,4},{3,5},{4,2},{5,3},{6,0},{7,1},{8,14},{9,15},{10,... | collective-permute-start | bytes 294920 | tf_op jit(solution)/shard_map/ppermute | solution.py:502
  98.0 5.1 %collective-permute-start.10 = (bf16[64,768]{1,0:T(8,128)(2,1)S(1)}, bf16[64,768]{1,0:T(8,128)(2,1)S(1)}, u32[]{:S(2)}, u32[]{:S(2)}) collective-permute-start(bf16[64,768]{1,0:T(8,128)(2,1)S(1)} %add_owners.1.after.a), channel_id=1, source_target_pairs={{0,4},{1,5},{2,6},{3,7},{4,0},{5,1},{6,2},{7,3},{8,12},{9,13},{10,... | collective-permute-start | bytes 294920 | tf_op jit(solution)/shard_map/ppermute | solution.py:502
  98.5 4.6 %collective-permute-start.9 = (bf16[64,768]{1,0:T(8,128)(2,1)S(1)}, bf16[64,768]{1,0:T(8,128)(2,1)S(1)}, u32[]{:S(2)}, u32[]{:S(2)}) collective-permute-start(bf16[64,768]{1,0:T(8,128)(2,1)S(1)} %add_owners.1.after.a), channel_id=1, source_target_pairs={{0,2},{1,3},{2,0},{3,1},{4,6},{5,7},{6,4},{7,5},{8,10},{9,11},{10,... | collective-permute-start | bytes 294920 | tf_op jit(solution)/shard_map/ppermute | solution.py:502
  99.0 8.3 %copy-start.2 = (bf16[128,1,768]{2,0,1:T(8,128)(2,1)S(1)}, bf16[128,1,768]{2,0,1:T(8,128)(2,1)}, u32[]{:S(2)}) copy-start(bf16[128,1,768]{2,0,1:T(8,128)(2,1)} %param.13) | copy-start | bytes 589828
  99.0 8.3 %copy-start.4 = (f32[768]{0:T(1024)S(1)}, f32[768]{0:T(1024)}, u32[]{:S(2)}) copy-start(f32[768]{0:T(1024)} %gain.3) | copy-start | bytes 9220
  103.1 4.1 %collective-permute-start.12 = (bf16[64,768]{1,0:T(8,128)(2,1)S(1)}, bf16[64,768]{1,0:T(8,128)(2,1)S(1)}, u32[]{:S(2)}, u32[]{:S(2)}) collective-permute-start(bf16[64,768]{1,0:T(8,128)(2,1)S(1)} %add_parts.1.d_mine), channel_id=1, source_target_pairs={{0,1},{1,0},{2,3},{3,2},{4,5},{5,4},{6,7},{7,6},{8,9},{9,8},{10,11... | collective-permute-start | bytes 294920 | tf_op jit(solution)/shard_map/ppermute | solution.py:502
